TPU v7x, 32 devices: a whole 2x2x4 slice. The times are simulated.
32 devices in a mesh: dp: 8 (over y, x, core), tensor: 4 (over z).
Axes of the slice: x: 2, y: 2, z: 4, core: 2. Of those that a mesh axis runs over, the one named last changes fastest.
Arguments:
- hidden: bfloat16 [2, 1024, 2048], P(None, 'dp'), may hold values from -6 to 6
- embedding: bfloat16 [2, 1024, 2048], P(None, 'dp'), may hold values from -6 to 6
- lengths: int32 [2, 8, 5], P(None, 'dp'), may hold values from 1 to 64, 128 in all within a row
- query_key_value_weight: bfloat16 [4096, 3, 4096], P('dp', None, 'tensor'), may hold values from -0.09375 to 0.09375
- attention_output_weight: bfloat16 [4096, 4096], P('tensor', 'dp'), may hold values from -0.375 to 0.375
- attention_gain: bfloat16 [4096], P('dp'), may hold values from 0.099609375 to 1.8984375
- feedforward_gain: bfloat16 [4096], P('dp'), may hold values from 0.099609375 to 1.8984375
- gate_up_weight: bfloat16 [4096, 2, 8192], P('dp', None, 'tensor'), may hold values from -0.09375 to 0.09375
- adapter_down: bfloat16 [4096, 128], P('dp'), may hold values from -0.09375 to 0.09375
- adapter_up: bfloat16 [128, 2, 8192], P('dp', None, 'tensor'), may hold values from -0.5 to 0.5
- down_weight: bfloat16 [8192, 4096], P('tensor', 'dp'), may hold values from -0.0625 to 0.0625
- shared_projection_weight: bfloat16 [4096, 2048], P('tensor', 'dp'), may hold values from -0.09375 to 0.09375
- mixer_gain: bfloat16 [2048], P('dp'), may hold values from 0.099609375 to 1.8984375
- mixer_input_weight: bfloat16 [2048, 2, 4096], P('dp', None, 'tensor'), may hold values from -0.125 to 0.125
- state_map_weight: bfloat16 [2048, 256], P('dp'), may hold values from -0.125 to 0.125
- step_weight: bfloat16 [2048, 64], P('dp', 'tensor'), may hold values from -0.125 to 0.125
- mixer_output_weight: bfloat16 [4096, 2048], P('tensor', 'dp'), may hold values from -0.09375 to 0.09375
- mixer_input_taps: float32 [4, 4096], P(None, 'tensor'), may hold values from -3 to 3
- state_map_taps: float32 [4, 256], replicated, may hold values from -3 to 3
- step_bias: float32 [64], P('tensor'), may hold values from -6 to -2
- decay_logarithm: float32 [64], P('tensor'), may hold values from 0 to 2.77
- head_skip_weight: float32 [64], P('tensor'), may hold values from 0.5 to 1.5
- gated_norm_gain: float32 [4096], P('tensor'), may hold values from 0.1 to 1.9
- cotangent: bfloat16 [2, 1024, 2048], P(None, 'dp'), may hold values from -6 to 6
Outputs:
- output: bfloat16 [2, 1024, 2048], P(None, 'dp')
- d_hidden: bfloat16 [2, 1024, 2048], P(None, 'dp')
- d_embedding: bfloat16 [2, 1024, 2048], P(None, 'dp')
- grad_w_qkv: float32 [4096, 3, 4096], P('dp', None, 'tensor')
- grad_w_out: float32 [4096, 4096], P('tensor', 'dp')
- grad_g_attn: float32 [4096], P('dp')
- grad_g_mlp: float32 [4096], P('dp')
- grad_w_gate_up: float32 [4096, 2, 8192], P('dp', None, 'tensor')
- adapter_down_gradient: float32 [4096, 128], P('dp')
- adapter_up_gradient: float32 [128, 2, 8192], P('dp', None, 'tensor')
- grad_w_down: float32 [8192, 4096], P('tensor', 'dp')
- grad_w_proj: float32 [4096, 2048], P('tensor', 'dp')
- grad_g_mamba: float32 [2048], P('dp')
- grad_w_in: float32 [2048, 2, 4096], P('dp', None, 'tensor')
- grad_w_bc: float32 [2048, 256], P('dp')
- grad_w_dt: float32 [2048, 64], P('dp', 'tensor')
- grad_w_mout: float32 [4096, 2048], P('tensor', 'dp')
- grad_conv_x: float32 [4, 4096], P(None, 'tensor')
- grad_conv_bc: float32 [4, 256], replicated
- grad_dt_bias: float32 [64], P('tensor')
- grad_a_log: float32 [64], P('tensor')
- grad_d_skip: float32 [64], P('tensor')
- grad_g_gate: float32 [4096], P('tensor')
Inputs may be any that keep to these rules, and one draw needn't show every extreme that they name: Each row of lengths is one bin of 128 rows: its first 4 entries are the lengths of the sequences packed in order from the bin's first row, the last entry is the count of padding rows at the bin's end; each row sums to 128 and its largest entry is exactly 64.
All inputs are finite; a program needn't handle non-finite values.
Results may differ from a plain program's by a relative error of at most 0.03.
Values may be sent and summed in bfloat16 or wider, within the bound.
A program may use at most 448 MiB of HBM per device.

v0:
```python
from functools import partial

import jax
import jax.numpy as jnp
from jax import lax
from jax.sharding import PartitionSpec as P

HEAD = 128
INNER = 4096


EPSILON = 1e-05
ROPE_BASE = 10000.0
MASKED = -1e30
TOP_PRECISION = lax.Precision.HIGHEST
BROAD_DTYPE = jnp.float32
COMPACT_DTYPE = jnp.bfloat16


def layout(len_row, row_count):
    bounds = jnp.cumsum(len_row)[:-1]
    places = jnp.arange(row_count, dtype=jnp.int32)
    passed = places[:, None] >= bounds[None, :]
    segment = jnp.sum(passed.astype(jnp.int32), axis=1)
    starts = jnp.max(jnp.where(passed, bounds[None, :], 0), axis=1)
    position = places - starts
    valid = segment < bounds.shape[0]
    allowed = (segment[:, None] == segment[None, :]) & (places[None, :] <= places[:, None])
    return (segment, position, valid, allowed)


def rms_norm(values, gain):
    return values * lax.rsqrt(jnp.mean(values * values, axis=-1, keepdims=True) + EPSILON) * gain


def rotate(values, position):
    half_size = values.shape[-1] // 2
    frequency = ROPE_BASE ** (-2.0 * jnp.arange(half_size, dtype=jnp.float32) / values.shape[-1])
    angles = position.astype(jnp.float32)[:, None] * frequency[None, :]
    cosine = jnp.cos(angles)[:, None, :]
    sine_part = jnp.sin(angles)[:, None, :]
    leading = values[..., :half_size]
    trailing = values[..., half_size:]
    return jnp.concatenate(
        [leading * cosine - trailing * sine_part, trailing * cosine + leading * sine_part], axis=-1
    )


def rope_pair(query_raw, key_raw, position):
    return (rotate(query_raw, position), rotate(key_raw, position))


def causal_conv(values, taps, segment):
    row_count = values.shape[0]
    summed = jnp.zeros_like(values)
    for offset in range(taps.shape[0]):
        shifted = jnp.pad(values, ((offset, 0), (0, 0)))[:row_count]
        shifted_seg = jnp.pad(segment, (offset, 0), constant_values=-1)[:row_count]
        summed = (
            summed
            + jnp.where((shifted_seg == segment)[:, None], shifted, 0.0) * taps[offset][None, :]
        )
    return summed


def state_mix(inputs, step_size, log_decay, b_part, c_part, allowed, head_skip_weight):
    running = jnp.cumsum(log_decay, axis=0)
    log_gap = jnp.where(allowed[:, :, None], running[:, None, :] - running[None, :, :], MASKED)
    affinity = jnp.dot(c_part, b_part.T, precision=TOP_PRECISION)
    mixing = jnp.exp(log_gap) * affinity[:, :, None] * step_size[None, :, :]
    return (
        jnp.einsum("tsh,shp->thp", mixing, inputs, precision=TOP_PRECISION)
        + head_skip_weight[None, :, None] * inputs
    )


def mamba_local(
    gate_x,
    state_io,
    step_raw,
    mixer_input_taps,
    state_map_taps,
    step_bias,
    decay_logarithm,
    head_skip_weight,
    segment,
    allowed,
):
    row_count = gate_x.shape[0]
    head_count = step_raw.shape[1]
    head_size = gate_x.shape[2] // head_count
    conv_out = jax.nn.silu(causal_conv(gate_x[:, 1], mixer_input_taps, segment))
    state_conv = jax.nn.silu(causal_conv(state_io, state_map_taps, segment))
    state_size = state_io.shape[1] // 2
    step_size = jax.nn.softplus(step_raw + step_bias)
    log_decay = -step_size * jnp.exp(decay_logarithm)
    mixed_out = state_mix(
        conv_out.reshape(row_count, head_count, head_size),
        step_size,
        log_decay,
        state_conv[:, :state_size],
        state_conv[:, state_size:],
        allowed,
        head_skip_weight,
    )
    return mixed_out.reshape(row_count, head_count * head_size) * jax.nn.silu(gate_x[:, 0])


def gated_gelu(gate_up_apply):
    return jax.nn.gelu(gate_up_apply[:, 0], approximate=True) * gate_up_apply[:, 1]


def head_sum(partial_rows):
    return lax.psum(partial_rows, "tensor")


def pair_sum(leading, trailing):
    return (
        lax.psum(leading.astype(jnp.bfloat16), "tensor").astype(jnp.float32),
        lax.psum(trailing.astype(jnp.bfloat16), "tensor").astype(jnp.float32),
    )


def row_sum(row_terms):
    return lax.psum(row_terms, "tensor")


def attention_scores(query_low, key_low, allowed):
    scale = query_low.shape[-1] ** (-0.5)
    scores = (
        jnp.einsum("thc,shc->hts", query_low, key_low, preferred_element_type=BROAD_DTYPE) * scale
    )
    return jnp.where(allowed[None], scores, MASKED)


def forward(weights, smalls, hid_rows, emb_rows, len_row):
    (
        query_key_value_weight,
        attention_output_weight,
        attention_gain,
        feedforward_gain,
        gate_up_weight,
        adapter_down,
        adapter_up,
        down_weight,
        shared_projection_weight,
        mixer_gain,
        mixer_input_weight,
        state_map_weight,
        step_weight,
        mixer_output_weight,
    ) = weights
    (
        mixer_input_taps,
        state_map_taps,
        step_bias,
        decay_logarithm,
        head_skip_weight,
        gated_norm_gain,
    ) = smalls
    row_count = hid_rows.shape[0]
    segment, position, valid, allowed = layout(len_row, row_count)
    head_count = attention_output_weight.shape[0] // HEAD
    joined = jnp.concatenate([hid_rows, emb_rows], axis=1).astype(BROAD_DTYPE)
    normed, attn_norm_back = jax.vjp(rms_norm, joined, attention_gain.astype(BROAD_DTYPE))
    attn_in = normed.astype(COMPACT_DTYPE)
    qkv_rows = jnp.einsum(
        "td,dkc->tkc", attn_in, query_key_value_weight, preferred_element_type=BROAD_DTYPE
    )
    (query, key_rot), rope_back = jax.vjp(
        partial(rope_pair, position=position),
        qkv_rows[:, 0].reshape(row_count, head_count, HEAD),
        qkv_rows[:, 1].reshape(row_count, head_count, HEAD),
    )
    query_low = query.astype(COMPACT_DTYPE)
    key_low = key_rot.astype(COMPACT_DTYPE)
    value_low = qkv_rows[:, 2].reshape(row_count, head_count, HEAD).astype(COMPACT_DTYPE)
    scores = attention_scores(query_low, key_low, allowed)
    row_max = jnp.max(scores, axis=-1, keepdims=True)
    log_total = row_max + jnp.log(jnp.sum(jnp.exp(scores - row_max), axis=-1, keepdims=True))
    probs = jnp.exp(scores - log_total)
    attended = jnp.einsum(
        "hts,shc->thc", probs.astype(COMPACT_DTYPE), value_low, preferred_element_type=BROAD_DTYPE
    )
    attended = attended.reshape(row_count, head_count * HEAD).astype(COMPACT_DTYPE)
    mid_res = joined + head_sum(
        jnp.dot(attended, attention_output_weight, preferred_element_type=BROAD_DTYPE)
    )
    mlp_normed, mlp_norm_back = jax.vjp(rms_norm, mid_res, feedforward_gain.astype(BROAD_DTYPE))
    feedforward_input = mlp_normed.astype(COMPACT_DTYPE)
    adapter_apply = jnp.dot(
        feedforward_input, adapter_down, preferred_element_type=BROAD_DTYPE
    ).astype(COMPACT_DTYPE)
    gate_up_apply = jnp.einsum(
        "td,dkc->tkc", feedforward_input, gate_up_weight, preferred_element_type=BROAD_DTYPE
    )
    gate_up_apply = gate_up_apply + jnp.einsum(
        "yb,bos->yos", adapter_apply, adapter_up, preferred_element_type=BROAD_DTYPE
    )
    activated, gate_back = jax.vjp(gated_gelu, gate_up_apply)
    hidden_low = activated.astype(COMPACT_DTYPE)
    block_low = (
        mid_res + head_sum(jnp.dot(hidden_low, down_weight, preferred_element_type=BROAD_DTYPE))
    ).astype(COMPACT_DTYPE)
    part_width = shared_projection_weight.shape[0]
    block_part = lax.dynamic_slice_in_dim(
        block_low, lax.axis_index("tensor") * part_width, part_width, 1
    )
    shared = head_sum(
        jnp.dot(block_part, shared_projection_weight, preferred_element_type=BROAD_DTYPE)
    ).astype(COMPACT_DTYPE)
    mamba_in = hid_rows.astype(BROAD_DTYPE) + shared.astype(BROAD_DTYPE)
    ssm_normed, ssm_norm_back = jax.vjp(rms_norm, mamba_in, mixer_gain.astype(BROAD_DTYPE))
    ssm_in = ssm_normed.astype(COMPACT_DTYPE)
    gate_x = jnp.einsum(
        "td,dkc->tkc", ssm_in, mixer_input_weight, preferred_element_type=BROAD_DTYPE
    )
    state_io = jnp.dot(ssm_in, state_map_weight, preferred_element_type=BROAD_DTYPE)
    step_raw = jnp.dot(ssm_in, step_weight, preferred_element_type=BROAD_DTYPE)
    gated, mix_back = jax.vjp(
        partial(mamba_local, segment=segment, allowed=allowed),
        gate_x,
        state_io,
        step_raw,
        mixer_input_taps,
        state_map_taps,
        step_bias,
        decay_logarithm,
        head_skip_weight,
    )
    squares = row_sum(jnp.sum(gated * gated, axis=1))
    row_scale = lax.rsqrt(squares / INNER + EPSILON)
    gated_norm = (gated * row_scale[:, None] * gated_norm_gain).astype(COMPACT_DTYPE)
    mamba_out = head_sum(
        jnp.dot(gated_norm, mixer_output_weight, preferred_element_type=BROAD_DTYPE)
    )
    result = ((mamba_in + mamba_out) * valid[:, None].astype(BROAD_DTYPE)).astype(COMPACT_DTYPE)
    stored = (
        valid,
        allowed,
        attn_norm_back,
        attn_in,
        rope_back,
        query_low,
        key_low,
        value_low,
        log_total,
        attended,
        mlp_norm_back,
        feedforward_input,
        adapter_apply,
        gate_back,
        hidden_low,
        block_part,
        ssm_norm_back,
        ssm_in,
        mix_back,
        gated,
        row_scale,
        gated_norm,
    )
    return (result, stored)


def backward(weights, smalls, stored, grad_rows):
    (
        query_key_value_weight,
        attention_output_weight,
        attention_gain,
        feedforward_gain,
        gate_up_weight,
        adapter_down,
        adapter_up,
        down_weight,
        shared_projection_weight,
        mixer_gain,
        mixer_input_weight,
        state_map_weight,
        step_weight,
        mixer_output_weight,
    ) = weights
    gated_norm_gain = smalls[5]
    (
        valid,
        allowed,
        attn_norm_back,
        attn_in,
        rope_back,
        query_low,
        key_low,
        value_low,
        log_total,
        attended,
        mlp_norm_back,
        feedforward_input,
        adapter_apply,
        gate_back,
        hidden_low,
        block_part,
        ssm_norm_back,
        ssm_in,
        mix_back,
        gated,
        row_scale,
        gated_norm,
    ) = stored
    row_count = grad_rows.shape[0]
    head_count = attention_output_weight.shape[0] // HEAD
    grad_low = grad_rows * valid[:, None].astype(COMPACT_DTYPE)
    grad_full = grad_low.astype(BROAD_DTYPE)
    grad_mout = jnp.dot(gated_norm.T, grad_low, preferred_element_type=BROAD_DTYPE)
    d_norm = jnp.dot(grad_low, mixer_output_weight.T, preferred_element_type=BROAD_DTYPE)
    grad_gain = jnp.sum(d_norm * gated * row_scale[:, None], axis=0)
    weighted = row_sum(jnp.sum(d_norm * gated_norm_gain * gated, axis=1))
    d_gated = (
        d_norm * gated_norm_gain * row_scale[:, None]
        - gated * (row_scale**3 * weighted / INNER)[:, None]
    )
    (
        d_gate_x,
        d_state_io,
        d_step_raw,
        grad_conv_x,
        grad_conv_part,
        grad_dt_bias,
        grad_a_log,
        grad_skip,
    ) = mix_back(d_gated)
    gate_x_low = d_gate_x.astype(COMPACT_DTYPE)
    step_low = d_step_raw.astype(COMPACT_DTYPE)
    grad_in = jnp.einsum("td,tkc->dkc", ssm_in, gate_x_low, preferred_element_type=BROAD_DTYPE)
    grad_dt = jnp.dot(ssm_in.T, step_low, preferred_element_type=BROAD_DTYPE)
    part_in = jnp.einsum(
        "tkc,dkc->td", gate_x_low, mixer_input_weight, preferred_element_type=BROAD_DTYPE
    )
    part_in = part_in + jnp.dot(step_low, step_weight.T, preferred_element_type=BROAD_DTYPE)
    summed_in, state_terms = pair_sum(
        part_in, jnp.concatenate([d_state_io, grad_conv_part], axis=0)
    )
    state_low = state_terms[:row_count].astype(COMPACT_DTYPE)
    grad_conv_bc = state_terms[row_count:]
    grad_bc = jnp.dot(ssm_in.T, state_low, preferred_element_type=BROAD_DTYPE)
    d_ssm = summed_in + jnp.dot(state_low, state_map_weight.T, preferred_element_type=BROAD_DTYPE)
    d_mamba_in, grad_g_mamba = ssm_norm_back(d_ssm)
    d_mamba_in = d_mamba_in + grad_full
    shared_low = d_mamba_in.astype(COMPACT_DTYPE)
    grad_proj = jnp.dot(block_part.T, shared_low, preferred_element_type=BROAD_DTYPE)
    d_block = lax.all_gather(
        jnp.dot(shared_low, shared_projection_weight.T, preferred_element_type=BROAD_DTYPE).astype(
            jnp.bfloat16
        ),
        "tensor",
        axis=1,
        tiled=True,
    ).astype(jnp.float32)
    mlp_low = d_block.astype(COMPACT_DTYPE)
    grad_down = jnp.dot(hidden_low.T, mlp_low, preferred_element_type=BROAD_DTYPE)
    (d_gate_up,) = gate_back(jnp.dot(mlp_low, down_weight.T, preferred_element_type=BROAD_DTYPE))
    gate_up_apply_low = d_gate_up.astype(COMPACT_DTYPE)
    grad_gate_up = jnp.einsum(
        "td,tkc->dkc", feedforward_input, gate_up_apply_low, preferred_element_type=BROAD_DTYPE
    )
    adapter_up_gradient = jnp.einsum(
        "wa,whd->ahd", adapter_apply, gate_up_apply_low, preferred_element_type=BROAD_DTYPE
    )
    feedforward_summed, d_adapter = pair_sum(
        jnp.einsum(
            "tkc,dkc->td", gate_up_apply_low, gate_up_weight, preferred_element_type=BROAD_DTYPE
        ),
        jnp.einsum(
            "yoi,voi->yv", gate_up_apply_low, adapter_up, preferred_element_type=BROAD_DTYPE
        ),
    )
    adapter_apply_low = d_adapter.astype(COMPACT_DTYPE)
    adapter_down_gradient = jnp.dot(
        feedforward_input.T, adapter_apply_low, preferred_element_type=BROAD_DTYPE
    )
    d_mid, grad_g_mlp = mlp_norm_back(
        feedforward_summed
        + jnp.dot(adapter_apply_low, adapter_down.T, preferred_element_type=BROAD_DTYPE)
    )
    d_mid = d_mid + d_block
    attn_low = d_mid.astype(COMPACT_DTYPE)
    grad_out_w = jnp.dot(attended.T, attn_low, preferred_element_type=BROAD_DTYPE)
    d_attended = jnp.dot(
        attn_low, attention_output_weight.T, preferred_element_type=BROAD_DTYPE
    ).astype(COMPACT_DTYPE)
    d_attended = d_attended.reshape(row_count, head_count, HEAD)
    probs = jnp.exp(attention_scores(query_low, key_low, allowed) - log_total)
    d_values = jnp.einsum(
        "hts,thc->shc", probs.astype(COMPACT_DTYPE), d_attended, preferred_element_type=BROAD_DTYPE
    )
    d_probs = jnp.einsum("thc,shc->hts", d_attended, value_low, preferred_element_type=BROAD_DTYPE)
    d_scores = probs * (d_probs - jnp.sum(probs * d_probs, axis=-1, keepdims=True)) * HEAD ** (-0.5)
    d_scores = d_scores.astype(COMPACT_DTYPE)
    d_query = jnp.einsum("hts,shc->thc", d_scores, key_low, preferred_element_type=BROAD_DTYPE)
    d_key = jnp.einsum("hts,thc->shc", d_scores, query_low, preferred_element_type=BROAD_DTYPE)
    d_query, d_key = rope_back((d_query, d_key))
    d_qkv = jnp.stack(
        [
            d_query.reshape(row_count, -1),
            d_key.reshape(row_count, -1),
            d_values.reshape(row_count, -1),
        ],
        axis=1,
    ).astype(COMPACT_DTYPE)
    grad_qkv = jnp.einsum("td,tkc->dkc", attn_in, d_qkv, preferred_element_type=BROAD_DTYPE)
    d_joined, grad_g_attn = attn_norm_back(
        head_sum(
            jnp.einsum(
                "tkc,dkc->td", d_qkv, query_key_value_weight, preferred_element_type=BROAD_DTYPE
            )
        )
    )
    d_joined = d_joined + d_mid
    model_width = d_mamba_in.shape[1]
    d_hid = (d_joined[:, :model_width] + d_mamba_in).astype(COMPACT_DTYPE)
    d_emb = d_joined[:, model_width:].astype(COMPACT_DTYPE)
    grads = (
        grad_qkv,
        grad_out_w,
        grad_g_attn,
        grad_g_mlp,
        grad_gate_up,
        adapter_down_gradient,
        adapter_up_gradient,
        grad_down,
        grad_proj,
        grad_g_mamba,
        grad_in,
        grad_bc,
        grad_dt,
        grad_mout,
    )
    small_grads = (grad_conv_x, grad_conv_bc, grad_dt_bias, grad_a_log, grad_skip, grad_gain)
    return (d_hid, d_emb, grads, small_grads)


def local(
    hidden,
    embedding,
    lengths,
    query_key_value_weight,
    attention_output_weight,
    attention_gain,
    feedforward_gain,
    gate_up_weight,
    adapter_down,
    adapter_up,
    down_weight,
    shared_projection_weight,
    mixer_gain,
    mixer_input_weight,
    state_map_weight,
    step_weight,
    mixer_output_weight,
    mixer_input_taps,
    state_map_taps,
    step_bias,
    decay_logarithm,
    head_skip_weight,
    gated_norm_gain,
    cotangent,
):
    smalls = (
        mixer_input_taps,
        state_map_taps,
        step_bias,
        decay_logarithm,
        head_skip_weight,
        gated_norm_gain,
    )
    results = []
    hid_grads = []
    emb_grads = []
    grad_sums = None
    small_sums = None
    for batch in range(hidden.shape[0]):
        gathered = (
            lax.all_gather(query_key_value_weight, "dp", axis=0, tiled=True),
            lax.all_gather(attention_output_weight, "dp", axis=1, tiled=True),
            lax.all_gather(attention_gain, "dp", axis=0, tiled=True),
            lax.all_gather(feedforward_gain, "dp", axis=0, tiled=True),
            lax.all_gather(gate_up_weight, "dp", axis=0, tiled=True),
            lax.all_gather(adapter_down, "dp", axis=0, tiled=True),
            lax.all_gather(adapter_up, "dp", axis=0, tiled=True),
            lax.all_gather(down_weight, "dp", axis=1, tiled=True),
            lax.all_gather(shared_projection_weight, "dp", axis=1, tiled=True),
            lax.all_gather(mixer_gain, "dp", axis=0, tiled=True),
            lax.all_gather(mixer_input_weight, "dp", axis=0, tiled=True),
            lax.all_gather(state_map_weight, "dp", axis=0, tiled=True),
            lax.all_gather(step_weight, "dp", axis=0, tiled=True),
            lax.all_gather(mixer_output_weight, "dp", axis=1, tiled=True),
        )
        result, stored = forward(
            gathered, smalls, hidden[batch], embedding[batch], lengths[batch, 0]
        )
        regained = (
            lax.all_gather(query_key_value_weight, "dp", axis=0, tiled=True),
            lax.all_gather(attention_output_weight, "dp", axis=1, tiled=True),
            lax.all_gather(attention_gain, "dp", axis=0, tiled=True),
            lax.all_gather(feedforward_gain, "dp", axis=0, tiled=True),
            lax.all_gather(gate_up_weight, "dp", axis=0, tiled=True),
            lax.all_gather(adapter_down, "dp", axis=0, tiled=True),
            lax.all_gather(adapter_up, "dp", axis=0, tiled=True),
            lax.all_gather(down_weight, "dp", axis=1, tiled=True),
            lax.all_gather(shared_projection_weight, "dp", axis=1, tiled=True),
            lax.all_gather(mixer_gain, "dp", axis=0, tiled=True),
            lax.all_gather(mixer_input_weight, "dp", axis=0, tiled=True),
            lax.all_gather(state_map_weight, "dp", axis=0, tiled=True),
            lax.all_gather(step_weight, "dp", axis=0, tiled=True),
            lax.all_gather(mixer_output_weight, "dp", axis=1, tiled=True),
        )
        d_hid, d_emb, grads, small_grads = backward(regained, smalls, stored, cotangent[batch])
        grad_sums = grads if grad_sums is None else jax.tree.map(jnp.add, grad_sums, tuple(grads))
        small_sums = (
            small_grads if small_sums is None else jax.tree.map(jnp.add, small_sums, small_grads)
        )
        results.append(result)
        hid_grads.append(d_hid)
        emb_grads.append(d_emb)
    grad_sums = (
        lax.psum_scatter(
            grad_sums[0].astype(jnp.bfloat16), "dp", scatter_dimension=0, tiled=True
        ).astype(jnp.float32),
        lax.psum_scatter(
            grad_sums[1].astype(jnp.bfloat16), "dp", scatter_dimension=1, tiled=True
        ).astype(jnp.float32),
        lax.psum_scatter(
            grad_sums[2].astype(jnp.bfloat16), "dp", scatter_dimension=0, tiled=True
        ).astype(jnp.float32),
        lax.psum_scatter(
            grad_sums[3].astype(jnp.bfloat16), "dp", scatter_dimension=0, tiled=True
        ).astype(jnp.float32),
        lax.psum_scatter(
            grad_sums[4].astype(jnp.bfloat16), "dp", scatter_dimension=0, tiled=True
        ).astype(jnp.float32),
        lax.psum_scatter(
            grad_sums[5].astype(jnp.bfloat16), "dp", scatter_dimension=0, tiled=True
        ).astype(jnp.float32),
        lax.psum_scatter(
            grad_sums[6].astype(jnp.bfloat16), "dp", scatter_dimension=0, tiled=True
        ).astype(jnp.float32),
        lax.psum_scatter(
            grad_sums[7].astype(jnp.bfloat16), "dp", scatter_dimension=1, tiled=True
        ).astype(jnp.float32),
        lax.psum_scatter(
            grad_sums[8].astype(jnp.bfloat16), "dp", scatter_dimension=1, tiled=True
        ).astype(jnp.float32),
        lax.psum_scatter(
            grad_sums[9].astype(jnp.bfloat16), "dp", scatter_dimension=0, tiled=True
        ).astype(jnp.float32),
        lax.psum_scatter(
            grad_sums[10].astype(jnp.bfloat16), "dp", scatter_dimension=0, tiled=True
        ).astype(jnp.float32),
        lax.psum_scatter(
            grad_sums[11].astype(jnp.bfloat16), "dp", scatter_dimension=0, tiled=True
        ).astype(jnp.float32),
        lax.psum_scatter(
            grad_sums[12].astype(jnp.bfloat16), "dp", scatter_dimension=0, tiled=True
        ).astype(jnp.float32),
        lax.psum_scatter(
            grad_sums[13].astype(jnp.bfloat16), "dp", scatter_dimension=1, tiled=True
        ).astype(jnp.float32),
    )
    small_sums = lax.psum(
        (small_sums[0], small_sums[1], small_sums[2], small_sums[3], small_sums[4], small_sums[5]),
        "dp",
    )
    return (
        jnp.stack(results),
        jnp.stack(hid_grads),
        jnp.stack(emb_grads),
        grad_sums[0],
        grad_sums[1],
        grad_sums[2],
        grad_sums[3],
        grad_sums[4],
        grad_sums[5],
        grad_sums[6],
        grad_sums[7],
        grad_sums[8],
        grad_sums[9],
        grad_sums[10],
        grad_sums[11],
        grad_sums[12],
        grad_sums[13],
        small_sums[0],
        small_sums[1],
        small_sums[2],
        small_sums[3],
        small_sums[4],
        small_sums[5],
    )


def solution(mesh):
    placed = (
        P(None, "dp", None),
        P(None, "dp", None),
        P(None, "dp", None),
        P("dp", None, "tensor"),
        P("tensor", "dp"),
        P("dp"),
        P("dp"),
        P("dp", None, "tensor"),
        P("dp", None),
        P("dp", None, "tensor"),
        P("tensor", "dp"),
        P("tensor", "dp"),
        P("dp"),
        P("dp", None, "tensor"),
        P("dp", None),
        P("dp", "tensor"),
        P("tensor", "dp"),
        P(None, "tensor"),
        P(),
        P("tensor"),
        P("tensor"),
        P("tensor"),
        P("tensor"),
        P(None, "dp", None),
    )
    return jax.shard_map(
        local,
        mesh=mesh,
        in_specs=placed,
        out_specs=(
            P(None, "dp", None),
            P(None, "dp", None),
            P(None, "dp", None),
            P("dp", None, "tensor"),
            P("tensor", "dp"),
            P("dp"),
            P("dp"),
            P("dp", None, "tensor"),
            P("dp", None),
            P("dp", None, "tensor"),
            P("tensor", "dp"),
            P("tensor", "dp"),
            P("dp"),
            P("dp", None, "tensor"),
            P("dp", None),
            P("dp", "tensor"),
            P("tensor", "dp"),
            P(None, "tensor"),
            P(),
            P("tensor"),
            P("tensor"),
            P("tensor"),
            P("tensor"),
        ),
        check_vma=False,
    )
```

profile of v0, /device:TPU:0, one launch (start us, length us, event | category | flops | bytes accessed | tf_op | source)
XLA Modules:
  0.0 2563.2 jit_solution(10330663971500474526)
XLA Ops:
  21.8 116.2 %all-gather.16.cloned.1.call-done = bf16[4096,3,1024]{2,0,1:T(8,128)(2,1)} async-done(((bf16[512,3,1024]{2,0,1:T(8,128)(2,1)}), bf16[4096,3,1024]{2,0,1:T(8,128)(2,1)}) %all-gather.16.cloned.1.call-update) | async-done | bytes 25165840 | tf_op jit(solution)/shard_map/all_gather | solution.py:480
  163.3 32.6 %all-gather.18.cloned.1.call-done = bf16[1024,4096]{1,0:T(8,128)(2,1)} async-done(((bf16[1024,512]{1,0:T(8,128)(2,1)}), bf16[1024,4096]{1,0:T(8,128)(2,1)}) %all-gather.18.cloned.1.call-update) | async-done | bytes 8388624 | tf_op jit(solution)/shard_map/all_gather | solution.py:481
  235.1 125.1 %all-reduce.92.cloned.1.call-done = (f32[128,4096]{1,0:T(8,128)}, f32[128,4096]{1,0:T(8,128)}) async-done(((f32[128,4096]{1,0:T(8,128)}, f32[128,4096]{1,0:T(8,128)}), (f32[128,4096]{1,0:T(8,128)}, f32[128,4096]{1,0:T(8,128)})) %all-reduce.92.cloned.1.call-update) | async-done | bytes 4194320 | tf_op jit(solution)/shard_map/psum | solution.py:114
  366.1 18.6 all-gather.22.cloned.1.call-done
  386.9 161.0 %all-gather.20.cloned.1.call-done = bf16[4096,2,2048]{2,0,1:T(8,128)(2,1)} async-done(((bf16[512,2,2048]{2,0,1:T(8,128)(2,1)}), bf16[4096,2,2048]{2,0,1:T(8,128)(2,1)}) %all-gather.20.cloned.1.call-update) | async-done | bytes 33554448 | tf_op jit(solution)/shard_map/all_gather | solution.py:484
  548.0 14.3 fusion.65
  576.4 15.5 fusion.69
  594.0 75.1 %all-gather.26.cloned.1.call-done = bf16[2048,4096]{1,0:T(8,128)(2,1)} async-done(((bf16[2048,512]{1,0:T(8,128)(2,1)}), bf16[2048,4096]{1,0:T(8,128)(2,1)}) %all-gather.26.cloned.1.call-update) | async-done | bytes 16777232 | tf_op jit(solution)/shard_map/all_gather | solution.py:487
  714.4 153.5 %all-reduce.90.cloned.1.call-done = (f32[128,4096]{1,0:T(8,128)}, f32[128,4096]{1,0:T(8,128)}) async-done(((f32[128,4096]{1,0:T(8,128)}, f32[128,4096]{1,0:T(8,128)}), (f32[128,4096]{1,0:T(8,128)}, f32[128,4096]{1,0:T(8,128)})) %all-reduce.90.cloned.1.call-update) | async-done | bytes 4194320 | tf_op jit(solution)/shard_map/psum | solution.py:114
  869.2 36.9 %all-gather.28.cloned.1.call-done = bf16[1024,2048]{1,0:T(8,128)(2,1)} async-done(((bf16[1024,256]{1,0:T(8,128)(2,1)}), bf16[1024,2048]{1,0:T(8,128)(2,1)}) %all-gather.28.cloned.1.call-update) | async-done | bytes 4194320 | tf_op jit(solution)/shard_map/all_gather | solution.py:488
  913.0 79.6 %all-reduce.99 = (bf16[128,2048]{1,0:T(8,128)(2,1)}, bf16[128,2048]{1,0:T(8,128)(2,1)}) all-reduce(f32[128,2048]{1,0:T(8,128)} %fusion.348, f32[128,2048]{1,0:T(8,128)} %fusion.352), channel_id=1, replica_groups=mesh['dp'=8,'tensor'=4] {'tensor'}, use_global_device_ids=true, to_apply=%region_9.10 | all-reduce | flops 524288 | bytes 3145728 | tf_op jit(solution)/shard_map/psum | solution.py:114
  1154.2 55.0 %all-reduce.98.cloned.1.call-done = (bf16[128,2048]{1,0:T(8,128)(2,1)}, bf16[132,256]{1,0:T(8,128)(2,1)}, bf16[128,2048]{1,0:T(8,128)(2,1)}, bf16[132,256]{1,0:T(8,128)(2,1)}) async-done(((bf16[128,2048]{1,0:T(8,128)(2,1)}, bf16[132,256]{1,0:T(8,128)(2,1)}, bf16[128,2048]{1,0:T(8,128)(2,1)}, bf16[132,256]{1,0:T(8,128)(2,1)}), (bf16[128,2048]{1,0:T(8,128)(2,1)}, bf16[132,256]{1,0:T(8,128)(2,1)}, ...) | async-done | bytes 1183760 | tf_op jit(solution)/shard_map/psum | solution.py:119
  1224.7 22.5 all-gather.38.cloned.1.call-done
  1247.1 14.1 multiply_bitcast_fusion
  1295.8 17.2 fusion.2
  1313.0 16.4 fusion.3
  1360.1 59.4 %all-reduce.96.cloned.1.call-done = (bf16[128,4096]{1,0:T(8,128)(2,1)}, bf16[128,4096]{1,0:T(8,128)(2,1)}) async-done(((bf16[128,4096]{1,0:T(8,128)(2,1)}, bf16[128,4096]{1,0:T(8,128)(2,1)}), (bf16[128,4096]{1,0:T(8,128)(2,1)}, bf16[128,4096]{1,0:T(8,128)(2,1)})) %all-reduce.96.cloned.1.call-update) | async-done | bytes 2097168 | tf_op jit(solution)/shard_map/psum | solution.py:119
  1489.8 14.3 convolution_bitcast_fusion.2
  1504.1 14.3 convolution_bitcast_fusion
  1574.8 19.2 add_convert_fusion.2
  1595.3 20.9 fusion.94
  1616.2 27.0 %add_convert_fusion.1 = bf16[4096,3,1024]{2,0,1:T(8,128)(2,1)} fusion(f32[4096,3,1024]{2,0,1:T(8,128)} %fusion.94, f32[128]{0:T(128)S(1)} %copy-done.175, f32[4096]{0:T(1024)S(1)} %bitcast.499, bf16[128,1,1024]{2,0,1:T(8,128)(2,1)S(1)} %copy.361, bf16[128,1,1024]{2,0,1:T(8,128)(2,1)S(1)} %copy-done.87, bf16[128,1,1024]{2,0,1:T(8,128)(2,1)S(1)} %copy-done.86, ...), kind=kOutput, calls=%fused_computation.3 | convolution fusion | flops 3252420608 | bytes 77349376 | tf_op jit(solution)/shard_map/td,tkc->dkc/dot_general | solution.py:407
  1644.8 24.1 fusion.67
  1668.9 33.9 %add_convert_fusion = bf16[4096,2,2048]{2,0,1:T(8,128)(2,1)} fusion(f32[4096,2,2048]{2,0,1:T(8,128)} %fusion.67, bf16[128,2,2048]{2,0,1:T(8,128)(2,1)} %add_convert_fusion.7, bf16[128,4096]{1,0:T(8,128)(2,1)S(1)} %copy-done.14), kind=kOutput, calls=%fused_computation.2 | convolution fusion | flops 4328521728 | bytes 102760448 | tf_op jit(solution)/shard_map/td,tkc->dkc/dot_general | solution.py:360
  1708.0 26.0 %all-reduce.69 = (f32[4,1024]{1,0:T(4,128)}, f32[4,256]{1,0:T(4,128)}, f32[16]{0:T(128)}, f32[16]{0:T(128)}, f32[16]{0:T(128)}, /*index=5*/f32[1024]{0:T(1024)}) all-reduce(f32[4,1024]{1,0:T(4,128)S(1)} %add_add_fusion.6, f32[4,256]{1,0:T(4,128)S(1)} %convert_add_fusion.4, ...), channel_id=1, replica_groups=mesh['dp'=8,'tensor'=4] {'dp'}, use_global_device_ids=true, to_apply=%region_98.100 | all-reduce | flops 6192 | bytes 49536 | tf_op jit(solution)/shard_map/psum | solution.py:566
  1743.5 165.1 %all-reduce.88.cloned.1.call-done = (f32[128,2048]{1,0:T(8,128)}, f32[128,2048]{1,0:T(8,128)}, f32[128,4096]{1,0:T(8,128)}, f32[128,4096]{1,0:T(8,128)}) async-done(((f32[128,2048]{1,0:T(8,128)}, f32[128,2048]{1,0:T(8,128)}, f32[128,4096]{1,0:T(8,128)}, f32[128,4096]{1,0:T(8,128)}), (f32[128,2048]{1,0:T(8,128)}, f32[128,2048]{1,0:T(8,128)}, f32[128,4096]{1,0:T(8,128)}, ...) | async-done | bytes 6291472 | tf_op jit(solution)/shard_map/psum | solution.py:114
  1912.4 24.3 all-reduce.76
  1950.3 31.8 %reduce-scatter.26.cloned.1.call-done = bf16[256,2,1024]{2,0,1:T(8,128)(2,1)} async-done(((bf16[2048,2,1024]{2,0,1:T(8,128)(2,1)}), bf16[256,2,1024]{2,0,1:T(8,128)(2,1)}) %reduce-scatter.26.cloned.1.call-update) | async-done | bytes 1048592 | tf_op jit(solution)/shard_map/reduce_scatter | solution.py:553
  1985.8 72.0 %reduce-scatter.14.cloned.1.call-done = bf16[1024,512]{1,0:T(8,128)(2,1)} async-done(((bf16[1024,4096]{1,0:T(8,128)(2,1)}), bf16[1024,512]{1,0:T(8,128)(2,1)}) %reduce-scatter.14.cloned.1.call-update) | async-done | bytes 1048592 | tf_op jit(solution)/shard_map/reduce_scatter | solution.py:526
  2060.6 116.6 %reduce-scatter.22.cloned.1.call-done = bf16[2048,512]{1,0:T(8,128)(2,1)} async-done(((bf16[2048,4096]{1,0:T(8,128)(2,1)}), bf16[2048,512]{1,0:T(8,128)(2,1)}) %reduce-scatter.22.cloned.1.call-update) | async-done | bytes 2097168 | tf_op jit(solution)/shard_map/reduce_scatter | solution.py:544
  2181.4 156.3 %reduce-scatter.12.cloned.1.call-done = bf16[512,3,1024]{2,0,1:T(8,128)(2,1)} async-done(((bf16[4096,3,1024]{2,0,1:T(8,128)(2,1)}), bf16[512,3,1024]{2,0,1:T(8,128)(2,1)}) %reduce-scatter.12.cloned.1.call-update) | async-done | bytes 3145744 | tf_op jit(solution)/shard_map/reduce_scatter | solution.py:523
  2343.0 203.5 %reduce-scatter.16.cloned.1.call-done = bf16[512,2,2048]{2,0,1:T(8,128)(2,1)} async-done(((bf16[4096,2,2048]{2,0,1:T(8,128)(2,1)}), bf16[512,2,2048]{2,0,1:T(8,128)(2,1)}) %reduce-scatter.16.cloned.1.call-update) | async-done | bytes 4194320 | tf_op jit(solution)/shard_map/reduce_scatter | solution.py:535
  (817 shorter events, 582.2 us)
Async XLA Ops:
  7.2 130.8 %all-gather.16.cloned.1.call-start = ((), (), s32[]{:S(2)}) async-start(), calls=%async_computation.11 | async-start | bytes 28311552 | tf_op jit(solution)/shard_map/all_gather | solution.py:480
  8.0 187.9 %all-gather.18.cloned.1.call-start = ((), (), s32[]{:S(2)}) async-start(), calls=%async_computation.12 | async-start | bytes 9437184 | tf_op jit(solution)/shard_map/all_gather | solution.py:481
  8.7 351.5 %all-reduce.92.cloned.1.call-start = ((), (), s32[]{:S(2)}) async-start(), calls=%async_computation.36 | async-start | bytes 8388608 | tf_op jit(solution)/shard_map/psum | solution.py:114
  19.8 340.4 %copy-start.31 = (bf16[128,2048]{1,0:T(8,128)(2,1)}, bf16[128,2048]{1,0:T(8,128)(2,1)S(1)}, u32[]{:S(2)}) copy-start(bf16[128,2048]{1,0:T(8,128)(2,1)S(1)} %get-tuple-element.265) | copy-start | bytes 1572868
  19.9 342.6 %copy-start.28 = (bf16[128,2048]{1,0:T(8,128)(2,1)}, bf16[128,2048]{1,0:T(8,128)(2,1)S(1)}, u32[]{:S(2)}) copy-start(bf16[128,2048]{1,0:T(8,128)(2,1)S(1)} %get-tuple-element.264) | copy-start | bytes 1572868
  204.7 179.9 %all-gather.22.cloned.1.call-start = ((), (), s32[]{:S(2)}) async-start(), calls=%async_computation.14 | async-start | bytes 1179648 | tf_op jit(solution)/shard_map/all_gather | solution.py:485
  205.3 342.7 %all-gather.20.cloned.1.call-start = ((), (), s32[]{:S(2)}) async-start(), calls=%async_computation.13 | async-start | bytes 37748736 | tf_op jit(solution)/shard_map/all_gather | solution.py:484
  223.0 350.9 %all-gather.24.cloned.1.call-start = ((), (), s32[]{:S(2)}) async-start(), calls=%async_computation.15 | async-start | bytes 1179648 | tf_op jit(solution)/shard_map/all_gather | solution.py:486
  224.6 444.5 %all-gather.26.cloned.1.call-start = ((), (), s32[]{:S(2)}) async-start(), calls=%async_computation.16 | async-start | bytes 18874368 | tf_op jit(solution)/shard_map/all_gather | solution.py:487
  225.4 484.5 %all-gather.34.cloned.1.call-start = ((), (), s32[]{:S(2)}) async-start(), calls=%async_computation.20 | async-start | bytes 4718592 | tf_op jit(solution)/shard_map/all_gather | solution.py:493
  226.1 641.8 %all-reduce.90.cloned.1.call-start = ((), (), s32[]{:S(2)}) async-start(), calls=%async_computation.35 | async-start | bytes 8388608 | tf_op jit(solution)/shard_map/psum | solution.py:114
  366.1 181.9 %copy-start.12 = (bf16[128,4096]{1,0:T(8,128)(2,1)}, bf16[128,4096]{1,0:T(8,128)(2,1)S(1)}, u32[]{:S(2)}) copy-start(bf16[128,4096]{1,0:T(8,128)(2,1)S(1)} %get-tuple-element.316) | copy-start | bytes 3145732
  684.6 221.5 %all-gather.28.cloned.1.call-start = ((), (), s32[]{:S(2)}) async-start(), calls=%async_computation.17 | async-start | bytes 4718592 | tf_op jit(solution)/shard_map/all_gather | solution.py:488
  685.2 320.5 %all-gather.32.cloned.1.call-start = ((), (), s32[]{:S(2)}) async-start(), calls=%async_computation.19 | async-start | bytes 1179648 | tf_op jit(solution)/shard_map/all_gather | solution.py:491
  685.9 326.5 %all-gather.30.cloned.1.call-start = ((), (), s32[]{:S(2)}) async-start(), calls=%async_computation.18 | async-start | bytes 9437184 | tf_op jit(solution)/shard_map/all_gather | solution.py:490
  688.5 520.7 %all-reduce.98.cloned.1.call-start = ((), (), s32[]{:S(2)}) async-start(), calls=%async_computation.39 | async-start | bytes 2375680 | tf_op jit(solution)/shard_map/psum | solution.py:119
  1154.1 93.0 %all-gather.38.cloned.1.call-start = ((), (), s32[]{:S(2)}) async-start(), calls=%async_computation.22 | async-start | bytes 1310720 | tf_op jit(solution)/shard_map/all_gather | solution.py:348
  1219.4 57.2 %all-gather.36.cloned.1.call-start = ((), (), s32[]{:S(2)}) async-start(), calls=%async_computation.21 | async-start | bytes 1310720 | tf_op jit(solution)/shard_map/all_gather | solution.py:348
  1224.2 114.0 %all-reduce.94.cloned.1.call-start = ((), (), s32[]{:S(2)}) async-start(), calls=%async_computation.37 | async-start | bytes 131072 | tf_op jit(solution)/shard_map/psum | solution.py:120
  1295.6 124.0 %all-reduce.96.cloned.1.call-start = ((), (), s32[]{:S(2)}) async-start(), calls=%async_computation.38 | async-start | bytes 4194304 | tf_op jit(solution)/shard_map/psum | solution.py:119
  1329.5 376.6 %reduce-scatter.30.cloned.1.call-start = ((), (), s32[]{:S(2)}) async-start(), calls=%async_computation.32 | async-start | bytes 73728 | tf_op jit(solution)/shard_map/reduce_scatter | solution.py:559
  1331.1 403.0 %reduce-scatter.28.cloned.1.call-start = ((), (), s32[]{:S(2)}) async-start(), calls=%async_computation.31 | async-start | bytes 1179648 | tf_op jit(solution)/shard_map/reduce_scatter | solution.py:556
  1334.8 401.0 %reduce-scatter.20.cloned.1.call-start = ((), (), s32[]{:S(2)}) async-start(), calls=%async_computation.27 | async-start | bytes 1179648 | tf_op jit(solution)/shard_map/reduce_scatter | solution.py:541
  1338.1 399.5 %reduce-scatter.18.cloned.1.call-start = ((), (), s32[]{:S(2)}) async-start(), calls=%async_computation.26 | async-start | bytes 1179648 | tf_op jit(solution)/shard_map/reduce_scatter | solution.py:538
  1341.6 397.7 %reduce-scatter.32.cloned.1.call-start = ((), (), s32[]{:S(2)}) async-start(), calls=%async_computation.33 | async-start | bytes 4718592 | tf_op jit(solution)/shard_map/reduce_scatter | solution.py:562
  1349.0 392.4 %reduce-scatter.24.cloned.1.call-start = ((), (), s32[]{:S(2)}) async-start(), calls=%async_computation.29 | async-start | bytes 4718592 | tf_op jit(solution)/shard_map/reduce_scatter | solution.py:547
  1359.7 548.9 %all-reduce.88.cloned.1.call-start = ((), (), s32[]{:S(2)}) async-start(), calls=%async_computation.34 | async-start | bytes 12582912 | tf_op jit(solution)/shard_map/psum | solution.py:114
  1518.5 463.7 %reduce-scatter.26.cloned.1.call-start = ((), (), s32[]{:S(2)}) async-start(), calls=%async_computation.30 | async-start | bytes 9437184 | tf_op jit(solution)/shard_map/reduce_scatter | solution.py:553
  1539.6 518.1 %reduce-scatter.14.cloned.1.call-start = ((), (), s32[]{:S(2)}) async-start(), calls=%async_computation.24 | async-start | bytes 9437184 | tf_op jit(solution)/shard_map/reduce_scatter | solution.py:526
  1560.3 616.9 %reduce-scatter.22.cloned.1.call-start = ((), (), s32[]{:S(2)}) async-start(), calls=%async_computation.28 | async-start | bytes 18874368 | tf_op jit(solution)/shard_map/reduce_scatter | solution.py:544
  1594.1 743.6 %reduce-scatter.12.cloned.1.call-start = ((), (), s32[]{:S(2)}) async-start(), calls=%async_computation.23 | async-start | bytes 28311552 | tf_op jit(solution)/shard_map/reduce_scatter | solution.py:523
  1643.2 903.3 %reduce-scatter.16.cloned.1.call-start = ((), (), s32[]{:S(2)}) async-start(), calls=%async_computation.25 | async-start | bytes 37748736 | tf_op jit(solution)/shard_map/reduce_scatter | solution.py:535
  (238 other events, 3892.1 us)
Sparse Core Ops, SparseCore 0:
  10.0 128.0 all-gather.15
  139.9 55.9 all-gather.17
  204.8 155.3 all-reduce.91
  362.1 22.4 all-gather.21
  387.1 160.7 all-gather.19
  550.5 23.4 all-gather.23
  576.0 93.0 all-gather.25
  671.2 37.6 all-gather.33
  712.6 155.3 all-reduce.89
  869.7 36.4 all-gather.27
  908.0 23.4 all-gather.31
  933.9 54.3 all-gather.29
  1154.2 54.8 all-reduce.97
  1219.5 27.5 all-gather.37
  1249.2 27.4 all-gather.35
  1295.7 33.6 all-reduce.93
  1332.8 86.7 all-reduce.95
  1422.7 30.4 reduce-scatter.29
  1456.3 36.0 reduce-scatter.27
  1495.4 36.0 reduce-scatter.19
  1534.7 35.9 reduce-scatter.17
  1574.6 51.2 reduce-scatter.31
  1630.3 51.3 reduce-scatter.23
  1684.7 223.8 all-reduce.87
  1912.0 70.1 reduce-scatter.25
  1986.5 71.2 reduce-scatter.13
  2061.2 115.9 reduce-scatter.21
  2180.8 156.8 reduce-scatter.11
  2341.3 205.2 reduce-scatter.15
where the time goes:
time: 2580 us; the launch traced here: 2560 us
  waiting for transfers between devices  1630 us (63%)
  matrix products  495 us (19%)
  blocking collectives  187 us (7%)
  other arithmetic  111 us (4%)
  local copies, waits for them, and re-layouts  107 us (4%)
    psum x3, waiting for transfers between devices, head_sum(): return lax.psum(partial_rows, 'tensor')  444 us
    reduce_scatter x1, waiting for transfers between devices, local(): lax.psum_scatter(grad_sums[4].astype(jnp.bfloat16), 'dp', scatter_dimensi...  203 us
    all_gather x1, waiting for transfers between devices, local(): lax.all_gather(gate_up_weight, 'dp', axis=0, tiled=True)  161 us
    reduce_scatter x1, waiting for transfers between devices, local(): lax.psum_scatter(grad_sums[0].astype(jnp.bfloat16), 'dp', scatter_dimensi...  156 us
    reduce_scatter x1, waiting for transfers between devices, local(): lax.psum_scatter(grad_sums[7].astype(jnp.bfloat16), 'dp', scatter_dimensi...  117 us
    all_gather x1, waiting for transfers between devices, local(): lax.all_gather(query_key_value_weight, 'dp', axis=0, tiled=True)  116 us
    psum x2, waiting for transfers between devices, pair_sum(): lax.psum(leading.astype(jnp.bfloat16), 'tensor').astype(jnp.float32)  114 us
    psum x1, blocking collectives, head_sum(): return lax.psum(partial_rows, 'tensor')  79.6 us
  transfers between devices with their start and end apart: 29, of which 19 were waited for; matrix products, arithmetic and copies ran while one was open for 21% of the time, Pallas kernels for 0%

commit v1 on v0

v1 whole, which is shorter than its diff:
```python
from functools import partial
from types import SimpleNamespace

import jax
import jax.numpy as jnp
from jax import lax
from jax.experimental import pallas as pl
from jax.experimental.pallas import tpu as pltpu
from jax.sharding import PartitionSpec as P

HEAD = 128
EPSILON = 1e-05
ROPE_BASE = 10000.0
MASKED = -1e30
TOP_PRECISION = lax.Precision.HIGHEST
F32 = jnp.float32
BF16 = jnp.bfloat16


def layout(len_row, places):
    bounds = jnp.cumsum(len_row)[:-1]
    passed = places[:, None] >= bounds[None, :]
    segment = jnp.sum(passed.astype(jnp.int32), axis=1)
    starts = jnp.max(jnp.where(passed, bounds[None, :], 0), axis=1)
    position = places - starts
    valid = segment < bounds.shape[0]
    allowed = (segment[:, None] == segment[None, :]) & (places[None, :] <= places[:, None])
    return (segment, position, valid, allowed)


def rope_tables(position):
    half = HEAD // 2
    frequency = ROPE_BASE ** (-2.0 * jnp.arange(half, dtype=F32) / HEAD)
    angles = position.astype(F32)[:, None] * frequency[None, :]
    cosine, sine = jnp.cos(angles), jnp.sin(angles)
    return jnp.concatenate([cosine, cosine], axis=1), jnp.concatenate([-sine, sine], axis=1)


def rows_down(x, count):
    return x if count == 0 else pltpu.roll(x, count, 0)


def rows_up(x, count):
    return x if count == 0 else pltpu.roll(x, x.shape[0] - count, 0)


def conv_taps(x, taps_ref, same_ref):
    summed = x * taps_ref[0:1, :]
    for j in range(1, taps_ref.shape[0]):
        summed = summed + rows_down(x, j) * same_ref[:, j : j + 1] * taps_ref[j : j + 1, :]
    return summed


def conv_taps_back(x, d_out, taps_ref, same_ref, d_taps_ref, cols):
    d_x = d_out * taps_ref[0:1, cols]
    d_taps_ref[0:1, cols] = jnp.sum(d_out * x, axis=0, keepdims=True)
    for j in range(1, taps_ref.shape[0]):
        kept = d_out * same_ref[:, j : j + 1]
        d_taps_ref[j : j + 1, cols] = jnp.sum(kept * rows_down(x, j), axis=0, keepdims=True)
        d_x = d_x + rows_up(kept * taps_ref[j : j + 1, cols], j)
    return d_x


def exact(a, b, dims):
    return lax.dot_general(
        a, b, (dims, ((), ())), precision=TOP_PRECISION, preferred_element_type=F32
    )


def fast(a, b, dims):
    return lax.dot_general(
        a.astype(BF16), b.astype(BF16), (dims, ((), ())), preferred_element_type=F32
    )


PLAIN = ((1,), (0,))
BY_COLS = ((1,), (1,))
BY_ROWS = ((0,), (0,))


def triangle(rows):
    t = lax.broadcasted_iota(jnp.int32, (rows, rows), 0)
    s = lax.broadcasted_iota(jnp.int32, (rows, rows), 1)
    return t, s


def step_terms(step_ref, bias_ref, decay_ref, rows):
    t, s = triangle(rows)
    raw = step_ref[...] + bias_ref[...]
    step = jnp.maximum(raw, 0.0) + jnp.log1p(jnp.exp(-jnp.abs(raw)))
    log_decay = -step * jnp.exp(decay_ref[...])
    running = exact((s <= t).astype(F32), log_decay, PLAIN)
    running_t = exact(log_decay, (t <= s).astype(F32), BY_ROWS)
    step_t = exact(step, (t == s).astype(F32), BY_ROWS)
    return raw, step, log_decay, running, running_t, step_t


def decayed(running, running_t, h, allowed):
    gap = running[:, h : h + 1] - running_t[h : h + 1, :]
    return jnp.exp(jnp.where(allowed, gap, MASKED))


def mix_kernel(
    gate_ref, state_ref, step_ref, taps_x_ref, taps_bc_ref, bias_ref, decay_ref, skip_ref,
    same_ref, allowed_ref, d_scaled_ref, gated_ref, sums_ref,
):
    rows = state_ref.shape[0]
    size = state_ref.shape[1] // 2
    heads = step_ref.shape[1]
    lanes = 128
    per = lanes * heads // gate_ref.shape[2]
    allowed = allowed_ref[...] > 0.0
    _, _, _, running, running_t, step_t = step_terms(step_ref, bias_ref, decay_ref, rows)
    conv_bc = conv_taps(state_ref[...], taps_bc_ref, same_ref)
    state = conv_bc * jax.nn.sigmoid(conv_bc)
    affinity = exact(state[:, size:], state[:, :size], BY_COLS)
    lane = lax.broadcasted_iota(jnp.int32, (rows, lanes), 1) * per // lanes
    squares = jnp.zeros((rows, lanes), F32)
    weighted = jnp.zeros((rows, lanes), F32)
    for group in range(gate_ref.shape[2] // lanes):
        cols = slice(group * lanes, (group + 1) * lanes)
        x = gate_ref[1, :, cols]
        conv = x * taps_x_ref[0:1, cols]
        for j in range(1, taps_x_ref.shape[0]):
            conv = conv + rows_down(x, j) * same_ref[:, j : j + 1] * taps_x_ref[j : j + 1, cols]
        act = conv * jax.nn.sigmoid(conv)
        mixed = act * skip_ref[0:1, cols]
        for i in range(per):
            h = group * per + i
            mixing = decayed(running, running_t, h, allowed) * affinity * step_t[h : h + 1, :]
            mixed = mixed + jnp.where(lane == i, fast(mixing, act, PLAIN), 0.0)
        z = gate_ref[0, :, cols]
        gated = mixed * (z * jax.nn.sigmoid(z))
        gated_ref[:, cols] = gated
        squares = squares + gated * gated
        weighted = weighted + gated * d_scaled_ref[:, cols]
    sums_ref[:, 0:1] = jnp.sum(squares, axis=1, keepdims=True)
    sums_ref[:, 1:2] = jnp.sum(weighted, axis=1, keepdims=True)


def mix_back_kernel(
    gate_ref, state_ref, step_ref, taps_x_ref, taps_bc_ref, bias_ref, decay_ref, skip_ref,
    same_ref, allowed_ref, d_scaled_ref, gated_ref, scales_ref,
    d_gate_ref, d_state_ref, d_step_ref, d_taps_x_ref, d_taps_bc_ref, d_bias_ref, d_decay_ref,
    d_skip_ref,
):
    rows = state_ref.shape[0]
    size = state_ref.shape[1] // 2
    heads = step_ref.shape[1]
    lanes = 128
    per = lanes * heads // gate_ref.shape[2]
    allowed = allowed_ref[...] > 0.0
    raw, step, log_decay, running, running_t, step_t = step_terms(
        step_ref, bias_ref, decay_ref, rows
    )
    conv_bc = conv_taps(state_ref[...], taps_bc_ref, same_ref)
    sig_bc = jax.nn.sigmoid(conv_bc)
    state = conv_bc * sig_bc
    affinity = exact(state[:, size:], state[:, :size], BY_COLS)
    lane = lax.broadcasted_iota(jnp.int32, (rows, lanes), 1) * per // lanes
    head_lane = lax.broadcasted_iota(jnp.int32, (rows, heads), 1)
    head_row = lax.broadcasted_iota(jnp.int32, (heads, rows), 0)
    d_affinity = jnp.zeros((rows, rows), F32)
    d_run = jnp.zeros((rows, heads), F32)
    d_step_t = jnp.zeros((heads, rows), F32)
    for group in range(gate_ref.shape[2] // lanes):
        cols = slice(group * lanes, (group + 1) * lanes)
        x = gate_ref[1, :, cols]
        conv = x * taps_x_ref[0:1, cols]
        for j in range(1, taps_x_ref.shape[0]):
            conv = conv + rows_down(x, j) * same_ref[:, j : j + 1] * taps_x_ref[j : j + 1, cols]
        sig = jax.nn.sigmoid(conv)
        act = conv * sig
        z = gate_ref[0, :, cols]
        sig_z = jax.nn.sigmoid(z)
        d_gated = d_scaled_ref[:, cols] * scales_ref[:, 0:1] - gated_ref[:, cols] * scales_ref[:, 1:2]
        d_mixed = d_gated * (z * sig_z)
        mixed = act * skip_ref[0:1, cols]
        d_act = d_mixed * skip_ref[0:1, cols]
        d_skip_ref[0:1, cols] = jnp.sum(d_mixed * act, axis=0, keepdims=True)
        for i in range(per):
            h = group * per + i
            decay = decayed(running, running_t, h, allowed)
            weight = affinity * step_t[h : h + 1, :]
            mixing = decay * weight
            mixed = mixed + jnp.where(lane == i, fast(mixing, act, PLAIN), 0.0)
            d_act = d_act + jnp.where(lane == i, fast(mixing, d_mixed, BY_ROWS), 0.0)
            d_mixing = fast(jnp.where(lane == i, d_mixed, 0.0), act, BY_COLS) * decay
            d_affinity = d_affinity + d_mixing * step_t[h : h + 1, :]
            by_aff = d_mixing * affinity
            d_step_t = d_step_t + jnp.where(
                head_row == h, jnp.sum(by_aff, axis=0, keepdims=True), 0.0
            )
            by_gap = jnp.sum(by_aff * step_t[h : h + 1, :], axis=1, keepdims=True)
            d_run = d_run + jnp.where(head_lane == h, by_gap, 0.0)
        d_gate_ref[0, :, cols] = (d_gated * mixed * (sig_z * (1.0 + z * (1.0 - sig_z)))).astype(BF16)
        d_conv = d_act * (sig * (1.0 + conv * (1.0 - sig)))
        d_x = conv_taps_back(x, d_conv, taps_x_ref, same_ref, d_taps_x_ref, cols)
        d_gate_ref[1, :, cols] = d_x.astype(BF16)
    t, s = triangle(rows)
    eye = (t == s).astype(F32)
    d_run = d_run - exact(eye, d_step_t * step_t, BY_COLS)
    d_log = exact((s >= t).astype(F32), d_run, PLAIN)
    d_step = exact(eye, d_step_t, BY_COLS) - jnp.exp(decay_ref[...]) * d_log
    d_raw = d_step * jax.nn.sigmoid(raw)
    d_step_ref[...] = d_raw
    d_bias_ref[...] = jnp.sum(d_raw, axis=0, keepdims=True)
    d_decay_ref[...] = jnp.sum(d_log * log_decay, axis=0, keepdims=True)
    d_b = exact(d_affinity, state[:, size:], BY_ROWS)
    d_c = exact(d_affinity, state[:, :size], PLAIN)
    d_silu = sig_bc * (1.0 + conv_bc * (1.0 - sig_bc))
    for part, d_part in enumerate((d_b, d_c)):
        cols = slice(part * size, (part + 1) * size)
        d_conv = d_part * d_silu[:, cols]
        d_x = conv_taps_back(
            state_ref[:, cols], d_conv, taps_bc_ref, same_ref, d_taps_bc_ref, cols
        )
        d_state_ref[:, cols] = d_x.astype(BF16)


def turned(x, cos_ref, sin_ref, sign):
    return x * cos_ref[...] + pltpu.roll(x, HEAD // 2, 1) * (sign * sin_ref[...])


def probabilities(query, key, allowed):
    scores = fast(query, key, BY_COLS) * HEAD ** (-0.5)
    scores = jnp.where(allowed, scores, MASKED)
    raised = jnp.exp(scores - jnp.max(scores, axis=1, keepdims=True))
    return raised / jnp.sum(raised, axis=1, keepdims=True)


def attend_kernel(qkv_ref, cos_ref, sin_ref, allowed_ref, low_ref, attended_ref):
    allowed = allowed_ref[...] > 0.0
    width = attended_ref.shape[1]
    for h in range(width // HEAD):
        q, k, v = (slice(i * width + h * HEAD, i * width + (h + 1) * HEAD) for i in range(3))
        query = turned(qkv_ref[:, q], cos_ref, sin_ref, 1.0).astype(BF16)
        key = turned(qkv_ref[:, k], cos_ref, sin_ref, 1.0).astype(BF16)
        value = qkv_ref[:, v].astype(BF16)
        low_ref[:, q] = query
        low_ref[:, k] = key
        low_ref[:, v] = value
        probs = probabilities(query, key, allowed)
        attended_ref[:, q] = fast(probs, value, PLAIN).astype(BF16)


def attend_back_kernel(low_ref, d_ref, cos_ref, sin_ref, allowed_ref, d_qkv_ref):
    allowed = allowed_ref[...] > 0.0
    width = d_ref.shape[1]
    for h in range(width // HEAD):
        q, k, v = (slice(i * width + h * HEAD, i * width + (h + 1) * HEAD) for i in range(3))
        query, key, value = low_ref[:, q], low_ref[:, k], low_ref[:, v]
        d_out = d_ref[:, q].astype(BF16)
        probs = probabilities(query, key, allowed)
        d_qkv_ref[:, v] = fast(probs, d_out, BY_ROWS).astype(BF16)
        d_probs = fast(d_out, value, BY_COLS)
        inner = jnp.sum(probs * d_probs, axis=1, keepdims=True)
        d_scores = (probs * (d_probs - inner) * HEAD ** (-0.5)).astype(BF16)
        d_query = fast(d_scores, key, PLAIN)
        d_key = fast(d_scores, query, BY_ROWS)
        d_qkv_ref[:, q] = turned(d_query, cos_ref, sin_ref, -1.0).astype(BF16)
        d_qkv_ref[:, k] = turned(d_key, cos_ref, sin_ref, -1.0).astype(BF16)


def in_vmem(kernel, outs, args, flops):
    size = sum(x.size * x.dtype.itemsize for x in tuple(args) + tuple(outs))
    return pl.pallas_call(
        kernel,
        out_shape=outs,
        in_specs=[pl.BlockSpec(memory_space=pltpu.VMEM)] * len(args),
        out_specs=[pl.BlockSpec(memory_space=pltpu.VMEM)] * len(outs),
        compiler_params=pltpu.CompilerParams(vmem_limit_bytes=40 * 2**20),
        cost_estimate=pl.CostEstimate(flops=flops, bytes_accessed=size, transcendentals=0),
    )(*args)


def gated_gelu(gate_up):
    half = gate_up.shape[1] // 2
    return jax.nn.gelu(gate_up[:, :half], approximate=True) * gate_up[:, half:]


def total(values):
    summed = values[0]
    for value in values[1:]:
        summed = summed + value
    return summed


def after(x, done):
    mark = done[(-1,) * done.ndim].astype(F32)
    return x + jnp.minimum(jnp.abs(mark), 0.0).astype(x.dtype)


class Links:
    def __init__(self, n_dp, n_t):
        self.n_dp = n_dp
        self.n_t = n_t
        self.chips = n_dp // 2
        self.chip_bits = self.chips.bit_length() - 1
        self.z_bits = n_t.bit_length() - 1
        d = lax.axis_index("dp")
        self.d = d
        self.core = d % 2
        self.chip = d // 2
        self.t = lax.axis_index("tensor")

    def core_swap(self, x):
        return lax.ppermute(x, "dp", [(i, i ^ 1) for i in range(self.n_dp)])

    def chip_swap(self, x, rel):
        return lax.ppermute(x, "dp", [(i, i ^ (rel << 1)) for i in range(self.n_dp)])

    def z_swap(self, x, rel):
        return lax.ppermute(x, "tensor", [(i, i ^ rel) for i in range(self.n_t)])

    def row_parts(self, rows):
        count = max(1, min(self.chip_bits, rows // 16))
        units = rows // 16
        edges = [0] + [16 * ((units * (i + 1)) // count) for i in range(count)]
        edges[-1] = rows
        return [(edges[i], edges[i + 1]) for i in range(count)]

    def chip_rs(self, terms, axis, direct=False):
        if direct:
            blocks = [
                lax.index_in_dim(terms, rel, axis, keepdims=False) for rel in range(self.chips)
            ]
            return total([block.astype(F32) for block in self.chip_a2a(blocks)])
        outs = []
        bits = self.chip_bits
        for number, (low, high) in enumerate(self.row_parts(terms.shape[axis + 1])):
            cur = lax.slice_in_dim(terms, low, high, axis=axis + 1)
            cur = cur.reshape(cur.shape[:axis] + (2,) * bits + cur.shape[axis + 1 :])
            left = list(range(bits))[::-1]
            for step in range(bits):
                bit = (number + step) % bits
                at = axis + left.index(bit)
                left.remove(bit)
                keep = lax.index_in_dim(cur, 0, at, keepdims=False)
                send = lax.index_in_dim(cur, 1, at, keepdims=False)
                got = self.chip_swap(send.astype(BF16), 1 << bit)
                cur = keep.astype(F32) + got.astype(F32)
            outs.append(cur)
        return outs[0] if len(outs) == 1 else jnp.concatenate(outs, axis=axis)

    def chip_ag(self, x, axis, direct=False):
        if direct:
            return jnp.stack(self.chip_a2a([x] * self.chips), axis=axis)
        bits = self.chip_bits
        outs = []
        for number, (low, high) in enumerate(self.row_parts(x.shape[axis])):
            blocks = {0: lax.slice_in_dim(x, low, high, axis=axis)}
            for step in range(bits):
                bit = (number + step) % bits
                for rel in list(blocks):
                    blocks[rel | (1 << bit)] = self.chip_swap(blocks[rel], 1 << bit)
            outs.append([blocks[rel] for rel in range(self.chips)])
        merged = []
        for rel in range(self.chips):
            pieces = [part[rel] for part in outs]
            merged.append(pieces[0] if len(pieces) == 1 else jnp.concatenate(pieces, axis=axis))
        return jnp.stack(merged, axis=axis)

    def chip_a2a(self, blocks):
        return [blocks[0]] + [self.chip_swap(blocks[rel], rel) for rel in range(1, self.chips)]

    def chip_sum(self, x):
        total = x
        for rel in range(1, self.chips):
            moved = jnp.stack([x[i ^ rel] for i in range(self.chips)], 0)
            total = total + self.chip_swap(moved, rel)
        return total

    def z_sum(self, x):
        return total([x] + [self.z_swap(x, rel) for rel in range(1, self.n_t)])

    def dp_sum(self, x):
        x = x + self.core_swap(x)
        return total(self.chip_a2a([x] * self.chips))

    def z_rs(self, terms, axis):
        bits = self.z_bits
        cur = terms.reshape(terms.shape[:axis] + (2,) * bits + terms.shape[axis + 1 :])
        left = list(range(bits))[::-1]
        for bit in range(bits):
            at = axis + left.index(bit)
            left.remove(bit)
            keep = lax.index_in_dim(cur, 0, at, keepdims=False)
            send = lax.index_in_dim(cur, 1, at, keepdims=False)
            got = self.z_swap(send.astype(BF16), 1 << bit)
            cur = keep.astype(F32) + got.astype(F32)
        return cur

    def z_ag(self, x, axis):
        blocks = {0: x}
        for bit in range(self.z_bits)[::-1]:
            for rel in list(blocks):
                blocks[rel | (1 << bit)] = self.z_swap(blocks[rel], 1 << bit)
        return jnp.stack([blocks[rel] for rel in range(self.n_t)], axis=axis)

    def by_index(self, x, axis, own):
        count = x.shape[axis]
        return jnp.concatenate(
            [lax.dynamic_slice_in_dim(x, own ^ i, 1, axis=axis) for i in range(count)], axis=axis
        )

    def rows_by_t(self, x):
        rows = x.shape[0]
        split = x.reshape((self.n_t, rows // self.n_t) + x.shape[1:])
        return self.by_index(split, 0, self.t).reshape(x.shape)


def core_pair(links, x, axis):
    return jnp.concatenate([x, links.core_swap(x)], axis=axis)


def core_rs(links, x, axis):
    half = x.shape[axis] // 2
    own = lax.slice_in_dim(x, 0, half, axis=axis)
    other = lax.slice_in_dim(x, half, 2 * half, axis=axis)
    return own + links.core_swap(other.astype(BF16)).astype(F32)


def dotf(spec, a, b):
    return jnp.einsum(spec, a, b, preferred_element_type=F32)


def dotl(spec, a, b):
    return jnp.einsum(spec, a, b, preferred_element_type=F32).astype(BF16)


def proj_spread(links, w):
    rows = links.z_ag(w, 0)
    if links.chips == links.n_t:
        blocks = [
            lax.dynamic_index_in_dim(rows, links.chip ^ links.t ^ rel, 0, keepdims=False)
            for rel in range(links.chips)
        ]
    else:
        rows = links.by_index(rows, 0, links.t).reshape(links.chips, -1, w.shape[1])
        blocks = [
            lax.dynamic_index_in_dim(rows, links.chip ^ rel, 0, keepdims=False)
            for rel in range(links.chips)
        ]
    came = jnp.stack(links.chip_a2a(blocks), 0)
    return jnp.stack([came, links.core_swap(came)], 1)


def proj_collect(links, own, other):
    mine = (own + links.core_swap(other).astype(F32)).astype(BF16)
    blocks = [mine[:, rel] for rel in range(links.chips)]
    rows = jnp.stack(links.chip_a2a(blocks), 0)
    if links.chips == links.n_t:
        rows = links.by_index(rows, 0, links.chip ^ links.t)
    else:
        rows = links.by_index(rows, 0, links.chip).reshape(links.n_t, -1, own.shape[2])
        rows = links.by_index(rows, 0, links.t)
    return links.z_rs(rows, 0)


def core_halves(links, x):
    split = x.reshape(x.shape[:-1] + (2, x.shape[-1] // 2))
    return links.by_index(split, x.ndim - 1, links.core).reshape(x.shape)


def enter(links, w, m):
    rows = m.hid.shape[0]
    joined = links.rows_by_t(jnp.concatenate([m.hid, m.emb], axis=1))
    wide = joined.astype(F32)
    m.inverse = lax.rsqrt(jnp.mean(wide * wide, axis=1) + EPSILON)
    half = joined.shape[1] // links.n_dp
    blocks = []
    for rel in range(links.chips):
        at = 2 * (links.chip ^ rel)
        pieces = [
            lax.dynamic_slice_in_dim(joined, (at + (links.core ^ j)) * half, half, axis=1)
            for j in range(2)
        ]
        blocks.append(jnp.concatenate(pieces, axis=1))
    m.joined = jnp.stack(links.chip_a2a(blocks), 0)
    places = jnp.arange(rows, dtype=jnp.int32)
    m.true = layout(m.lens, places)
    _, position, _, allowed = layout(m.lens, links.rows_by_t(places))
    m.allowed_rel = allowed.astype(F32)
    m.cos, m.sin = rope_tables(position)


def attend(links, w, m):
    wide = m.joined.astype(F32) * m.inv_attn[:, :, None]
    m.attn_in = lax.optimization_barrier((wide * w.g_attn).astype(BF16))
    qkv = links.chip_rs(dotl("crd,dn->crn", m.attn_in, w.qkv), 0)
    rows, width = qkv.shape[0], qkv.shape[1] // 3
    outs = (
        jax.ShapeDtypeStruct((rows, 3 * width), BF16),
        jax.ShapeDtypeStruct((rows, width), BF16),
    )
    args = (qkv, m.cos, m.sin, m.allowed_rel)
    m.qkv_low, attended = in_vmem(attend_kernel, outs, args, 4 * rows * rows * width)
    m.attended = links.chip_ag(attended, 0, direct=True)


def z_split(links, x, axis):
    rows = x.shape[axis]
    return x.reshape(x.shape[:axis] + (links.n_t, rows // links.n_t) + x.shape[axis + 1 :])


def z_join(x, axis):
    return x.reshape(x.shape[:axis] + (-1,) + x.shape[axis + 2 :])


def attend_out(links, w, m):
    part = dotl("crn,nd->crd", m.attended, w.out)
    summed = links.z_rs(z_split(links, part, 1), 1)
    rows = summed.shape[1]
    m.joined_z = m.joined[:, :rows].astype(F32)
    m.inv_attn_z = m.inv_attn[:, :rows]
    mid = m.joined_z + summed
    m.mid = mid
    squares = links.chip_sum(jnp.sum(mid * mid, axis=2))
    width = mid.shape[2] * links.chips
    m.inv_mlp = lax.rsqrt(squares / width + EPSILON)
    low = (mid * m.inv_mlp[:, :, None] * w.g_mlp).astype(BF16)
    m.mlp_in = z_join(links.z_ag(low, 1), 1)


def feed(links, w, m):
    summed = links.chip_rs(dotl("crd,dn->crn", m.mlp_in, w.gate_up), 0)
    units = 2 * w.down.shape[0]
    m.adapter = summed[:, units:].astype(BF16)
    gate_up = summed[:, :units] + dotf("ra,an->rn", m.adapter, w.adapter_up)
    activated, m.gate_back = jax.vjp(gated_gelu, gate_up)
    m.hidden = links.chip_ag(activated.astype(BF16), 0, direct=True)


def feed_out(links, w, m):
    part = dotl("crn,nd->crd", m.hidden, w.down)
    summed = links.z_rs(z_split(links, part, 1), 1)
    m.block = (m.mid + summed).astype(BF16)
    m.block = core_halves(links, m.block)
    part = dotl("crd,xydn->xycrn", m.block, w.proj)
    part = links.by_index(links.by_index(part, 1, links.core), 0, links.chip)
    part = z_join(part, 0).transpose(1, 2, 0, 3)
    part = part.reshape(part.shape[:2] + (-1,))
    shared = links.chip_rs(part, 0, direct=True).astype(BF16)
    whole = links.by_index(links.z_ag(shared, 0), 0, links.t)
    shared_full = whole.reshape(-1, whole.shape[2])
    m.mamba_in = m.hid.astype(F32) + shared_full.astype(F32)
    own = z_split(links, m.hid, 0)
    own = lax.dynamic_index_in_dim(own, links.t, 0, keepdims=False)
    m.mamba_in_z = own.astype(F32) + shared.astype(F32)


def mix(links, w, m):
    taps_x, taps_bc, step_bias, decay_log, skip, gate_gain = w.smalls
    segment, _, valid, allowed = m.true
    mamba_in = m.mamba_in
    inverse = lax.rsqrt(jnp.mean(mamba_in * mamba_in, axis=1, keepdims=True) + EPSILON)
    ssm_in = (mamba_in * inverse * w.g_mamba).astype(BF16)
    gate_x = dotf("td,kdc->ktc", ssm_in, w.w_in)
    state_io = dotf("td,dn->tn", ssm_in, w.bc)
    step_raw = dotf("td,dn->tn", ssm_in, w.dt)
    grad_low = m.cot * valid[:, None].astype(BF16)
    d_norm = dotf("tn,in->ti", grad_low, w.mout)
    d_scaled = d_norm * gate_gain
    rows, width = gate_x.shape[1:]
    heads = step_raw.shape[1]
    earlier = [jnp.pad(segment, (j, 0), constant_values=-1)[:rows] for j in range(taps_x.shape[0])]
    same = jnp.stack([(e == segment).astype(F32) for e in earlier], 1)
    skips = jnp.repeat(skip, width // heads)[None, :]
    args = (gate_x, state_io, step_raw, taps_x, taps_bc, step_bias[None, :], decay_log[None, :])
    args += (skips, same, allowed.astype(F32), d_scaled)
    outs = (jax.ShapeDtypeStruct((rows, width), F32), jax.ShapeDtypeStruct((rows, 2), F32))
    gated, sums = in_vmem(mix_kernel, outs, args, 4 * rows * rows * width)
    inner = width * links.n_t
    sums = links.z_sum(sums)
    squares, weighted = sums[:, 0], sums[:, 1]
    row_scale = lax.rsqrt(squares / inner + EPSILON)
    m.gated_norm = (gated * row_scale[:, None] * gate_gain).astype(BF16)
    m.mamba_out = dotl("ti,in->tn", m.gated_norm, w.mout)

    grad_gain = jnp.sum(d_norm * gated * row_scale[:, None], axis=0)
    scales = jnp.stack([row_scale, row_scale**3 * weighted / inner], 1)
    outs = (
        jax.ShapeDtypeStruct(gate_x.shape, BF16),
        jax.ShapeDtypeStruct(state_io.shape, BF16),
        jax.ShapeDtypeStruct(step_raw.shape, F32),
        jax.ShapeDtypeStruct(taps_x.shape, F32),
        jax.ShapeDtypeStruct(taps_bc.shape, F32),
        jax.ShapeDtypeStruct((1, heads), F32),
        jax.ShapeDtypeStruct((1, heads), F32),
        jax.ShapeDtypeStruct((1, width), F32),
    )
    args += (gated, scales)
    grads = in_vmem(mix_back_kernel, outs, args, 16 * rows * rows * width)
    m.gate_x_low, d_state_io, d_step, d_taps_x, d_taps_bc, d_bias, d_decay, d_skip = grads
    d_skip = jnp.sum(d_skip.reshape(heads, width // heads), axis=1)
    m.step_low = d_step.astype(BF16)
    part_in = dotf("ktc,kdc->td", m.gate_x_low, w.w_in) + dotf("tn,dn->td", m.step_low, w.dt)
    terms = jnp.concatenate([part_in.astype(BF16), d_state_io], axis=1)
    m.terms = z_split(links, links.rows_by_t(terms), 0)
    m.ssm_in = ssm_in
    m.ssm_in_z = own_rows(links, ssm_in)
    m.grad_low = grad_low
    m.sums_dp = (d_taps_x, grad_gain, d_bias[0], d_decay[0], d_skip)
    m.d_taps_bc = d_taps_bc


def settle(links, w, m):
    summed = links.z_rs(m.terms, 0)
    model_width = m.mamba_in_z.shape[1]
    m.state_low = summed[:, model_width:].astype(BF16)
    dy = summed[:, :model_width] + dotf("tn,dn->td", m.state_low, w.bc)
    v = m.mamba_in_z
    inv = lax.rsqrt(jnp.mean(v * v, axis=1, keepdims=True) + EPSILON)
    scaled = dy * w.g_mamba
    dv = inv * scaled - v * (inv**3 * jnp.mean(scaled * v, axis=1, keepdims=True))
    grad_g_mamba = jnp.sum(dy * v * inv, axis=0)
    m.sums_all = (m.d_taps_bc, grad_g_mamba)
    m.d_mamba = dv + own_rows(links, m.grad_low).astype(F32)
    m.shared_low = links.chip_ag(m.d_mamba.astype(BF16), 0, direct=True)
    split = m.shared_low.reshape(m.shared_low.shape[:2] + w.proj.shape[:2] + (-1,))
    m.shared_cols = links.by_index(links.by_index(split, 3, links.core), 2, links.chip)
    d_block = core_halves(links, dotf("crxyn,xydn->crd", m.shared_cols, w.proj))
    m.d_block = d_block
    m.mlp_low = z_join(links.z_ag(d_block.astype(BF16), 1), 1)


def own_rows(links, x):
    return lax.dynamic_index_in_dim(z_split(links, x, 0), links.t, 0, keepdims=False)


def finish_output(links, micro):
    terms = jnp.stack([z_split(links, links.rows_by_t(m.mamba_out), 0) for m in micro], 0)
    summed = links.z_rs(terms, 1)
    base = jnp.stack([m.mamba_in_z for m in micro], 0)
    valid = jnp.stack([own_rows(links, m.true[2]) for m in micro], 0)
    low = ((base + summed) * valid[:, :, None].astype(F32)).astype(BF16)
    whole = links.by_index(links.z_ag(low, 1), 1, links.t)
    return z_join(whole, 1)


def feed_back(links, w, m):
    part = dotl("crd,nd->crn", m.mlp_low, w.down)
    d_hidden = links.chip_rs(part, 0)
    (d_gate_up,) = m.gate_back(d_hidden)
    m.gate_up_own = d_gate_up.astype(BF16)
    part = dotl("rn,an->ra", m.gate_up_own, w.adapter_up)
    m.gate_up_low = links.chip_ag(jnp.concatenate([m.gate_up_own, part], 1), 0)


def feed_back_out(links, w, m):
    part = dotl("crn,dn->crd", m.gate_up_low, w.gate_up)
    dy = links.z_rs(z_split(links, part, 1), 1)
    scaled = dy * w.g_mlp
    v, inv = m.mid, m.inv_mlp
    weighted = links.chip_sum(jnp.sum(scaled * v, axis=2))
    width = v.shape[2] * links.chips
    dv = scaled * inv[:, :, None] - v * (inv**3 * weighted / width)[:, :, None]
    m.grad_g_mlp = jnp.sum(dy * v * inv[:, :, None], axis=(0, 1))
    m.d_mid = dv + m.d_block
    m.attn_low = z_join(links.z_ag(m.d_mid.astype(BF16), 1), 1)


def attend_back(links, w, m):
    part = dotl("crd,nd->crn", m.attn_low, w.out)
    d_attended = links.chip_rs(part, 0, direct=True)
    rows, width = d_attended.shape
    outs = (jax.ShapeDtypeStruct((rows, 3 * width), BF16),)
    args = (m.qkv_low, d_attended, m.cos, m.sin, m.allowed_rel)
    (d_qkv,) = in_vmem(attend_back_kernel, outs, args, 10 * rows * rows * width)
    m.d_qkv = links.chip_ag(d_qkv, 0)


def leave(links, w, m):
    part = dotl("crn,dn->crd", m.d_qkv, w.qkv)
    dy = links.z_rs(z_split(links, part, 1), 1)
    scaled = dy * w.g_attn
    v, inv = m.joined_z, m.inv_attn_z
    weighted = links.chip_sum(jnp.sum(scaled * v, axis=2))
    width = v.shape[2] * links.chips
    dv = scaled * inv[:, :, None] - v * (inv**3 * weighted / width)[:, :, None]
    m.grad_g_attn = jnp.sum(dy * v * inv[:, :, None], axis=(0, 1))
    d_joined = (dv + m.d_mid).astype(BF16)
    came = jnp.stack(links.chip_a2a([d_joined[rel] for rel in range(links.chips)]), 0)
    rows = came.shape[1]
    came = came.reshape(links.chips, rows, 2, -1)
    came = links.by_index(links.by_index(came, 2, links.core), 0, links.chip)
    came = came.transpose(1, 0, 2, 3).reshape(rows, -1)
    model_width = m.d_mamba.shape[1]
    d_hid = (came[:, :model_width].astype(F32) + m.d_mamba).astype(BF16)
    both = jnp.concatenate([d_hid, came[:, model_width:]], axis=1)
    whole = links.by_index(links.z_ag(both, 0), 0, links.t)
    whole = whole.reshape(-1, both.shape[1])
    m.d_hid, m.d_emb = whole[:, :model_width], whole[:, model_width:]


def local(
    hidden,
    embedding,
    lengths,
    query_key_value_weight,
    attention_output_weight,
    attention_gain,
    feedforward_gain,
    gate_up_weight,
    adapter_down,
    adapter_up,
    down_weight,
    shared_projection_weight,
    mixer_gain,
    mixer_input_weight,
    state_map_weight,
    step_weight,
    mixer_output_weight,
    mixer_input_taps,
    state_map_taps,
    step_bias,
    decay_logarithm,
    head_skip_weight,
    gated_norm_gain,
    cotangent,
    n_dp,
    n_t,
):
    links = Links(n_dp, n_t)
    smalls = (
        mixer_input_taps,
        state_map_taps,
        step_bias,
        decay_logarithm,
        head_skip_weight,
        gated_norm_gain,
    )
    micro = [
        SimpleNamespace(
            hid=hidden[b], emb=embedding[b], lens=lengths[b, 0], cot=cotangent[b]
        )
        for b in range(hidden.shape[0])
    ]
    w = SimpleNamespace()
    gains = core_pair(links, jnp.stack([attention_gain, feedforward_gain], 0), 1).astype(F32)
    w.g_attn, w.g_mlp = gains[0], gains[1]
    flat = jnp.concatenate([query_key_value_weight[:, i] for i in range(3)], axis=1)
    w.qkv = lax.optimization_barrier(core_pair(links, flat, 0))
    def stage(work, m):
        with jax.named_scope(f"{work.__name__}_micro{micro.index(m)}"):
            work(links, w, m)

    for m in micro:
        stage(enter, m)
    inverses = jnp.stack([m.inverse for m in micro], 0)
    inverses = jnp.stack(links.chip_a2a([inverses] * links.chips), 1)
    for b, m in enumerate(micro):
        m.inv_attn = inverses[b]
    first = micro[0]
    units = gate_up_weight.shape[2]
    up_own = adapter_up.reshape(adapter_up.shape[0], 2 * units)
    cols = jnp.concatenate([gate_up_weight[:, 0], gate_up_weight[:, 1], adapter_down], axis=1)
    w.out = lax.optimization_barrier(core_pair(links, attention_output_weight, 1))
    w.gate_up = lax.optimization_barrier(core_pair(links, cols, 0))
    w.down = lax.optimization_barrier(core_pair(links, down_weight, 1))
    state_cols, step_cols = state_map_weight.shape[1], step_weight.shape[1]
    packed = jnp.concatenate([state_map_weight, step_weight, mixer_gain[:, None]], axis=1)

    w.smalls = smalls
    stages = [attend, attend_out, feed, feed_out, mix, settle]
    stages += [feed_back, feed_back_out, attend_back, leave]
    entries = ["joined", "attended", "mlp_in", "hidden", "mamba_in", "terms"]
    entries += ["mlp_low", "gate_up_low", "attn_low", "d_qkv"]
    for work, entry in zip(stages, entries):
        for m in micro:
            setattr(m, entry, lax.optimization_barrier(getattr(m, entry)))
            stage(work, m)
        if work is attend:
            w.adapter_up = lax.all_gather(after(up_own, first.joined), "dp", axis=0, tiled=True)
            w.proj = proj_spread(links, shared_projection_weight)
            packed = lax.all_gather(after(packed, first.attended), "dp", axis=0, tiled=True)
            w.bc = packed[:, :state_cols]
            w.dt = packed[:, state_cols : state_cols + step_cols]
            w.g_mamba = packed[:, state_cols + step_cols].astype(F32)
            shard = after(mixer_input_weight.transpose(1, 0, 2), first.attended)
            w.w_in = lax.all_gather(shard, "dp", axis=1, tiled=True)
            shard = after(mixer_output_weight, first.attended)
            w.mout = lax.all_gather(shard, "dp", axis=1, tiled=True)
    with jax.named_scope("outputs"):
        results = finish_output(links, micro)

    def both(get, axis=0):
        return jnp.concatenate([get(m) for m in micro], axis=axis)

    ssm_in = both(lambda m: m.ssm_in)
    grad_in = dotl("td,ktc->kdc", ssm_in, both(lambda m: m.gate_x_low, 1))
    grad_in = lax.psum_scatter(grad_in, "dp", scatter_dimension=1, tiled=True)
    grad_mout = dotl("tn,ti->ni", both(lambda m: m.grad_low), both(lambda m: m.gated_norm))
    grad_mout = lax.psum_scatter(grad_mout, "dp", scatter_dimension=0, tiled=True)
    grad_bc = dotl("td,tn->dn", both(lambda m: m.ssm_in_z), both(lambda m: m.state_low))
    grad_dt = dotl("td,tn->dn", ssm_in, both(lambda m: m.step_low))
    grad_small = jnp.concatenate([grad_bc, grad_dt], axis=1)
    grad_small = lax.psum_scatter(grad_small, "dp", scatter_dimension=0, tiled=True)
    grad_up = dotl("ra,rn->an", both(lambda m: m.adapter), both(lambda m: m.gate_up_own))
    grad_up = lax.psum_scatter(grad_up, "dp", scatter_dimension=0, tiled=True)

    sums_dp = jax.tree.map(lambda *v: total(v), *[m.sums_dp for m in micro])
    sums_all = jax.tree.map(lambda *v: total(v), *[m.sums_all for m in micro])
    flat_all = links.z_sum(jnp.concatenate([v.reshape(-1) for v in sums_all]))
    flat = links.dp_sum(jnp.concatenate([v.reshape(-1) for v in sums_dp] + [flat_all]))
    small_sums = []
    for v in sums_dp + sums_all:
        small_sums.append(flat[: v.size].reshape(v.shape))
        flat = flat[v.size :]
    own_gain = mixer_gain.shape[0]
    grad_g_mamba = lax.dynamic_slice_in_dim(small_sums[6], links.d * own_gain, own_gain)

    g_rows = total([jnp.stack([m.grad_g_attn, m.grad_g_mlp], 0) for m in micro])
    half = g_rows.shape[1] // 2
    g_rows = g_rows[:, :half] + links.core_swap(g_rows[:, half:])
    g_rows = links.z_sum(g_rows)

    def grad(spec, get_a, get_b, axis):
        return core_rs(links, total([dotf(spec, get_a(m), get_b(m)) for m in micro]), axis)

    block = both(lambda m: m.block)
    cols = both(lambda m: m.shared_cols)
    spec = "crd,crxn->dxn"
    grad_proj = proj_collect(
        links, dotf(spec, block, cols[:, :, :, 0]), dotl(spec, block, cols[:, :, :, 1])
    )
    grad_down = grad("crn,crd->nd", lambda m: m.hidden, lambda m: m.mlp_low, 1)
    grad_cols = grad("crd,crn->dn", lambda m: m.mlp_in, lambda m: m.gate_up_low, 0)
    grad_out = grad("crn,crd->nd", lambda m: m.attended, lambda m: m.attn_low, 1)
    grad_qkv = grad("crd,crn->dn", lambda m: m.attn_in, lambda m: m.d_qkv, 0)
    grad_qkv = jnp.stack(jnp.split(grad_qkv, 3, axis=1), 1)
    grad_gate_up = jnp.stack([grad_cols[:, :units], grad_cols[:, units : 2 * units]], 1)
    partial_t = [grad_cols[:, 2 * units :].astype(BF16), grad_small[:, :state_cols]]
    sizes = [v.size for v in partial_t]
    whole_t = links.z_sum(jnp.concatenate([v.reshape(-1, HEAD) for v in partial_t], 0))
    split = sizes[0] // HEAD
    grad_adapter_down = whole_t[:split].reshape(partial_t[0].shape).astype(F32)
    grad_bc = whole_t[split:].reshape(partial_t[1].shape).astype(F32)

    return (
        results,
        jnp.stack([m.d_hid for m in micro]),
        jnp.stack([m.d_emb for m in micro]),
        grad_qkv,
        grad_out,
        g_rows[0],
        g_rows[1],
        grad_gate_up,
        grad_adapter_down,
        grad_up.reshape(adapter_up.shape).astype(F32),
        grad_down,
        grad_proj,
        grad_g_mamba,
        grad_in.transpose(1, 0, 2).astype(F32),
        grad_bc,
        grad_small[:, state_cols:].astype(F32),
        grad_mout.T.astype(F32),
        small_sums[0],
        small_sums[5],
        small_sums[2],
        small_sums[3],
        small_sums[4],
        small_sums[1],
    )


def solution(mesh):
    rows = P(None, "dp", None)
    by_dp = P("dp", None, "tensor")
    by_t = P("tensor", "dp")
    weights = (by_dp, by_t, P("dp"), P("dp"), by_dp, P("dp", None), by_dp, by_t, by_t, P("dp"))
    weights += (by_dp, P("dp", None), P("dp", "tensor"), by_t)
    smalls = (P(None, "tensor"), P(), P("tensor"), P("tensor"), P("tensor"), P("tensor"))
    return jax.shard_map(
        partial(local, n_dp=mesh.shape["dp"], n_t=mesh.shape["tensor"]),
        mesh=mesh,
        in_specs=(rows, rows, rows) + weights + smalls + (rows,),
        out_specs=(rows, rows, rows) + weights + smalls,
        check_vma=False,
    )
```

time: 2580 us -> 1370 us (0.53)
  waiting for transfers between devices: 1630 us -> 604 us
  matrix products: 495 us -> 164 us
  starting transfers between devices: 14.4 us -> 228 us
  blocking collectives: 187 us -> 0 us
  other arithmetic: 111 us -> 178 us
  local copies, waits for them, and re-layouts: 107 us -> 137 us
  Pallas kernels: 0 us -> 27.4 us
    ppermute x0 -> x208, waiting for transfers between devices: none -> 603 us  [the longest x120 372 us: chip_swap(): return lax.ppermute(x, 'dp', [(i, i ^ rel << 1) for i in range(self.n_dp)])]
    reduce_scatter x11 -> x4, waiting for transfers between devices: 580 us -> 0.03 us  [the longest x1 0.02 us: local(): lax.psum_scatter(grad_small, 'dp', scatter_dimension=0, tiled=True)]
    psum x6 -> x0, waiting for transfers between devices: 558 us -> none  [the longest x3 444 us: head_sum(): return lax.psum(partial_rows, 'tensor')]
    all_gather x12 -> x4, waiting for transfers between devices: 487 us -> 0.06 us  [the longest x1 0.02 us: local(): w.mout = lax.all_gather(shard, 'dp', axis=1, tiled=True)]
    dot_general x90 -> x55, matrix products: 495 us -> 164 us  [the longest x28 82.7 us: dotl(): return jnp.einsum(spec, a, b, preferred_element_type=F32).astype(BF16)]
    ppermute x0 -> x208, starting transfers between devices: none -> 227 us  [the longest x120 143 us: chip_swap(): return lax.ppermute(x, 'dp', [(i, i ^ rel << 1) for i in range(self.n_dp)])]
    psum x4 -> x0, blocking collectives: 126 us -> none  [the longest x1 79.6 us: head_sum(): return lax.psum(partial_rows, 'tensor')]
    concatenate x2 -> x53, other arithmetic: 1.27 us -> 69.3 us  [the longest x4 49.8 us: core_pair(): return jnp.concatenate([x, links.core_swap(x)], axis=axis)]
  transfers between devices with their start and end apart: 29 -> 216, of which waited for: 19 -> 108; matrix products, arithmetic and copies ran while one was open for 21% -> 32% of each run, Pallas kernels for 0% -> 2%
where the time goes in v1:
time: 1370 us; the launch traced here: 1360 us
  waiting for transfers between devices  604 us (44%)
  starting transfers between devices  228 us (17%)
  other arithmetic  178 us (13%)
  matrix products  164 us (12%)
  local copies, waits for them, and re-layouts  137 us (10%)
  Pallas kernels  27.4 us (2%)
  between operations  21.8 us (2%)
    ppermute x120, waiting for transfers between devices, chip_swap(): return lax.ppermute(x, 'dp', [(i, i ^ rel << 1) for i in range(self.n_dp)])  372 us
    ppermute x75, waiting for transfers between devices, z_swap(): return lax.ppermute(x, 'tensor', [(i, i ^ rel) for i in range(self.n_t)])  231 us
    ppermute x120, starting transfers between devices, chip_swap(): return lax.ppermute(x, 'dp', [(i, i ^ rel << 1) for i in range(self.n_dp)])  143 us
    dot_general x28, matrix products, dotl(): return jnp.einsum(spec, a, b, preferred_element_type=F32).astype(BF16)  82.7 us
    ppermute x75, starting transfers between devices, z_swap(): return lax.ppermute(x, 'tensor', [(i, i ^ rel) for i in range(self.n_t)])  82.4 us
    dot_general x27, matrix products, dotf(): return jnp.einsum(spec, a, b, preferred_element_type=F32)  81.8 us
    unnamed x535, local copies, waits for them, and re-layouts  55.1 us
    concatenate x4, other arithmetic, core_pair(): return jnp.concatenate([x, links.core_swap(x)], axis=axis)  49.8 us
  transfers between devices with their start and end apart: 216, of which 108 were waited for; matrix products, arithmetic and copies ran while one was open for 32% of the time, Pallas kernels for 2%

profile of v1, /device:TPU:0, one launch (start us, length us, event | category | flops | bytes accessed | tf_op | source)
XLA Modules:
  0.0 1360.6 jit_solution(6118904898307751684)
XLA Ops:
  88.2 8.8 collective-permute-done.2
  101.8 19.7 %pad_maximum_fusion.2 = bf16[1024,3072]{1,0:T(8,128)(2,1)S(1)} fusion(bf16[512,3072]{1,0:T(8,128)(2,1)} %collective-permute-done.14, bf16[512,1024]{1,0:T(8,128)(2,1)S(1)} %copy-done.71, bf16[512,1024]{1,0:T(8,128)(2,1)S(1)} %copy-done.73, bf16[512,1024]{1,0:T(8,128)(2,1)S(1)} %get-tuple-element.237), kind=kLoop, calls=%fused_computation.20 | loop fusion | flops 25165824 | bytes 12582912 | tf_op jit(solution)/shard_map/concatenate | solution.py:414
  131.9 14.0 %collective-permute-done.50 = bf16[2,64,3072]{2,1,0:T(8,128)(2,1)S(1)} collective-permute-done((bf16[2,64,3072]{2,1,0:T(8,128)(2,1)S(1)}, bf16[2,64,3072]{2,1,0:T(8,128)(2,1)S(1)}, u32[]{:S(2)}, u32[]{:S(2)}) %collective-permute-start.50) | collective-permute-done | bytes 786464 | tf_op jit(solution)/shard_map/attend_micro1/ppermute | solution.py:311
  147.9 11.5 collective-permute-done.17
  163.6 13.5 collective-permute-done.15
  265.8 8.6 collective-permute-done.55
  275.5 9.0 collective-permute-done.23
  307.3 24.4 %pad_maximum_fusion = bf16[1024,4224]{1,0:T(8,128)(2,1)} fusion(bf16[512,4224]{1,0:T(8,128)(2,1)S(1)} %collective-permute-done.31, bf16[512,128]{1,0:T(8,128)(2,1)S(1)} %copy-done.168, bf16[512,2048]{1,0:T(8,128)(2,1)S(1)} %bitcast.999, bf16[512,2048]{1,0:T(8,128)(2,1)S(1)} %bitcast.997), kind=kLoop, calls=%fused_computation.4 | loop fusion | flops 34603008 | bytes 17301504 | tf_op jit(solution)/shard_map/concatenate | solution.py:414
  338.0 8.6 collective-permute-done.29
  353.5 8.9 fusion.11
  373.9 40.5 %collective-permute-done.65 = bf16[2,64,4224]{2,1,0:T(8,128)(2,1)S(1)} collective-permute-done((bf16[2,64,4224]{2,1,0:T(8,128)(2,1)S(1)}, bf16[2,64,4224]{2,1,0:T(8,128)(2,1)S(1)}, u32[]{:S(2)}, u32[]{:S(2)}) %collective-permute-start.65) | collective-permute-done | bytes 1081376 | tf_op jit(solution)/shard_map/feed_micro1/ppermute | solution.py:311
  417.3 20.3 %collective-permute-done.34 = bf16[2,64,4224]{2,1,0:T(8,128)(2,1)S(1)} collective-permute-done((bf16[2,64,4224]{2,1,0:T(8,128)(2,1)S(1)}, bf16[2,64,4224]{2,1,0:T(8,128)(2,1)S(1)}, u32[]{:S(2)}, u32[]{:S(2)}) %collective-permute-start.34) | collective-permute-done | bytes 1081376 | tf_op jit(solution)/shard_map/feed_micro0/ppermute | solution.py:311
  467.1 14.9 %collective-permute-done.68 = bf16[128,2048]{1,0:T(8,128)(2,1)S(1)} collective-permute-done((bf16[128,2048]{1,0:T(8,128)(2,1)S(1)}, bf16[128,2048]{1,0:T(8,128)(2,1)S(1)}, u32[]{:S(2)}, u32[]{:S(2)}) %collective-permute-start.68) | collective-permute-done | bytes 524320 | tf_op jit(solution)/shard_map/feed_micro1/ppermute | solution.py:311
  514.3 8.9 collective-permute-done.40
  727.4 10.6 collective-permute-done.102
  794.3 9.5 collective-permute-done.87
  808.5 8.9 collective-permute-done.88
  822.1 9.5 collective-permute-done.90
  861.8 8.9 collective-permute-done.153
  876.4 20.5 %collective-permute-done.104 = bf16[64,4224]{1,0:T(8,128)(2,1)S(1)} collective-permute-done((bf16[64,4224]{1,0:T(8,128)(2,1)S(1)}, bf16[64,4224]{1,0:T(8,128)(2,1)S(1)}, u32[]{:S(2)}, u32[]{:S(2)}) %collective-permute-start.104) | collective-permute-done | bytes 540704 | tf_op jit(solution)/shard_map/feed_back_micro0/ppermute | solution.py:311
  896.9 22.2 %collective-permute-done.105 = bf16[64,4224]{1,0:T(8,128)(2,1)S(1)} collective-permute-done((bf16[64,4224]{1,0:T(8,128)(2,1)S(1)}, bf16[64,4224]{1,0:T(8,128)(2,1)S(1)}, u32[]{:S(2)}, u32[]{:S(2)}) %collective-permute-start.105) | collective-permute-done | bytes 540704 | tf_op jit(solution)/shard_map/feed_back_micro0/ppermute | solution.py:311
  927.3 10.0 collective-permute-done.154
  947.6 19.5 %collective-permute-done.108 = bf16[64,4224]{1,0:T(8,128)(2,1)S(1)} collective-permute-done((bf16[64,4224]{1,0:T(8,128)(2,1)S(1)}, bf16[64,4224]{1,0:T(8,128)(2,1)S(1)}, u32[]{:S(2)}, u32[]{:S(2)}) %collective-permute-start.108) | collective-permute-done | bytes 540704 | tf_op jit(solution)/shard_map/feed_back_micro0/ppermute | solution.py:311
  972.0 8.4 fusion.382
  980.4 12.2 bitcast_add_fusion
  1018.7 13.2 collective-permute-done.157
  1058.0 17.4 %collective-permute-done.116 = bf16[4,32,1024]{2,1,0:T(8,128)(2,1)} collective-permute-done((bf16[4,32,1024]{2,1,0:T(8,128)(2,1)}, bf16[4,32,1024]{2,1,0:T(8,128)(2,1)}, u32[]{:S(2)}, u32[]{:S(2)}) %collective-permute-start.116) | collective-permute-done | bytes 262176 | tf_op jit(solution)/shard_map/feed_back_out_micro0/ppermute | solution.py:314
  1084.9 9.3 collective-permute-done.115
  1094.2 14.9 %collective-permute-done.117 = bf16[4,32,1024]{2,1,0:T(8,128)(2,1)S(1)} collective-permute-done((bf16[4,32,1024]{2,1,0:T(8,128)(2,1)}, bf16[4,32,1024]{2,1,0:T(8,128)(2,1)S(1)}, u32[]{:S(2)}, u32[]{:S(2)}) %collective-permute-start.117) | collective-permute-done | bytes 262176 | tf_op jit(solution)/shard_map/feed_back_out_micro0/ppermute | solution.py:314
  1220.8 13.0 collective-permute-done.128
  1282.5 10.4 collective-permute-done.182
  1327.5 11.1 copy.510
  (1479 shorter events, 897.7 us)
Async XLA Ops:
  7.2 443.1 %all-gather.5.cloned.1.call-start = ((), (), s32[]{:S(2)}) async-start(), calls=%async_computation.4 | async-start | bytes 1179648 | tf_op jit(solution)/shard_map/all_gather | solution.py:775
  21.0 80.8 %collective-permute-start.14 = (bf16[512,3072]{1,0:T(8,128)(2,1)}, bf16[512,3072]{1,0:T(8,128)(2,1)}, u32[]{:S(2)}, u32[]{:S(2)}) collective-permute-start(bf16[512,3072]{1,0:T(8,128)(2,1)} %pad_maximum_fusion.9), channel_id=1, source_target_pairs={{0,4},{4,0},{8,12},{12,8},{16,20},{20,16},{24,28},{28,24},{1,5},{5... | collective-permute-start | bytes 9437192 | tf_op jit(solution)/shard_map/ppermute | solution.py:308
  78.2 430.8 %all-gather.9.cloned.1.call-start = ((), (), s32[]{:S(2)}) async-start(), calls=%async_computation.6 | async-start | bytes 1769472 | tf_op jit(solution)/shard_map/all_gather | solution.py:777
  81.5 154.0 %collective-permute-start.22 = (bf16[1024,512]{1,0:T(8,128)(2,1)}, bf16[1024,512]{1,0:T(8,128)(2,1)}, u32[]{:S(2)}, u32[]{:S(2)}) collective-permute-start(bf16[1024,512]{1,0:T(8,128)(2,1)} %param.28), channel_id=1, source_target_pairs={{0,4},{4,0},{8,12},{12,8},{16,20},{20,16},{24,28},{28,24},{1,5},{5... | collective-permute-start | bytes 3145736 | tf_op jit(solution)/shard_map/ppermute | solution.py:308
  81.5 179.3 %collective-permute-start.39 = (bf16[2048,512]{1,0:T(8,128)(2,1)}, bf16[2048,512]{1,0:T(8,128)(2,1)}, u32[]{:S(2)}, u32[]{:S(2)}) collective-permute-start(bf16[2048,512]{1,0:T(8,128)(2,1)} %param.34), channel_id=1, source_target_pairs={{0,4},{4,0},{8,12},{12,8},{16,20},{20,16},{24,28},{28,24},{1,5},{5... | collective-permute-start | bytes 6291464 | tf_op jit(solution)/shard_map/ppermute | solution.py:308
  100.1 135.5 %collective-permute-start.5 = (bf16[1024,256]{1,0:T(8,128)(2,1)}, bf16[1024,256]{1,0:T(8,128)(2,1)}, u32[]{:S(2)}, u32[]{:S(2)}) collective-permute-start(bf16[1024,256]{1,0:T(8,128)(2,1)} %get-tuple-element.251), channel_id=1, source_target_pairs={{0,24},{4,28},{8,16},{12,20},{16,8},{20,12},{24,0},{28,4},{1,25},{... | collective-permute-start | bytes 1572872 | tf_op jit(solution)/shard_map/ppermute | solution.py:311
  161.8 75.3 %collective-permute-start.4 = (bf16[1024,256]{1,0:T(8,128)(2,1)}, bf16[1024,256]{1,0:T(8,128)(2,1)}, u32[]{:S(2)}, u32[]{:S(2)}) collective-permute-start(bf16[1024,256]{1,0:T(8,128)(2,1)} %get-tuple-element.252), channel_id=1, source_target_pairs={{0,16},{4,20},{8,24},{12,28},{16,0},{20,4},{24,8},{28,12},{1,17},{... | collective-permute-start | bytes 1572872 | tf_op jit(solution)/shard_map/ppermute | solution.py:311
  210.6 361.2 %all-gather.11.cloned.1.call-start = ((), (), s32[]{:S(2)}) async-start(), calls=%async_computation.7 | async-start | bytes 4718592 | tf_op jit(solution)/shard_map/all_gather | solution.py:784
  232.0 344.6 %all-gather.7.cloned.1.call-start = ((), (), s32[]{:S(2)}) async-start(), calls=%async_computation.5 | async-start | bytes 9437184 | tf_op jit(solution)/shard_map/all_gather | solution.py:782
  241.8 65.5 %collective-permute-start.31 = (bf16[512,4224]{1,0:T(8,128)(2,1)}, bf16[512,4224]{1,0:T(8,128)(2,1)S(1)}, u32[]{:S(2)}, u32[]{:S(2)}) collective-permute-start(bf16[512,4224]{1,0:T(8,128)(2,1)} %pad_maximum_fusion.4), channel_id=1, source_target_pairs={{0,4},{4,0},{8,12},{12,8},{16,20},{20,16},{24,28},{28,24},{1,5},{5... | collective-permute-start | bytes 12976136 | tf_op jit(solution)/shard_map/ppermute | solution.py:308
  245.6 284.4 %collective-permute-start.6 = (bf16[4,1024,256]{2,1,0:T(8,128)(2,1)}, bf16[4,1024,256]{2,1,0:T(8,128)(2,1)}, u32[]{:S(2)}, u32[]{:S(2)}) collective-permute-start(bf16[4,1024,256]{2,1,0:T(8,128)(2,1)} %get-tuple-element.249), channel_id=1, source_target_pairs={{0,4},{4,0},{8,12},{12,8},{16,20},{20,16},{24,28},{28,24},{1,5},{5... | collective-permute-start | bytes 6291464 | tf_op jit(solution)/shard_map/ppermute | solution.py:308
  337.8 511.1 %reduce-scatter.5.cloned.1.call-start = ((), (), s32[]{:S(2)}) async-start(), calls=%async_computation.8 | async-start | bytes 1253376 | tf_op jit(solution)/shard_map/reduce_scatter | solution.py:799
  369.5 44.9 %collective-permute-start.65 = (bf16[2,64,4224]{2,1,0:T(8,128)(2,1)S(1)}, bf16[2,64,4224]{2,1,0:T(8,128)(2,1)S(1)}, u32[]{:S(2)}, u32[]{:S(2)}) collective-permute-start(bf16[2,64,4224]{2,1,0:T(8,128)(2,1)S(1)} %slice.1244), channel_id=1, source_target_pairs={{0,16},{4,20},{8,24},{12,28},{16,0},{20,4},{24,8},{28,12},{1,17},{... | collective-permute-start | bytes 3244040 | tf_op jit(solution)/shard_map/feed_micro1/ppermute | solution.py:311
  370.6 45.4 %collective-permute-start.63 = (bf16[2,64,4224]{2,1,0:T(8,128)(2,1)S(1)}, bf16[2,64,4224]{2,1,0:T(8,128)(2,1)S(1)}, u32[]{:S(2)}, u32[]{:S(2)}) collective-permute-start(bf16[2,64,4224]{2,1,0:T(8,128)(2,1)S(1)} %slice_bitcast_fusion.7), channel_id=1, source_target_pairs={{0,8},{4,12},{8,0},{12,4},{16,24},{20,28},{24,16},{28,20},{1,9},{5... | collective-permute-start | bytes 3244040 | tf_op jit(solution)/shard_map/feed_micro1/ppermute | solution.py:311
  371.9 65.6 %collective-permute-start.34 = (bf16[2,64,4224]{2,1,0:T(8,128)(2,1)S(1)}, bf16[2,64,4224]{2,1,0:T(8,128)(2,1)S(1)}, u32[]{:S(2)}, u32[]{:S(2)}) collective-permute-start(bf16[2,64,4224]{2,1,0:T(8,128)(2,1)S(1)} %slice.1207), channel_id=1, source_target_pairs={{0,16},{4,20},{8,24},{12,28},{16,0},{20,4},{24,8},{28,12},{1,17},{... | collective-permute-start | bytes 3244040 | tf_op jit(solution)/shard_map/feed_micro0/ppermute | solution.py:311
  372.6 66.6 %collective-permute-start.32 = (bf16[2,64,4224]{2,1,0:T(8,128)(2,1)S(1)}, bf16[2,64,4224]{2,1,0:T(8,128)(2,1)S(1)}, u32[]{:S(2)}, u32[]{:S(2)}) collective-permute-start(bf16[2,64,4224]{2,1,0:T(8,128)(2,1)S(1)} %slice_bitcast_fusion.11), channel_id=1, source_target_pairs={{0,8},{4,12},{8,0},{12,4},{16,24},{20,28},{24,16},{28,20},{1,9},{5... | collective-permute-start | bytes 3244040 | tf_op jit(solution)/shard_map/feed_micro0/ppermute | solution.py:311
  706.4 349.2 %reduce-scatter.7.cloned.1.call-start = ((), (), s32[]{:S(2)}) async-start(), calls=%async_computation.9 | async-start | bytes 1179648 | tf_op jit(solution)/shard_map/reduce_scatter | solution.py:801
  757.5 535.4 %reduce-scatter.11.cloned.1.call-start = ((), (), s32[]{:S(2)}) async-start(), calls=%async_computation.11 | async-start | bytes 4718592 | tf_op jit(solution)/shard_map/reduce_scatter | solution.py:795
  763.1 586.5 %reduce-scatter.9.cloned.1.call-start = ((), (), s32[]{:S(2)}) async-start(), calls=%async_computation.10 | async-start | bytes 9437184 | tf_op jit(solution)/shard_map/reduce_scatter | solution.py:793
  819.7 103.5 %collective-permute-start.195 = (bf16[1024,4,256]{2,0,1:T(8,128)(2,1)}, bf16[1024,4,256]{2,0,1:T(8,128)(2,1)}, u32[]{:S(2)}, u32[]{:S(2)}) collective-permute-start(bf16[1024,4,256]{2,0,1:T(8,128)(2,1)} %bitcast_convert_fusion), channel_id=1, source_target_pairs={{0,4},{4,0},{8,12},{12,8},{16,20},{20,16},{24,28},{28,24},{1,5},{5... | collective-permute-start | bytes 6291464 | tf_op jit(solution)/shard_map/ppermute | solution.py:308
  838.5 212.7 %collective-permute-start.194 = (bf16[2048,512]{1,0:T(8,128)(2,1)}, bf16[2048,512]{1,0:T(8,128)(2,1)}, u32[]{:S(2)}, u32[]{:S(2)}) collective-permute-start(bf16[2048,512]{1,0:T(8,128)(2,1)} %slice.1844), channel_id=1, source_target_pairs={{0,4},{4,0},{8,12},{12,8},{16,20},{20,16},{24,28},{28,24},{1,5},{5... | collective-permute-start | bytes 6291464 | tf_op jit(solution)/shard_map/ppermute | solution.py:308
  870.7 48.5 %collective-permute-start.106 = (bf16[64,4224]{1,0:T(8,128)(2,1)S(1)}, bf16[64,4224]{1,0:T(8,128)(2,1)S(1)}, u32[]{:S(2)}, u32[]{:S(2)}) collective-permute-start(bf16[64,4224]{1,0:T(8,128)(2,1)S(1)} %get-tuple-element.254), channel_id=1, source_target_pairs={{0,16},{4,20},{8,24},{12,28},{16,0},{20,4},{24,8},{28,12},{1,17},{... | collective-permute-start | bytes 1622024 | tf_op jit(solution)/shard_map/feed_back_micro0/ppermute | solution.py:311
  874.4 44.7 %collective-permute-start.105 = (bf16[64,4224]{1,0:T(8,128)(2,1)S(1)}, bf16[64,4224]{1,0:T(8,128)(2,1)S(1)}, u32[]{:S(2)}, u32[]{:S(2)}) collective-permute-start(bf16[64,4224]{1,0:T(8,128)(2,1)S(1)} %get-tuple-element.255), channel_id=1, source_target_pairs={{0,8},{4,12},{8,0},{12,4},{16,24},{20,28},{24,16},{28,20},{1,9},{5... | collective-permute-start | bytes 1622024 | tf_op jit(solution)/shard_map/feed_back_micro0/ppermute | solution.py:311
  921.1 46.0 %collective-permute-start.108 = (bf16[64,4224]{1,0:T(8,128)(2,1)S(1)}, bf16[64,4224]{1,0:T(8,128)(2,1)S(1)}, u32[]{:S(2)}, u32[]{:S(2)}) collective-permute-start(bf16[64,4224]{1,0:T(8,128)(2,1)S(1)} %collective-permute-done.104), channel_id=1, source_target_pairs={{0,16},{4,20},{8,24},{12,28},{16,0},{20,4},{24,8},{28,12},{1,17},{... | collective-permute-start | bytes 1622024 | tf_op jit(solution)/shard_map/feed_back_micro0/ppermute | solution.py:311
  923.2 45.8 %collective-permute-start.109 = (bf16[64,4224]{1,0:T(8,128)(2,1)S(1)}, bf16[64,4224]{1,0:T(8,128)(2,1)S(1)}, u32[]{:S(2)}, u32[]{:S(2)}) collective-permute-start(bf16[64,4224]{1,0:T(8,128)(2,1)S(1)} %collective-permute-done.107), channel_id=1, source_target_pairs={{0,8},{4,12},{8,0},{12,4},{16,24},{20,28},{24,16},{28,20},{1,9},{5... | collective-permute-start | bytes 1622024 | tf_op jit(solution)/shard_map/feed_back_micro0/ppermute | solution.py:311
  937.3 69.6 %collective-permute-start.198 = (bf16[1024,256]{1,0:T(8,128)(2,1)}, bf16[1024,256]{1,0:T(8,128)(2,1)}, u32[]{:S(2)}, u32[]{:S(2)}) collective-permute-start(bf16[1024,256]{1,0:T(8,128)(2,1)} %get-tuple-element.245), channel_id=1, source_target_pairs={{0,24},{4,28},{8,16},{12,20},{16,8},{20,12},{24,0},{28,4},{1,25},{... | collective-permute-start | bytes 1572872 | tf_op jit(solution)/shard_map/ppermute | solution.py:311
  938.6 68.6 %collective-permute-start.197 = (bf16[1024,256]{1,0:T(8,128)(2,1)}, bf16[1024,256]{1,0:T(8,128)(2,1)}, u32[]{:S(2)}, u32[]{:S(2)}) collective-permute-start(bf16[1024,256]{1,0:T(8,128)(2,1)} %get-tuple-element.246), channel_id=1, source_target_pairs={{0,16},{4,20},{8,24},{12,28},{16,0},{20,4},{24,8},{28,12},{1,17},{... | collective-permute-start | bytes 1572872 | tf_op jit(solution)/shard_map/ppermute | solution.py:311
  968.9 40.2 %collective-permute-start.156 = (bf16[4,2,32,1024]{3,2,0,1:T(8,128)(2,1)}, bf16[4,2,32,1024]{3,2,0,1:T(8,128)(2,1)}, u32[]{:S(2)}, u32[]{:S(2)}) collective-permute-start(bf16[4,2,32,1024]{3,2,0,1:T(8,128)(2,1)} %bitcast.969), channel_id=1, source_target_pairs={{0,1},{1,0},{2,3},{3,2},{4,5},{5,4},{6,7},{7,6},{8,9},{9,8},{10,11... | collective-permute-start | bytes 1572872 | tf_op jit(solution)/shard_map/feed_back_out_micro1/ppermute | solution.py:314
  1007.2 305.0 %collective-permute-start.190 = (bf16[512,4224]{1,0:T(8,128)(2,1)}, bf16[512,4224]{1,0:T(8,128)(2,1)}, u32[]{:S(2)}, u32[]{:S(2)}) collective-permute-start(bf16[512,4224]{1,0:T(8,128)(2,1)} %slice.1842), channel_id=1, source_target_pairs={{0,4},{4,0},{8,12},{12,8},{16,20},{20,16},{24,28},{28,24},{1,5},{5... | collective-permute-start | bytes 12976136 | tf_op jit(solution)/shard_map/ppermute | solution.py:308
  1094.2 52.7 %collective-permute-start.200 = (bf16[1024,256]{1,0:T(8,128)(2,1)S(1)}, bf16[1024,256]{1,0:T(8,128)(2,1)S(1)}, u32[]{:S(2)}, u32[]{:S(2)}) collective-permute-start(bf16[1024,256]{1,0:T(8,128)(2,1)S(1)} %fusion.171), channel_id=1, source_target_pairs={{0,2},{1,3},{2,0},{3,1},{4,6},{5,7},{6,4},{7,5},{8,10},{9,11},{10,... | collective-permute-start | bytes 1572872 | tf_op jit(solution)/shard_map/ppermute | solution.py:314
  1173.5 45.6 %collective-permute-start.185 = (bf16[1024,512]{1,0:T(8,128)(2,1)}, bf16[1024,512]{1,0:T(8,128)(2,1)S(1)}, u32[]{:S(2)}, u32[]{:S(2)}) collective-permute-start(bf16[1024,512]{1,0:T(8,128)(2,1)} %slice.1845), channel_id=1, source_target_pairs={{0,4},{4,0},{8,12},{12,8},{16,20},{20,16},{24,28},{28,24},{1,5},{5... | collective-permute-start | bytes 3145736 | tf_op jit(solution)/shard_map/ppermute | solution.py:308
  1210.7 130.4 %collective-permute-start.184 = (bf16[512,3072]{1,0:T(8,128)(2,1)}, bf16[512,3072]{1,0:T(8,128)(2,1)}, u32[]{:S(2)}, u32[]{:S(2)}) collective-permute-start(bf16[512,3072]{1,0:T(8,128)(2,1)} %slice.1843), channel_id=1, source_target_pairs={{0,4},{4,0},{8,12},{12,8},{16,20},{20,16},{24,28},{28,24},{1,5},{5... | collective-permute-start | bytes 9437192 | tf_op jit(solution)/shard_map/ppermute | solution.py:308
  (432 other events, 7257.1 us)
Sparse Core Ops, SparseCore 0:
  78.3 24.6 all-gather.4
  210.7 29.0 all-gather.8
  242.3 39.3 all-gather.10
  337.9 75.0 all-gather.6
  706.5 38.7 reduce-scatter.4
  757.6 34.7 reduce-scatter.6
  795.8 52.2 reduce-scatter.10
  852.0 106.7 reduce-scatter.8

commit v2 on v1

--- a/solution.py
+++ b/solution.py
@@ -429,6 +429,374 @@
     return jnp.einsum(spec, a, b, preferred_element_type=F32).astype(BF16)
 
 
+def flip(index, bit):
+    return index + (1 - 2 * ((index // bit) % 2)) * bit
+
+
+def chip_partner(rel):
+    d = lax.axis_index("dp")
+    for bit in (1, 2):
+        if rel & bit:
+            d = flip(d, 2 * bit)
+    return {"dp": d}
+
+
+def z_partner(rel):
+    return {"tensor": flip(lax.axis_index("tensor"), rel)}
+
+
+class Wire:
+    def __init__(self, send, recv):
+        self.send, self.recv, self.used = send, recv, 0
+
+    def start(self, src, dst, partner):
+        i = self.used
+        self.used += 1
+        copy = pltpu.make_async_remote_copy(
+            src_ref=src,
+            dst_ref=dst,
+            send_sem=self.send.at[i],
+            recv_sem=self.recv.at[i],
+            device_id=partner,
+            device_id_type=pl.DeviceIdType.MESH,
+        )
+        copy.start()
+        return copy
+
+
+def tile_of(width):
+    return next(size for size in (384, 256, 128) if width % size == 0)
+
+
+def over_tiles(width, body):
+    tile = tile_of(width)
+
+    def step(i, carry):
+        body(pl.ds(pl.multiple_of(i * tile, 128), tile))
+        return carry
+
+    lax.fori_loop(0, width // tile, step, 0)
+
+
+class ByChips:
+    copies = 12
+    partners = [("dp", 1), ("dp", 2)]
+
+    def __init__(self, x, w, by_cols, out_width, local, args, outs, scratch=()):
+        self.by_cols, self.local, self.count = by_cols, local, len(args)
+        self.rows = x.shape[1]
+        self.width = w.shape[0] if by_cols else w.shape[1]
+        self.args = (x, w) + tuple(args)
+        self.outs = (jax.ShapeDtypeStruct((4, self.rows, out_width), BF16),) + tuple(outs)
+        half = self.rows // 2
+        self.scratch = [
+            pltpu.VMEM((4, self.rows, self.width), BF16),
+            pltpu.VMEM((2, 2, half, self.width), BF16),
+            pltpu.VMEM((2, half, self.width), BF16),
+            pltpu.VMEM((self.rows, self.width), F32),
+        ] + list(scratch)
+        self.flops = 8 * self.rows * x.shape[2] * self.width
+
+    def run(self, wire, args, outs, scratch):
+        x, w = args[:2]
+        part, first, second, summed = scratch[:4]
+        gathered = outs[0]
+        rows, depth, half = self.rows, x.shape[2], self.rows // 2
+        dims = BY_COLS if self.by_cols else PLAIN
+
+        def dot(low, high):
+            def body(cols):
+                tile = w[cols, :] if self.by_cols else w[:, cols]
+                left = x[low:high].reshape((high - low) * rows, depth)
+                part[low:high, :, cols] = fast(left, tile, dims).astype(BF16).reshape(
+                    high - low, rows, tile_of(self.width)
+                )
+
+            over_tiles(self.width, body)
+
+        def piece(p):
+            return slice(p * half, (p + 1) * half), 1 << p, 1 << (1 - p)
+
+        dot(1, 4)
+        sent = []
+        for p in range(2):
+            at, bit, _ = piece(p)
+            for i, rel in enumerate((bit, 3)):
+                sent.append(wire.start(part.at[rel, at], first.at[p, i], chip_partner(bit)))
+        dot(0, 1)
+        yield
+        later = []
+        for p in range(2):
+            at, _, other = piece(p)
+            sent[2 * p + 1].wait_recv()
+
+            def add(cols, p=p, at=at, other=other):
+                both = part[other, at, cols].astype(F32) + first[p, 1, :, cols].astype(F32)
+                part[other, at, cols] = both.astype(BF16)
+
+            over_tiles(self.width, add)
+            later.append(wire.start(part.at[other, at], second.at[p], chip_partner(other)))
+        yield
+        for p in range(2):
+            at, _, _ = piece(p)
+            sent[2 * p].wait_recv()
+            later[p].wait_recv()
+
+            def finish(cols, p=p, at=at):
+                both = part[0, at, cols].astype(F32) + first[p, 0, :, cols].astype(F32)
+                summed[at, cols] = both + second[p, :, cols].astype(F32)
+
+            over_tiles(self.width, finish)
+        self.local(summed, gathered.at[0], args[2:], outs[1:], scratch[4:])
+        near, far = [], []
+        for p in range(2):
+            at, bit, other = piece(p)
+            near.append(wire.start(gathered.at[0, at], gathered.at[bit, at], chip_partner(bit)))
+            far.append(wire.start(gathered.at[0, at], gathered.at[other, at], chip_partner(other)))
+        yield
+        last = []
+        for p in range(2):
+            at, bit, other = piece(p)
+            near[p].wait_recv()
+            last.append(wire.start(gathered.at[bit, at], gathered.at[3, at], chip_partner(other)))
+        yield
+        for copy in far + last:
+            copy.wait_recv()
+        for copy in sent + later + near + far + last:
+            copy.wait_send()
+
+
+class ByTensor:
+    copies = 9
+    partners = [("tensor", 1), ("tensor", 2), ("dp", 1), ("dp", 2), ("dp", 3)]
+
+    def __init__(self, x, w, by_cols, local, args, outs, gather=True):
+        self.by_cols, self.local, self.gather = by_cols, local, gather
+        self.rows = x.shape[1]
+        self.width = w.shape[0] if by_cols else w.shape[1]
+        self.args = (x, w) + tuple(args)
+        shape = (4, 4, self.rows // 4, self.width)
+        self.outs = (jax.ShapeDtypeStruct(shape, BF16),) if gather else ()
+        self.outs += tuple(outs)
+        self.copies = 9 if gather else 6
+        self.scratch = [
+            pltpu.VMEM((4, self.rows, self.width), BF16),
+            pltpu.VMEM((2, self.rows, self.width), BF16),
+            pltpu.VMEM((self.rows, self.width), BF16),
+            pltpu.VMEM((self.rows, self.width), F32),
+            pltpu.VMEM((4, self.rows, 128), F32),
+        ]
+        self.flops = 8 * self.rows * x.shape[2] * self.width
+
+    def run(self, wire, args, outs, scratch):
+        x, w = args[:2]
+        part, first, second, summed, stats = scratch
+        rows, depth = self.rows, x.shape[2]
+        r = rows // 4
+        dims = BY_COLS if self.by_cols else PLAIN
+
+        def body(cols):
+            tile = w[cols, :] if self.by_cols else w[:, cols]
+            low = fast(x[...].reshape(4 * rows, depth), tile, dims).astype(BF16)
+            for c in range(4):
+                for z in range(4):
+                    part[z, c * r : (c + 1) * r, cols] = low[c * rows + z * r : c * rows + z * r + r]
+
+        over_tiles(self.width, body)
+        sent = [wire.start(part.at[z], first.at[i], z_partner(1)) for i, z in enumerate((1, 3))]
+        yield
+        sent[1].wait_recv()
+
+        def add(cols):
+            both = part[2, :, cols].astype(F32) + first[1, :, cols].astype(F32)
+            part[2, :, cols] = both.astype(BF16)
+
+        over_tiles(self.width, add)
+        later = wire.start(part.at[2], second, z_partner(2))
+        yield
+        sent[0].wait_recv()
+        later.wait_recv()
+
+        def finish(cols):
+            both = part[0, :, cols].astype(F32) + first[0, :, cols].astype(F32)
+            summed[:, cols] = both + second[:, cols].astype(F32)
+
+        over_tiles(self.width, finish)
+        rest = outs[1:] if self.gather else outs
+        local = self.local(summed, args[2:], rest)
+        stats[0] = jnp.broadcast_to(next(local), (rows, 128))
+        sums = [
+            wire.start(stats.at[0], stats.at[rel], chip_partner(rel)) for rel in range(1, 4)
+        ]
+        yield
+        total_sums = stats[0]
+        for rel in range(1, 4):
+            sums[rel - 1].wait_recv()
+            moved = [stats[rel, (i ^ rel) * r : (i ^ rel) * r + r, :] for i in range(4)]
+            total_sums = total_sums + jnp.concatenate(moved, axis=0)
+        low = local.send(total_sums[:, 0:1])
+        if self.gather:
+            gathered = outs[0]
+            for c in range(4):
+                gathered[c, 0] = low[c * r : (c + 1) * r]
+            far = wire.start(gathered.at[:, 0], gathered.at[:, 2], z_partner(2))
+            near = wire.start(gathered.at[:, 0], gathered.at[:, 1], z_partner(1))
+            yield
+            far.wait_recv()
+            last = wire.start(gathered.at[:, 2], gathered.at[:, 3], z_partner(1))
+            yield
+            near.wait_recv()
+            last.wait_recv()
+            sent += [far, near, last]
+        for copy in sent + [later] + sums:
+            copy.wait_send()
+
+
+def together(groups, collective_id):
+    partners = sorted({p for g in groups for p in g.partners})
+
+    def kernel(*refs):
+        refs = list(refs)
+
+        def take(count):
+            got = refs[:count]
+            del refs[:count]
+            return got
+
+        args = [take(len(g.args)) for g in groups]
+        outs = [take(len(g.outs)) for g in groups]
+        scratch = [take(len(g.scratch)) for g in groups]
+        wires = [Wire(*take(2)) for g in groups]
+        barrier = pltpu.get_barrier_semaphore()
+        for axis, rel in partners:
+            partner = chip_partner(rel) if axis == "dp" else z_partner(rel)
+            pl.semaphore_signal(
+                barrier, inc=1, device_id=partner, device_id_type=pl.DeviceIdType.MESH
+            )
+        pl.semaphore_wait(barrier, len(partners))
+        running = [
+            g.run(wire, a, o, s) for g, wire, a, o, s in zip(groups, wires, args, outs, scratch)
+        ]
+        while running:
+            left = []
+            for run in running:
+                if next(run, running) is not running:
+                    left.append(run)
+            running = left
+
+    args = [x for g in groups for x in g.args]
+    outs = [x for g in groups for x in g.outs]
+    scratch = [x for g in groups for x in g.scratch]
+    for g in groups:
+        scratch += [pltpu.SemaphoreType.DMA((g.copies,))] * 2
+    size = sum(x.size * x.dtype.itemsize for x in args + outs)
+    flat = pl.pallas_call(
+        kernel,
+        out_shape=outs,
+        in_specs=[pl.BlockSpec(memory_space=pltpu.VMEM)] * len(args),
+        out_specs=[pl.BlockSpec(memory_space=pltpu.VMEM)] * len(outs),
+        scratch_shapes=scratch,
+        compiler_params=pltpu.CompilerParams(
+            collective_id=collective_id, has_side_effects=True, vmem_limit_bytes=58 * 2**20
+        ),
+        cost_estimate=pl.CostEstimate(
+            flops=sum(g.flops for g in groups), bytes_accessed=size, transcendentals=0
+        ),
+    )(*args)
+    results = []
+    for g in groups:
+        results.append(flat[: len(g.outs)])
+        flat = flat[len(g.outs) :]
+    return results
+
+
+def attend_local(qkv, slot, args, outs, scratch):
+    cos, sin, allowed = args
+    attend_kernel(qkv, cos, sin, allowed, outs[0], slot)
+
+
+def attend_back_local(d_attended, slot, args, outs, scratch):
+    low, cos, sin, allowed = args
+    attend_back_kernel(low, d_attended, cos, sin, allowed, slot)
+
+
+GELU_SCALE = (2.0 / 3.141592653589793) ** 0.5
+
+
+def feed_local(summed, slot, args, outs, scratch):
+    (up,) = args
+    gate_up, adapter = outs
+    units = slot.shape[1]
+    low = summed[:, 2 * units :].astype(BF16)
+    adapter[...] = low
+
+    def widen(cols):
+        gate_up[:, cols] = summed[:, cols] + fast(low, up[:, cols], PLAIN)
+
+    over_tiles(2 * units, widen)
+    tile = 256
+
+    def act(i, carry):
+        at = pl.ds(pl.multiple_of(i * tile, 128), tile)
+        also = pl.ds(pl.multiple_of(units + i * tile, 128), tile)
+        v = gate_up[:, at]
+        bent = jnp.tanh(GELU_SCALE * (v + 0.044715 * (v * v * v)))
+        slot[:, at] = (0.5 * v * (1.0 + bent) * gate_up[:, also]).astype(BF16)
+        return carry
+
+    lax.fori_loop(0, units // tile, act, 0)
+
+
+def feed_back_local(d_hidden, slot, args, outs, scratch):
+    gate_up, up = args
+    (adapter,) = scratch
+    units = d_hidden.shape[1]
+    tile = 256
+    adapter[...] = jnp.zeros(adapter.shape, F32)
+
+    def act(i, carry):
+        at = pl.ds(pl.multiple_of(i * tile, 128), tile)
+        also = pl.ds(pl.multiple_of(units + i * tile, 128), tile)
+        v, u, d = gate_up[:, at], gate_up[:, also], d_hidden[:, at]
+        bent = jnp.tanh(GELU_SCALE * (v + 0.044715 * (v * v * v)))
+        slope = 0.5 * (1.0 + bent) + 0.5 * v * (1.0 - bent * bent) * GELU_SCALE * (
+            1.0 + 3.0 * 0.044715 * (v * v)
+        )
+        d_gate = (d * u * slope).astype(BF16)
+        d_up = (d * (0.5 * v * (1.0 + bent))).astype(BF16)
+        slot[:, at] = d_gate
+        slot[:, also] = d_up
+        adapter[...] += fast(d_gate, up[:, at], BY_COLS) + fast(d_up, up[:, also], BY_COLS)
+        return carry
+
+    lax.fori_loop(0, units // tile, act, 0)
+    slot[:, 2 * units :] = adapter[...].astype(BF16)
+
+
+def norm_local(width, summed, args, outs):
+    base, gain = args
+    mid, inverse = outs
+    value = base[...] + summed[...]
+    mid[...] = value
+    squares = yield jnp.sum(value * value, axis=1, keepdims=True)
+    inv = lax.rsqrt(squares / width + EPSILON)
+    inverse[...] = inv
+    yield (value * inv * gain[...]).astype(BF16)
+
+
+def norm_back_local(width, summed, args, outs):
+    value, inverse, gain, skip = args
+    d_value, d_gain = outs
+    dy = summed[...]
+    scaled = dy * gain[...]
+    v, inv = value[...], inverse[...]
+    weighted = yield jnp.sum(scaled * v, axis=1, keepdims=True)
+    d_gain[...] = jnp.sum(dy * v * inv, axis=0, keepdims=True)
+    result = scaled * inv - v * (inv * inv * inv * weighted / width) + skip[...]
+    d_value[...] = result
+    yield result.astype(BF16)
+
+
 def proj_spread(links, w):
     rows = links.z_ag(w, 0)
     if links.chips == links.n_t:
@@ -680,7 +1048,12 @@
     width = v.shape[2] * links.chips
     dv = scaled * inv[:, :, None] - v * (inv**3 * weighted / width)[:, :, None]
     m.grad_g_attn = jnp.sum(dy * v * inv[:, :, None], axis=(0, 1))
-    d_joined = (dv + m.d_mid).astype(BF16)
+    m.d_joined = (dv + m.d_mid).astype(BF16)
+    leave_rows(links, m)
+
+
+def leave_rows(links, m):
+    d_joined = m.d_joined.reshape(links.chips, -1, m.d_joined.shape[-1])
     came = jnp.stack(links.chip_a2a([d_joined[rel] for rel in range(links.chips)]), 0)
     rows = came.shape[1]
     came = came.reshape(links.chips, rows, 2, -1)
@@ -692,6 +1065,116 @@
     whole = links.by_index(links.z_ag(both, 0), 0, links.t)
     whole = whole.reshape(-1, both.shape[1])
     m.d_hid, m.d_emb = whole[:, :model_width], whole[:, model_width:]
+
+
+def sds(shape, dtype=F32):
+    return jax.ShapeDtypeStruct(shape, dtype)
+
+
+def attend_group(links, w, m):
+    wide = m.joined.astype(F32) * m.inv_attn[:, :, None]
+    m.attn_in = (wide * w.g_attn).astype(BF16)
+    rows, width = m.attn_in.shape[1], w.qkv.shape[1]
+    args = (m.cos, m.sin, m.allowed_rel)
+    outs = (sds((rows, width), BF16),)
+    return ByChips(m.attn_in, w.qkv, False, width // 3, attend_local, args, outs)
+
+
+def attend_out_group(links, w, m):
+    r, width = m.joined.shape[1] // links.n_t, m.joined.shape[2]
+    m.joined_z = m.joined[:, :r].astype(F32).reshape(-1, width)
+    m.inv_attn_z = m.inv_attn[:, :r].reshape(-1, 1)
+    outs = (sds(m.joined_z.shape), sds(m.inv_attn_z.shape))
+    args = (m.joined_z, w.g_mlp[None, :])
+    work = partial(norm_local, width * links.chips)
+    return ByTensor(m.attended, w.out, False, work, args, outs)
+
+
+def feed_group(links, w, m):
+    rows, units = m.mlp_in.shape[1], w.down.shape[0]
+    outs = (sds((rows, 2 * units)), sds((rows, w.gate_up.shape[1] - 2 * units), BF16))
+    args = (w.adapter_up,)
+    return ByChips(m.mlp_in, w.gate_up, False, units, feed_local, args, outs)
+
+
+def feed_back_group(links, w, m):
+    args = (m.gate_up, w.adapter_up)
+    rank = w.gate_up.shape[1] - m.gate_up.shape[1]
+    scratch = (pltpu.VMEM((m.gate_up.shape[0], rank), F32),)
+    width = w.gate_up.shape[1]
+    return ByChips(m.mlp_low, w.down, True, width, feed_back_local, args, (), scratch)
+
+
+def feed_back_out_group(links, w, m):
+    width = m.mid_z.shape[1]
+    args = (m.mid_z, m.inv_mlp, w.g_mlp[None, :], m.d_block.reshape(m.mid_z.shape))
+    outs = (sds(m.mid_z.shape), sds((1, width)))
+    work = partial(norm_back_local, width * links.chips)
+    return ByTensor(m.gate_up_low, w.gate_up, True, work, args, outs)
+
+
+def attend_back_group(links, w, m):
+    args = (m.qkv_low, m.cos, m.sin, m.allowed_rel)
+    width = w.qkv.shape[1]
+    return ByChips(m.attn_low, w.out, True, width, attend_back_local, args, ())
+
+
+def leave_group(links, w, m):
+    width = m.joined_z.shape[1]
+    args = (m.joined_z, m.inv_attn_z, w.g_attn[None, :], m.d_mid)
+    outs = (sds(m.joined_z.shape), sds((1, width)))
+    work = partial(norm_back_local, width * links.chips)
+    return ByTensor(m.d_qkv, w.qkv, True, work, args, outs, gather=False)
+
+
+def take_attend(m, got):
+    m.attended, m.qkv_low = got
+
+
+def take_attend_out(m, got):
+    gathered, m.mid_z, m.inv_mlp = got
+    m.mlp_in = z_join(gathered, 1)
+    m.mid = m.mid_z.reshape(gathered.shape[0], -1, gathered.shape[3])
+
+
+def take_feed(m, got):
+    m.hidden, m.gate_up, m.adapter = got
+
+
+def take_feed_back(m, got):
+    (m.gate_up_low,) = got
+    m.gate_up_own = m.gate_up_low[0, :, : m.gate_up.shape[1]]
+
+
+def take_feed_back_out(m, got):
+    gathered, m.d_mid, d_gain = got
+    m.attn_low = z_join(gathered, 1)
+    m.grad_g_mlp = d_gain[0]
+
+
+def take_attend_back(m, got):
+    (m.d_qkv,) = got
+
+
+def take_leave(m, got):
+    d_joined, d_gain = got
+    m.grad_g_attn = d_gain[0]
+    m.d_joined = d_joined.astype(BF16)
+
+
+def fused(links, w, number, *work):
+    groups = [make(links, w, m) for make, _, m in work]
+    for (_, taker, m), got in zip(work, together(groups, number)):
+        taker(m, got)
+
+
+ATTEND = (attend_group, take_attend)
+ATTEND_OUT = (attend_out_group, take_attend_out)
+FEED = (feed_group, take_feed)
+FEED_BACK = (feed_back_group, take_feed_back)
+FEED_BACK_OUT = (feed_back_out_group, take_feed_back_out)
+ATTEND_BACK = (attend_back_group, take_attend_back)
+LEAVE = (leave_group, take_leave)
 
 
 def local(
@@ -763,25 +1246,43 @@
     packed = jnp.concatenate([state_map_weight, step_weight, mixer_gain[:, None]], axis=1)
 
     w.smalls = smalls
-    stages = [attend, attend_out, feed, feed_out, mix, settle]
-    stages += [feed_back, feed_back_out, attend_back, leave]
-    entries = ["joined", "attended", "mlp_in", "hidden", "mamba_in", "terms"]
-    entries += ["mlp_low", "gate_up_low", "attn_low", "d_qkv"]
-    for work, entry in zip(stages, entries):
+    def gather_mixer():
+        w.adapter_up = lax.all_gather(after(up_own, first.joined), "dp", axis=0, tiled=True)
+        w.proj = proj_spread(links, shared_projection_weight)
+        whole = lax.all_gather(after(packed, first.attended), "dp", axis=0, tiled=True)
+        w.bc = whole[:, :state_cols]
+        w.dt = whole[:, state_cols : state_cols + step_cols]
+        w.g_mamba = whole[:, state_cols + step_cols].astype(F32)
+        shard = after(mixer_input_weight.transpose(1, 0, 2), first.attended)
+        w.w_in = lax.all_gather(shard, "dp", axis=1, tiled=True)
+        shard = after(mixer_output_weight, first.attended)
+        w.mout = lax.all_gather(shard, "dp", axis=1, tiled=True)
+
+    def run(*works):
+        for work in works:
+            for m in micro:
+                stage(work, m)
+
+    if links.chips == 4 and links.n_t == 4 and len(micro) == 2:
+        a, b = micro
+        fused(links, w, 1, (*ATTEND, a))
+        gather_mixer()
+        fused(links, w, 2, (*ATTEND, b), (*ATTEND_OUT, a))
+        fused(links, w, 3, (*FEED, a), (*ATTEND_OUT, b))
+        fused(links, w, 4, (*FEED, b))
+        run(feed_out, mix, settle)
+        fused(links, w, 5, (*FEED_BACK, a))
+        fused(links, w, 6, (*FEED_BACK, b), (*FEED_BACK_OUT, a))
+        fused(links, w, 7, (*ATTEND_BACK, a), (*FEED_BACK_OUT, b))
+        fused(links, w, 8, (*ATTEND_BACK, b), (*LEAVE, a))
+        fused(links, w, 9, (*LEAVE, b))
         for m in micro:
-            setattr(m, entry, lax.optimization_barrier(getattr(m, entry)))
-            stage(work, m)
-        if work is attend:
-            w.adapter_up = lax.all_gather(after(up_own, first.joined), "dp", axis=0, tiled=True)
-            w.proj = proj_spread(links, shared_projection_weight)
-            packed = lax.all_gather(after(packed, first.attended), "dp", axis=0, tiled=True)
-            w.bc = packed[:, :state_cols]
-            w.dt = packed[:, state_cols : state_cols + step_cols]
-            w.g_mamba = packed[:, state_cols + step_cols].astype(F32)
-            shard = after(mixer_input_weight.transpose(1, 0, 2), first.attended)
-            w.w_in = lax.all_gather(shard, "dp", axis=1, tiled=True)
-            shard = after(mixer_output_weight, first.attended)
-            w.mout = lax.all_gather(shard, "dp", axis=1, tiled=True)
+            leave_rows(links, m)
+    else:
+        run(attend)
+        gather_mixer()
+        run(attend_out, feed, feed_out, mix, settle)
+        run(feed_back, feed_back_out, attend_back, leave)
     with jax.named_scope("outputs"):
         results = finish_output(links, micro)
 

time: 1370 us -> 1400 us (1.022)
  Pallas kernels: 27.4 us -> 633 us
  waiting for transfers between devices: 604 us -> 185 us
  starting transfers between devices: 228 us -> 105 us
  matrix products: 164 us -> 138 us
    pallas_call x0 -> x9, Pallas kernels: none -> 619 us  [together(): pl.pallas_call(kernel, out_shape=outs, in_specs=[pl.BlockSpec(memory_spac...]
    ppermute x120 -> x36, waiting for transfers between devices: 372 us -> 70.2 us  [chip_swap(): return lax.ppermute(x, 'dp', [(i, i ^ rel << 1) for i in range(self.n_dp)])]
    ppermute x75 -> x51, waiting for transfers between devices: 231 us -> 113 us  [z_swap(): return lax.ppermute(x, 'tensor', [(i, i ^ rel) for i in range(self.n_t)])]
    ppermute x120 -> x36, starting transfers between devices: 143 us -> 45.3 us  [chip_swap(): return lax.ppermute(x, 'dp', [(i, i ^ rel << 1) for i in range(self.n_dp)])]
    dot_general x28 -> x12, matrix products: 82.7 us -> 35.7 us  [dotl(): return jnp.einsum(spec, a, b, preferred_element_type=F32).astype(BF16)]
    ppermute x75 -> x51, starting transfers between devices: 82.4 us -> 57.2 us  [z_swap(): return lax.ppermute(x, 'tensor', [(i, i ^ rel) for i in range(self.n_t)])]
    dot_general x27 -> x25, matrix products: 81.8 us -> 103 us  [dotf(): return jnp.einsum(spec, a, b, preferred_element_type=F32)]
    unnamed x535 -> x357, local copies, waits for them, and re-layouts: 55.1 us -> 41.4 us
  transfers between devices with their start and end apart: 216 -> 108, of which waited for: 108 -> 42; matrix products, arithmetic and copies ran while one was open for 32% -> 30% of each run, Pallas kernels for 2% -> 45%
where the time goes in v2:
time: 1400 us; the launch traced here: 1390 us
  Pallas kernels  633 us (45%)
  waiting for transfers between devices  185 us (13%)
  other arithmetic  173 us (12%)
  local copies, waits for them, and re-layouts  141 us (10%)
  matrix products  138 us (10%)
  starting transfers between devices  105 us (8%)
  between operations  19.2 us (1%)
    pallas_call x9, Pallas kernels, together(): pl.pallas_call(kernel, out_shape=outs, in_specs=[pl.BlockSpec(memory_spac...  619 us
    ppermute x51, waiting for transfers between devices, z_swap(): return lax.ppermute(x, 'tensor', [(i, i ^ rel) for i in range(self.n_t)])  113 us
    dot_general x25, matrix products, dotf(): return jnp.einsum(spec, a, b, preferred_element_type=F32)  103 us
    ppermute x36, waiting for transfers between devices, chip_swap(): return lax.ppermute(x, 'dp', [(i, i ^ rel << 1) for i in range(self.n_dp)])  70.2 us
    ppermute x51, starting transfers between devices, z_swap(): return lax.ppermute(x, 'tensor', [(i, i ^ rel) for i in range(self.n_t)])  57.2 us
    concatenate x4, other arithmetic, core_pair(): return jnp.concatenate([x, links.core_swap(x)], axis=axis)  52.2 us
    ppermute x36, starting transfers between devices, chip_swap(): return lax.ppermute(x, 'dp', [(i, i ^ rel << 1) for i in range(self.n_dp)])  45.3 us
    unnamed x357, local copies, waits for them, and re-layouts  41.4 us
  transfers between devices with their start and end apart: 108, of which 42 were waited for; matrix products, arithmetic and copies ran while one was open for 30% of the time, Pallas kernels for 45%

profile of v2, /device:TPU:0, one launch (start us, length us, event | category | flops | bytes accessed | tf_op | source)
XLA Modules:
  0.0 1393.7 jit_solution(14014218787837199899)
XLA Ops:
  55.4 6.1 collective-permute-done.15
  65.1 20.8 %pad_maximum_fusion.2.refs_1_.refs_7_ = bf16[1024,3072]{1,0:T(8,128)(2,1)} fusion(bf16[512,3072]{1,0:T(8,128)(2,1)} %collective-permute-done.14, bf16[512,1024]{1,0:T(8,128)(2,1)S(1)} %get-tuple-element.270, bf16[512,1024]{1,0:T(8,128)(2,1)S(1)} %get-tuple-element.271, bf16[512,1024]{1,0:T(8,128)(2,1)S(1)} %get-tuple-element.269), kind=kLoop, calls=%fused_computation.10 | loop fusion | flops 25165824 | bytes 12582912 | tf_op jit(solution)/shard_map/concatenate | solution.py:414
  85.9 52.0 %shard_map.407 = (bf16[4,128,1024]{2,1,0:T(8,128)(2,1)}, bf16[128,3072]{1,0:T(8,128)(2,1)}) custom-call(bf16[4,128,1024]{2,1,0:T(8,128)(2,1)} %get-tuple-element.457.refs_0_, bf16[1024,3072]{1,0:T(8,128)(2,1)} %pad_maximum_fusion.2.refs_1_.refs_7_, f32[128,128]{1,0:T(8,128)} %pad_maximum_fusion.57.refs_2_.refs_3_, ...), custom_call_target="tpu_custom_call" | custom-call | flops 3221225472 | bytes 9371648 | tf_op jit(solution)/shard_map/pallas_call | solution.py:693
  146.6 9.3 fusion.195
  195.5 6.1 collective-permute-done.5
  201.7 18.4 %collective-permute-done.4 = bf16[1024,256]{1,0:T(8,128)(2,1)} collective-permute-done((bf16[1024,256]{1,0:T(8,128)(2,1)}, bf16[1024,256]{1,0:T(8,128)(2,1)}, u32[]{:S(2)}, u32[]{:S(2)}) %collective-permute-start.4) | collective-permute-done | bytes 524320 | tf_op jit(solution)/shard_map/ppermute | solution.py:311
  228.5 100.7 %shard_map.408 = (bf16[4,128,1024]{2,1,0:T(8,128)(2,1)}, bf16[128,3072]{1,0:T(8,128)(2,1)}, bf16[4,4,32,1024]{3,2,1,0:T(8,128)(2,1)}, f32[128,1024]{1,0:T(8,128)}, f32[128,1]{1,0:T(8,128)}) custom-call(bf16[4,128,1024]{2,1,0:T(8,128)(2,1)} %get-tuple-element.456.refs_0_, bf16[1024,3072]{1,0:T(8,128)(2,1)} %pad_maximum_fusion.2.refs_1_.refs_7_, ...), custom_call_target="tpu_custom_call" | custom-call | flops 4294967296 | bytes 14619136 | tf_op jit(solution)/shard_map/pallas_call | solution.py:693
  329.2 23.4 %pad_maximum_fusion.refs_1_.refs_5_.refs_7_ = bf16[1024,4224]{1,0:T(8,128)(2,1)} fusion(bf16[512,4224]{1,0:T(8,128)(2,1)} %collective-permute-done.19, bf16[512,128]{1,0:T(8,128)(2,1)S(1)} %copy-done.89, bf16[512,2048]{1,0:T(8,128)(2,1)S(1)} %bitcast.577, bf16[512,2048]{1,0:T(8,128)(2,1)S(1)} %bitcast.575), kind=kLoop, calls=%fused_computation.4 | loop fusion | flops 34603008 | bytes 17301504 | tf_op jit(solution)/shard_map/concatenate | solution.py:414
  352.6 87.7 %shard_map.409 = (bf16[4,128,2048]{2,1,0:T(8,128)(2,1)}, f32[128,4096]{1,0:T(8,128)}, bf16[128,128]{1,0:T(8,128)(2,1)}, bf16[4,4,32,1024]{3,2,1,0:T(8,128)(2,1)}, f32[128,1024]{1,0:T(8,128)}, /*index=5*/f32[128,1]{1,0:T(8,128)}) custom-call(bf16[4,128,1024]{2,1,0:T(8,128)(2,1)} %bitcast.618, bf16[1024,4224]{1,0:T(8,128)(2,1)} %pad_maximum_fusion.refs_1_.refs_5_.refs_7_, ...), custom_call_target="tpu_custom_call" | custom-call | flops 5502926848 | bytes 20222464 | tf_op jit(solution)/shard_map/pallas_call | solution.py:693
  447.4 65.0 %shard_map.410 = (bf16[4,128,2048]{2,1,0:T(8,128)(2,1)}, f32[128,4096]{1,0:T(8,128)}, bf16[128,128]{1,0:T(8,128)(2,1)}) custom-call(bf16[4,128,1024]{2,1,0:T(8,128)(2,1)} %bitcast.620, bf16[1024,4224]{1,0:T(8,128)(2,1)} %pad_maximum_fusion.refs_1_.refs_5_.refs_7_, bf16[128,4096]{1,0:T(8,128)(2,1)} %all-gather.5.cloned.1.call-done.refs_2_.refs_3_), custom_call_target="tpu_custom_call" | custom-call | flops 4429185024 | bytes 14974976 | tf_op jit(solution)/shard_map/pallas_call | solution.py:693
  523.4 8.4 collective-permute-done.26
  586.5 6.4 convolution_bitcast_fusion.3.gate_ref
  725.9 62.5 %shard_map.411.refs_4_ = bf16[4,128,4224]{2,1,0:T(8,128)(2,1)} custom-call(bf16[4,128,1024]{2,1,0:T(8,128)(2,1)} %bitcast.589, bf16[2048,1024]{1,0:T(8,128)(2,1)} %pad_maximum_fusion.6.refs_1_, f32[128,4096]{1,0:T(8,128)} %get-tuple-element.91.refs_2_, bf16[128,4096]{1,0:T(8,128)(2,1)} %all-gather.5.cloned.1.call-done.refs_2_.refs_3_), custom_call_target="tpu_custom_call" | custom-call | flops 2147483648 | bytes 12713984 | tf_op jit(solution)/shard_map/pallas_call | solution.py:693
  791.8 69.3 %shard_map.412 = (bf16[4,128,4224]{2,1,0:T(8,128)(2,1)}, bf16[4,4,32,1024]{3,2,1,0:T(8,128)(2,1)}, f32[128,1024]{1,0:T(8,128)}, f32[1,1024]{1,0:T(1,128)}) custom-call(bf16[4,128,1024]{2,1,0:T(8,128)(2,1)} %bitcast.587, bf16[2048,1024]{1,0:T(8,128)(2,1)} %pad_maximum_fusion.6.refs_1_, f32[128,4096]{1,0:T(8,128)} %get-tuple-element.87.refs_2_, ...), custom_call_target="tpu_custom_call" | custom-call | flops 6576668672 | bytes 28320256 | tf_op jit(solution)/shard_map/pallas_call | solution.py:693
  906.5 6.6 collective-permute-done.43
  918.8 7.8 collective-permute-done.44
  932.7 9.0 fusion.214
  945.0 89.7 %shard_map.413 = (bf16[4,128,3072]{2,1,0:T(8,128)(2,1)}, bf16[4,4,32,1024]{3,2,1,0:T(8,128)(2,1)}, f32[128,1024]{1,0:T(8,128)}, f32[1,1024]{1,0:T(1,128)}) custom-call(bf16[4,128,1024]{2,1,0:T(8,128)(2,1)} %bitcast.638, bf16[1024,1024]{1,0:T(8,128)(2,1)} %pad_maximum_fusion.10.refs_6_.refs_4_.refs_1_, bf16[128,3072]{1,0:T(8,128)(2,1)} %get-tuple-element.94.refs_2_, ...), custom_call_target="tpu_custom_call" | custom-call | flops 5502926848 | bytes 22880768 | tf_op jit(solution)/shard_map/pallas_call | solution.py:693
  1034.7 57.8 %shard_map.414 = (bf16[4,128,3072]{2,1,0:T(8,128)(2,1)}, f32[128,1024]{1,0:T(8,128)}, f32[1,1024]{1,0:T(1,128)}) custom-call(bf16[4,128,1024]{2,1,0:T(8,128)(2,1)} %bitcast.622, bf16[1024,1024]{1,0:T(8,128)(2,1)} %pad_maximum_fusion.10.refs_6_.refs_4_.refs_1_, bf16[128,3072]{1,0:T(8,128)(2,1)} %get-tuple-element.98.refs_2_, ...), custom_call_target="tpu_custom_call" | custom-call | flops 4294967296 | bytes 18293248 | tf_op jit(solution)/shard_map/pallas_call | solution.py:693
  1092.5 8.4 fusion.212
  1101.0 34.2 %shard_map.415 = (f32[128,1024]{1,0:T(8,128)}, f32[1,1024]{1,0:T(1,128)}) custom-call(bf16[4,128,3072]{2,1,0:T(8,128)(2,1)} %get-tuple-element.102.refs_0_, bf16[1024,3072]{1,0:T(8,128)(2,1)} %pad_maximum_fusion.2.refs_1_.refs_7_, f32[128,1024]{1,0:T(8,128)} %bitcast_convert_fusion.1.refs_5_.refs_2_, f32[128,1]{1,0:T(8,128)} %reshape.747.refs_3_, ...), custom_call_target="tpu_custom_call" | custom-call | flops 3221225472 | bytes 11018752 | tf_op jit(solution)/shard_map/pallas_call | solution.py:693
  1145.3 9.4 bitcast_add_fusion.2
  1154.7 9.3 bitcast_add_fusion.1
  1164.0 12.1 bitcast_add_fusion
  1228.1 11.0 collective-permute-done.74
  1240.4 9.6 collective-permute-done.68
  1253.1 6.1 collective-permute-done.67
  1273.4 11.1 collective-permute-done.90
  1288.0 6.2 collective-permute-done.89
  1307.6 15.3 %collective-permute-done.91 = bf16[2,1024,256]{2,1,0:T(8,128)(2,1)} collective-permute-done((bf16[2,1024,256]{2,1,0:T(8,128)(2,1)}, bf16[2,1024,256]{2,1,0:T(8,128)(2,1)}, u32[]{:S(2)}, u32[]{:S(2)}) %collective-permute-start.91) | collective-permute-done | bytes 1048608 | tf_op jit(solution)/shard_map/ppermute | solution.py:314
  1333.7 16.3 %collective-permute-done.92 = bf16[1024,256]{1,0:T(8,128)(2,1)S(1)} collective-permute-done((bf16[1024,256]{1,0:T(8,128)(2,1)S(1)}, bf16[1024,256]{1,0:T(8,128)(2,1)S(1)}, u32[]{:S(2)}, u32[]{:S(2)}) %collective-permute-start.92) | collective-permute-done | bytes 524320 | tf_op jit(solution)/shard_map/ppermute | solution.py:314
  1366.0 11.1 copy.410
  (917 shorter events, 507.4 us)
Async XLA Ops:
  7.2 345.4 %all-gather.5.cloned.1.call-start = ((), (), s32[]{:S(2)}) async-start(), calls=%async_computation.4 | async-start | bytes 1179648 | tf_op jit(solution)/shard_map/all_gather | solution.py:1250
  12.3 27.4 %collective-permute-start.11 = (f32[2,128]{1,0:T(2,128)}, f32[2,128]{1,0:T(2,128)}, u32[]{:S(2)}, u32[]{:S(2)}) collective-permute-start(f32[2,128]{1,0:T(2,128)} %get-tuple-element.473), channel_id=1, source_target_pairs={{0,16},{4,20},{8,24},{12,28},{16,0},{20,4},{24,8},{28,12},{1,17},{... | collective-permute-start | bytes 3080 | tf_op jit(solution)/shard_map/ppermute | solution.py:311
  25.2 39.8 %collective-permute-start.14 = (bf16[512,3072]{1,0:T(8,128)(2,1)}, bf16[512,3072]{1,0:T(8,128)(2,1)}, u32[]{:S(2)}, u32[]{:S(2)}) collective-permute-start(bf16[512,3072]{1,0:T(8,128)(2,1)} %pad_maximum_fusion.7), channel_id=1, source_target_pairs={{0,4},{4,0},{8,12},{12,8},{16,20},{20,16},{24,28},{28,24},{1,5},{5... | collective-permute-start | bytes 9437192 | tf_op jit(solution)/shard_map/ppermute | solution.py:308
  48.1 486.6 %all-gather.9.cloned.1.call-start = ((), (), s32[]{:S(2)}) async-start(), calls=%async_computation.6 | async-start | bytes 1769472 | tf_op jit(solution)/shard_map/all_gather | solution.py:1252
  140.7 441.3 %all-gather.11.cloned.1.call-start = ((), (), s32[]{:S(2)}) async-start(), calls=%async_computation.7 | async-start | bytes 4718592 | tf_op jit(solution)/shard_map/all_gather | solution.py:1259
  141.6 444.9 %all-gather.7.cloned.1.call-start = ((), (), s32[]{:S(2)}) async-start(), calls=%async_computation.5 | async-start | bytes 9437184 | tf_op jit(solution)/shard_map/all_gather | solution.py:1257
  144.5 32.3 %collective-permute-start = (bf16[1024,256]{1,0:T(8,128)(2,1)}, bf16[1024,256]{1,0:T(8,128)(2,1)}, u32[]{:S(2)}, u32[]{:S(2)}) collective-permute-start(bf16[1024,256]{1,0:T(8,128)(2,1)} %param.35), channel_id=1, source_target_pairs={{0,1},{1,0},{2,3},{3,2},{4,5},{5,4},{6,7},{7,6},{8,9},{9,8},{10,11... | collective-permute-start | bytes 1572872 | tf_op jit(solution)/shard_map/ppermute | solution.py:314
  146.1 41.4 %collective-permute-start.18 = (bf16[1024,512]{1,0:T(8,128)(2,1)}, bf16[1024,512]{1,0:T(8,128)(2,1)}, u32[]{:S(2)}, u32[]{:S(2)}) collective-permute-start(bf16[1024,512]{1,0:T(8,128)(2,1)} %param.28), channel_id=1, source_target_pairs={{0,4},{4,0},{8,12},{12,8},{16,20},{20,16},{24,28},{28,24},{1,5},{5... | collective-permute-start | bytes 3145736 | tf_op jit(solution)/shard_map/ppermute | solution.py:308
  146.1 77.6 %collective-permute-start.20 = (bf16[2048,512]{1,0:T(8,128)(2,1)}, bf16[2048,512]{1,0:T(8,128)(2,1)}, u32[]{:S(2)}, u32[]{:S(2)}) collective-permute-start(bf16[2048,512]{1,0:T(8,128)(2,1)} %param.34), channel_id=1, source_target_pairs={{0,4},{4,0},{8,12},{12,8},{16,20},{20,16},{24,28},{28,24},{1,5},{5... | collective-permute-start | bytes 6291464 | tf_op jit(solution)/shard_map/ppermute | solution.py:308
  161.2 168.0 %collective-permute-start.19 = (bf16[512,4224]{1,0:T(8,128)(2,1)}, bf16[512,4224]{1,0:T(8,128)(2,1)}, u32[]{:S(2)}, u32[]{:S(2)}) collective-permute-start(bf16[512,4224]{1,0:T(8,128)(2,1)} %pad_maximum_fusion.4), channel_id=1, source_target_pairs={{0,4},{4,0},{8,12},{12,8},{16,20},{20,16},{24,28},{28,24},{1,5},{5... | collective-permute-start | bytes 12976136 | tf_op jit(solution)/shard_map/ppermute | solution.py:308
  187.0 33.0 %collective-permute-start.4 = (bf16[1024,256]{1,0:T(8,128)(2,1)}, bf16[1024,256]{1,0:T(8,128)(2,1)}, u32[]{:S(2)}, u32[]{:S(2)}) collective-permute-start(bf16[1024,256]{1,0:T(8,128)(2,1)} %get-tuple-element.284), channel_id=1, source_target_pairs={{0,16},{4,20},{8,24},{12,28},{16,0},{20,4},{24,8},{28,12},{1,17},{... | collective-permute-start | bytes 1572872 | tf_op jit(solution)/shard_map/ppermute | solution.py:311
  187.5 32.5 %collective-permute-start.3 = (bf16[1024,256]{1,0:T(8,128)(2,1)}, bf16[1024,256]{1,0:T(8,128)(2,1)}, u32[]{:S(2)}, u32[]{:S(2)}) collective-permute-start(bf16[1024,256]{1,0:T(8,128)(2,1)} %get-tuple-element.285), channel_id=1, source_target_pairs={{0,8},{4,12},{8,0},{12,4},{16,24},{20,28},{24,16},{28,20},{1,9},{5... | collective-permute-start | bytes 1572872 | tf_op jit(solution)/shard_map/ppermute | solution.py:311
  190.1 1095.4 %reduce-scatter.5.cloned.1.call-start = ((), (), s32[]{:S(2)}) async-start(), calls=%async_computation.8 | async-start | bytes 1253376 | tf_op jit(solution)/shard_map/reduce_scatter | solution.py:1300
  223.7 316.7 %collective-permute-start.6 = (bf16[4,1024,256]{2,1,0:T(8,128)(2,1)}, bf16[4,1024,256]{2,1,0:T(8,128)(2,1)}, u32[]{:S(2)}, u32[]{:S(2)}) collective-permute-start(bf16[4,1024,256]{2,1,0:T(8,128)(2,1)} %get-tuple-element.281), channel_id=1, source_target_pairs={{0,4},{4,0},{8,12},{12,8},{16,20},{20,16},{24,28},{28,24},{1,5},{5... | collective-permute-start | bytes 6291464 | tf_op jit(solution)/shard_map/ppermute | solution.py:308
  445.1 76.1 %collective-permute-start.21 = (bf16[4,2,32,1024]{3,2,0,1:T(8,128)(2,1)}, bf16[4,2,32,1024]{3,2,0,1:T(8,128)(2,1)S(1)}, u32[]{:S(2)}, u32[]{:S(2)}) collective-permute-start(bf16[4,2,32,1024]{3,2,0,1:T(8,128)(2,1)} %bitcast.558), channel_id=1, source_target_pairs={{0,1},{1,0},{2,3},{3,2},{4,5},{5,4},{6,7},{7,6},{8,9},{9,8},{10,11... | collective-permute-start | bytes 1572872 | tf_op jit(solution)/shard_map/feed_out_micro0/ppermute | solution.py:314
  658.4 37.1 %collective-permute-start.52 = (bf16[32,2048]{1,0:T(8,128)(2,1)S(1)}, bf16[32,2048]{1,0:T(8,128)(2,1)}, u32[]{:S(2)}, u32[]{:S(2)}) collective-permute-start(bf16[32,2048]{1,0:T(8,128)(2,1)S(1)} %get-tuple-element.254), channel_id=1, source_target_pairs={{0,24},{4,28},{8,16},{12,20},{16,8},{20,12},{24,0},{28,4},{1,25},{... | collective-permute-start | bytes 393224 | tf_op jit(solution)/shard_map/settle_micro1/ppermute | solution.py:311
  659.9 34.0 %collective-permute-start.51 = (bf16[32,2048]{1,0:T(8,128)(2,1)S(1)}, bf16[32,2048]{1,0:T(8,128)(2,1)}, u32[]{:S(2)}, u32[]{:S(2)}) collective-permute-start(bf16[32,2048]{1,0:T(8,128)(2,1)S(1)} %get-tuple-element.254), channel_id=1, source_target_pairs={{0,16},{4,20},{8,24},{12,28},{16,0},{20,4},{24,8},{28,12},{1,17},{... | collective-permute-start | bytes 393224 | tf_op jit(solution)/shard_map/settle_micro1/ppermute | solution.py:311
  661.1 31.0 %collective-permute-start.50 = (bf16[32,2048]{1,0:T(8,128)(2,1)S(1)}, bf16[32,2048]{1,0:T(8,128)(2,1)}, u32[]{:S(2)}, u32[]{:S(2)}) collective-permute-start(bf16[32,2048]{1,0:T(8,128)(2,1)S(1)} %get-tuple-element.254), channel_id=1, source_target_pairs={{0,8},{4,12},{8,0},{12,4},{16,24},{20,28},{24,16},{28,20},{1,9},{5... | collective-permute-start | bytes 393224 | tf_op jit(solution)/shard_map/settle_micro1/ppermute | solution.py:311
  690.3 33.2 %collective-permute-start.61 = (bf16[4,32,1024]{2,1,0:T(8,128)(2,1)}, bf16[4,32,1024]{2,1,0:T(8,128)(2,1)}, u32[]{:S(2)}, u32[]{:S(2)}) collective-permute-start(bf16[4,32,1024]{2,1,0:T(8,128)(2,1)} %convert_element_type.637), channel_id=1, source_target_pairs={{0,1},{1,0},{2,3},{3,2},{4,5},{5,4},{6,7},{7,6},{8,9},{9,8},{10,11... | collective-permute-start | bytes 786440 | tf_op jit(solution)/shard_map/settle_micro0/ppermute | solution.py:314
  716.4 583.8 %reduce-scatter.7.cloned.1.call-start = ((), (), s32[]{:S(2)}) async-start(), calls=%async_computation.9 | async-start | bytes 1179648 | tf_op jit(solution)/shard_map/reduce_scatter | solution.py:1302
  720.1 69.6 %collective-permute-start.53 = (bf16[4,32,1024]{2,1,0:T(8,128)(2,1)}, bf16[4,32,1024]{2,1,0:T(8,128)(2,1)S(1)}, u32[]{:S(2)}, u32[]{:S(2)}) collective-permute-start(bf16[4,32,1024]{2,1,0:T(8,128)(2,1)} %convert_element_type.623), channel_id=1, source_target_pairs={{0,1},{1,0},{2,3},{3,2},{4,5},{5,4},{6,7},{7,6},{8,9},{9,8},{10,11... | collective-permute-start | bytes 786440 | tf_op jit(solution)/shard_map/settle_micro1/ppermute | solution.py:314
  721.7 68.0 %collective-permute-start.55 = (bf16[4,32,1024]{2,1,0:T(8,128)(2,1)}, bf16[4,32,1024]{2,1,0:T(8,128)(2,1)S(1)}, u32[]{:S(2)}, u32[]{:S(2)}) collective-permute-start(bf16[4,32,1024]{2,1,0:T(8,128)(2,1)} %collective-permute-done.54), channel_id=1, source_target_pairs={{0,1},{1,0},{2,3},{3,2},{4,5},{5,4},{6,7},{7,6},{8,9},{9,8},{10,11... | collective-permute-start | bytes 786440 | tf_op jit(solution)/shard_map/settle_micro1/ppermute | solution.py:314
  863.9 516.5 %reduce-scatter.11.cloned.1.call-start = ((), (), s32[]{:S(2)}) async-start(), calls=%async_computation.11 | async-start | bytes 4718592 | tf_op jit(solution)/shard_map/reduce_scatter | solution.py:1296
  869.6 513.3 %reduce-scatter.9.cloned.1.call-start = ((), (), s32[]{:S(2)}) async-start(), calls=%async_computation.10 | async-start | bytes 9437184 | tf_op jit(solution)/shard_map/reduce_scatter | solution.py:1294
  918.8 345.9 %collective-permute-start.87 = (bf16[1024,4,256]{2,0,1:T(8,128)(2,1)}, bf16[1024,4,256]{2,0,1:T(8,128)(2,1)}, u32[]{:S(2)}, u32[]{:S(2)}) collective-permute-start(bf16[1024,4,256]{2,0,1:T(8,128)(2,1)} %bitcast_convert_fusion), channel_id=1, source_target_pairs={{0,4},{4,0},{8,12},{12,8},{16,20},{20,16},{24,28},{28,24},{1,5},{5... | collective-permute-start | bytes 6291464 | tf_op jit(solution)/shard_map/ppermute | solution.py:308
  926.8 271.4 %collective-permute-start.46 = (bf16[2,32,2048]{2,1,0:T(8,128)(2,1)S(1)}, bf16[2,32,2048]{2,1,0:T(8,128)(2,1)}, u32[]{:S(2)}, u32[]{:S(2)}) collective-permute-start(bf16[2,32,2048]{2,1,0:T(8,128)(2,1)S(1)} %fusion.57), channel_id=1, source_target_pairs={{0,2},{1,3},{2,0},{3,1},{4,6},{5,7},{6,4},{7,5},{8,10},{9,11},{10,... | collective-permute-start | bytes 786440 | tf_op jit(solution)/shard_map/outputs/ppermute | solution.py:314
  1138.6 37.6 %collective-permute-start.78 = (f32[2,512]{1,0:T(2,128)S(1)}, f32[2,512]{1,0:T(2,128)S(1)}, u32[]{:S(2)}, u32[]{:S(2)}) collective-permute-start(f32[2,512]{1,0:T(2,128)S(1)} %slice.613), channel_id=1, source_target_pairs={{0,4},{4,0},{8,12},{12,8},{16,20},{20,16},{24,28},{28,24},{1,5},{5... | collective-permute-start | bytes 12296 | tf_op jit(solution)/shard_map/ppermute | solution.py:308
  1198.2 26.3 %collective-permute-start.45 = (bf16[2,32,2048]{2,1,0:T(8,128)(2,1)S(1)}, bf16[2,32,2048]{2,1,0:T(8,128)(2,1)S(1)}, u32[]{:S(2)}, u32[]{:S(2)}) collective-permute-start(bf16[2,32,2048]{2,1,0:T(8,128)(2,1)S(1)} %fusion.57), channel_id=1, source_target_pairs={{0,1},{1,0},{2,3},{3,2},{4,5},{5,4},{6,7},{7,6},{8,9},{9,8},{10,11... | collective-permute-start | bytes 786440 | tf_op jit(solution)/shard_map/outputs/ppermute | solution.py:314
  1198.2 28.3 %collective-permute-start.47 = (bf16[2,32,2048]{2,1,0:T(8,128)(2,1)}, bf16[2,32,2048]{2,1,0:T(8,128)(2,1)S(1)}, u32[]{:S(2)}, u32[]{:S(2)}) collective-permute-start(bf16[2,32,2048]{2,1,0:T(8,128)(2,1)} %collective-permute-done.46), channel_id=1, source_target_pairs={{0,1},{1,0},{2,3},{3,2},{4,5},{5,4},{6,7},{7,6},{8,9},{9,8},{10,11... | collective-permute-start | bytes 786440 | tf_op jit(solution)/shard_map/outputs/ppermute | solution.py:314
  1220.5 81.6 %collective-permute-start.86 = (bf16[2048,512]{1,0:T(8,128)(2,1)}, bf16[2048,512]{1,0:T(8,128)(2,1)}, u32[]{:S(2)}, u32[]{:S(2)}) collective-permute-start(bf16[2048,512]{1,0:T(8,128)(2,1)} %slice.843), channel_id=1, source_target_pairs={{0,4},{4,0},{8,12},{12,8},{16,20},{20,16},{24,28},{28,24},{1,5},{5... | collective-permute-start | bytes 6291464 | tf_op jit(solution)/shard_map/ppermute | solution.py:308
  1240.4 84.9 %collective-permute-start.76 = (bf16[512,3072]{1,0:T(8,128)(2,1)}, bf16[512,3072]{1,0:T(8,128)(2,1)}, u32[]{:S(2)}, u32[]{:S(2)}) collective-permute-start(bf16[512,3072]{1,0:T(8,128)(2,1)} %slice.842), channel_id=1, source_target_pairs={{0,4},{4,0},{8,12},{12,8},{16,20},{20,16},{24,28},{28,24},{1,5},{5... | collective-permute-start | bytes 9437192 | tf_op jit(solution)/shard_map/ppermute | solution.py:308
  1294.1 56.9 %collective-permute-start.82 = (bf16[512,4224]{1,0:T(8,128)(2,1)}, bf16[512,4224]{1,0:T(8,128)(2,1)}, u32[]{:S(2)}, u32[]{:S(2)}) collective-permute-start(bf16[512,4224]{1,0:T(8,128)(2,1)} %slice.841), channel_id=1, source_target_pairs={{0,4},{4,0},{8,12},{12,8},{16,20},{20,16},{24,28},{28,24},{1,5},{5... | collective-permute-start | bytes 12976136 | tf_op jit(solution)/shard_map/ppermute | solution.py:308
  (237 other events, 2851.9 us)
Sparse Core Ops, SparseCore 0:
  48.2 24.3 all-gather.4
  140.8 28.4 all-gather.8
  171.2 54.5 all-gather.10
  228.1 85.4 all-gather.6
  716.5 39.1 reduce-scatter.4
  864.1 35.8 reduce-scatter.6
  903.3 55.4 reduce-scatter.10
  962.6 95.3 reduce-scatter.8

commit v3 on v2

--- a/solution.py
+++ b/solution.py
@@ -398,6 +398,11 @@
                 blocks[rel | (1 << bit)] = self.z_swap(blocks[rel], 1 << bit)
         return jnp.stack([blocks[rel] for rel in range(self.n_t)], axis=axis)
 
+    def dp_order(self, x, axis):
+        split = x.reshape(x.shape[:axis] + (self.chips, 2, -1) + x.shape[axis + 1 :])
+        split = self.by_index(self.by_index(split, axis + 1, self.core), axis, self.chip)
+        return split.reshape(x.shape)
+
     def by_index(self, x, axis, own):
         count = x.shape[axis]
         return jnp.concatenate(
@@ -443,6 +448,26 @@
 
 def z_partner(rel):
     return {"tensor": flip(lax.axis_index("tensor"), rel)}
+
+
+def core_partner():
+    return {"dp": flip(lax.axis_index("dp"), 1)}
+
+
+def partner_of(axis, rel):
+    if axis == "core":
+        return core_partner()
+    return chip_partner(rel) if axis == "dp" else z_partner(rel)
+
+
+def xor(a, b):
+    return sum(((a // bit + b // bit) % 2) * bit for bit in (1, 2))
+
+
+def core_order(x):
+    half = x.shape[-1] // 2
+    turned = jnp.concatenate([x[..., half:], x[..., :half]], axis=-1)
+    return jnp.where(lax.axis_index("dp") % 2 == 1, turned, x)
 
 
 class Wire:
@@ -464,18 +489,90 @@
         return copy
 
 
-def tile_of(width):
-    return next(size for size in (384, 256, 128) if width % size == 0)
-
-
-def over_tiles(width, body):
-    tile = tile_of(width)
-
+TILE = 256
+
+
+def over_tiles(width, body, offset=0):
     def step(i, carry):
-        body(pl.ds(pl.multiple_of(i * tile, 128), tile))
+        at = pl.ds(pl.multiple_of(i * TILE, 128), TILE)
+        body(at, pl.ds(pl.multiple_of(offset + i * TILE, 128), TILE))
         return carry
 
-    lax.fori_loop(0, width // tile, step, 0)
+    count = width // TILE
+    lax.fori_loop(0, count, step, 0)
+    if width % TILE:
+        low, left = count * TILE, width % TILE
+        body(pl.ds(low, left), pl.ds(offset + low, left))
+
+
+class RowPair:
+    def __init__(self, own, other):
+        self.args = (own, other)
+        self.parts = own.shape[0] if own.ndim == 3 else 1
+        self.half, self.cols = own.shape[-2:]
+        self.shape = (2 * self.half, self.parts * self.cols)
+
+    def whole(self):
+        both = jnp.concatenate(self.args, axis=-2)
+        return both if both.ndim == 2 else jnp.concatenate(list(both), axis=1)
+
+    def pick(self, ref, part):
+        return ref if self.parts == 1 else ref.at[part]
+
+    def times(self, x, refs, by_cols, store):
+        half, cols = self.half, self.cols
+        if by_cols:
+            for h, ref in enumerate(refs):
+
+                def body(at, to, ref=ref):
+                    store(
+                        to,
+                        total(
+                            [
+                                fast(x(slice(i * cols, i * cols + cols)), self.pick(ref, i)[at, :], BY_COLS)
+                                for i in range(self.parts)
+                            ]
+                        ),
+                    )
+
+                over_tiles(half, body, h * half)
+            return
+        for i in range(self.parts):
+
+            def body(at, to, i=i):
+                own, other = (self.pick(ref, i)[:, at] for ref in refs)
+                left, right = x(slice(0, half)), x(slice(half, 2 * half))
+                store(to, fast(left, own, PLAIN) + fast(right, other, PLAIN))
+
+            over_tiles(cols, body, i * cols)
+
+
+class ColPair:
+    def __init__(self, own, other):
+        self.args = (own, other)
+        self.rows, self.half = own.shape
+        self.shape = (self.rows, 2 * self.half)
+
+    def whole(self):
+        return jnp.concatenate(self.args, axis=1)
+
+    def times(self, x, refs, by_cols, store):
+        half = self.half
+        if by_cols:
+            own, other = refs
+
+            def body(at, to):
+                left, right = x(slice(0, half)), x(slice(half, 2 * half))
+                store(to, fast(left, own[at, :], BY_COLS) + fast(right, other[at, :], BY_COLS))
+
+            over_tiles(self.rows, body)
+            return
+        for h, ref in enumerate(refs):
+
+            def body(at, to, ref=ref):
+                store(to, fast(x(slice(0, self.rows)), ref[:, at], PLAIN))
+
+            over_tiles(half, body, h * half)
 
 
 class ByChips:
@@ -486,84 +583,216 @@
         self.by_cols, self.local, self.count = by_cols, local, len(args)
         self.rows = x.shape[1]
         self.width = w.shape[0] if by_cols else w.shape[1]
-        self.args = (x, w) + tuple(args)
+        self.w = w
+        self.args = (x,) + w.args + tuple(args)
         self.outs = (jax.ShapeDtypeStruct((4, self.rows, out_width), BF16),) + tuple(outs)
-        half = self.rows // 2
-        self.scratch = [
-            pltpu.VMEM((4, self.rows, self.width), BF16),
-            pltpu.VMEM((2, 2, half, self.width), BF16),
-            pltpu.VMEM((2, half, self.width), BF16),
-            pltpu.VMEM((self.rows, self.width), F32),
-        ] + list(scratch)
+        self.scratch = chip_scratch(self.rows, self.width)
+        self.scratch += [pltpu.VMEM((self.rows, self.width), F32)] + list(scratch)
         self.flops = 8 * self.rows * x.shape[2] * self.width
 
     def run(self, wire, args, outs, scratch):
-        x, w = args[:2]
+        x, w = args[0], args[1:3]
         part, first, second, summed = scratch[:4]
         gathered = outs[0]
-        rows, depth, half = self.rows, x.shape[2], self.rows // 2
-        dims = BY_COLS if self.by_cols else PLAIN
+        rows = self.rows
 
         def dot(low, high):
-            def body(cols):
-                tile = w[cols, :] if self.by_cols else w[:, cols]
-                left = x[low:high].reshape((high - low) * rows, depth)
-                part[low:high, :, cols] = fast(left, tile, dims).astype(BF16).reshape(
-                    high - low, rows, tile_of(self.width)
-                )
-
-            over_tiles(self.width, body)
-
-        def piece(p):
-            return slice(p * half, (p + 1) * half), 1 << p, 1 << (1 - p)
+            def left(at):
+                return x[low:high, :, at].reshape((high - low) * rows, at.stop - at.start)
+
+            def store(to, value):
+                part[low:high, :, to] = value.astype(BF16).reshape(high - low, rows, value.shape[1])
+
+            self.w.times(left, w, self.by_cols, store)
 
         dot(1, 4)
-        sent = []
-        for p in range(2):
-            at, bit, _ = piece(p)
-            for i, rel in enumerate((bit, 3)):
-                sent.append(wire.start(part.at[rel, at], first.at[p, i], chip_partner(bit)))
-        dot(0, 1)
+        yield from chip_sum(wire, part, first, second, summed, lambda: dot(0, 1))
+        self.local(summed, gathered.at[0], args[3:], outs[1:], scratch[4:])
+        yield from chip_gather(wire, [gathered.at[rel] for rel in range(4)], rows)
+
+
+def pieces(rows):
+    half = rows // 2
+    return [(p, slice(p * half, (p + 1) * half), 1 << p, 1 << (1 - p)) for p in range(2)]
+
+
+def chip_sum(wire, part, first, second, summed, meanwhile=None):
+    rows, width = summed.shape
+    sent, later = [], []
+    for p, at, bit, _ in pieces(rows):
+        for i, rel in enumerate((bit, 3)):
+            sent.append(wire.start(part.at[rel, at], first.at[p, i], chip_partner(bit)))
+    if meanwhile:
+        meanwhile()
+    yield
+    for p, at, _, other in pieces(rows):
+        sent[2 * p + 1].wait_recv()
+
+        def add(cols, _, p=p, at=at, other=other):
+            both = part[other, at, cols].astype(F32) + first[p, 1, :, cols].astype(F32)
+            part[other, at, cols] = both.astype(BF16)
+
+        over_tiles(width, add)
+        later.append(wire.start(part.at[other, at], second.at[p], chip_partner(other)))
+    yield
+    for p, at, _, _ in pieces(rows):
+        sent[2 * p].wait_recv()
+        later[p].wait_recv()
+
+        def finish(cols, _, p=p, at=at):
+            both = part[0, at, cols].astype(F32) + first[p, 0, :, cols].astype(F32)
+            summed[at, cols] = both + second[p, :, cols].astype(F32)
+
+        over_tiles(width, finish)
+    for copy in sent + later:
+        copy.wait_send()
+
+
+def chip_gather(wire, slots, rows):
+    near, far, last = [], [], []
+    for _, at, bit, other in pieces(rows):
+        near.append(wire.start(slots[0].at[at], slots[bit].at[at], chip_partner(bit)))
+        far.append(wire.start(slots[0].at[at], slots[other].at[at], chip_partner(other)))
+    yield
+    for p, at, bit, other in pieces(rows):
+        near[p].wait_recv()
+        last.append(wire.start(slots[bit].at[at], slots[3].at[at], chip_partner(other)))
+    yield
+    for copy in far + last:
+        copy.wait_recv()
+    for copy in near + far + last:
+        copy.wait_send()
+
+
+def chip_scratch(rows, width):
+    half = rows // 2
+    return [
+        pltpu.VMEM((4, rows, width), BF16),
+        pltpu.VMEM((2, 2, half, width), BF16),
+        pltpu.VMEM((2, half, width), BF16),
+    ]
+
+
+class GatherDp:
+    partners = [("dp", 1), ("dp", 2), ("core", 1)]
+    copies = 7
+    flops = 0
+
+    def __init__(self, x):
+        self.args, self.rows = (x,), x.shape[0]
+        self.outs = (jax.ShapeDtypeStruct((4, 2) + x.shape, BF16),)
+        self.scratch = []
+
+    def run(self, wire, args, outs, scratch):
+        (out,) = outs
+        out[0, 0] = args[0][...]
+        yield from chip_gather(wire, [out.at[rel, 0] for rel in range(4)], self.rows)
+        swap = wire.start(out.at[:, 0], out.at[:, 1], core_partner())
         yield
-        later = []
-        for p in range(2):
-            at, _, other = piece(p)
-            sent[2 * p + 1].wait_recv()
-
-            def add(cols, p=p, at=at, other=other):
-                both = part[other, at, cols].astype(F32) + first[p, 1, :, cols].astype(F32)
-                part[other, at, cols] = both.astype(BF16)
-
-            over_tiles(self.width, add)
-            later.append(wire.start(part.at[other, at], second.at[p], chip_partner(other)))
+        swap.wait_recv()
+        swap.wait_send()
+
+
+class ScatterDp:
+    partners = GatherDp.partners
+    copies = 7
+    flops = 0
+
+    def __init__(self, own, other):
+        self.args = (own, other)
+        shape = own.shape[1:]
+        self.outs = (jax.ShapeDtypeStruct(shape, F32),)
+        self.scratch = [pltpu.VMEM(own.shape, BF16)] + chip_scratch(*shape)
+
+    def run(self, wire, args, outs, scratch):
+        own, other = args
+        swapped, part, first, second = scratch
+        swap = wire.start(other, swapped, core_partner())
         yield
-        for p in range(2):
-            at, _, _ = piece(p)
-            sent[2 * p].wait_recv()
-            later[p].wait_recv()
-
-            def finish(cols, p=p, at=at):
-                both = part[0, at, cols].astype(F32) + first[p, 0, :, cols].astype(F32)
-                summed[at, cols] = both + second[p, :, cols].astype(F32)
-
-            over_tiles(self.width, finish)
-        self.local(summed, gathered.at[0], args[2:], outs[1:], scratch[4:])
-        near, far = [], []
-        for p in range(2):
-            at, bit, other = piece(p)
-            near.append(wire.start(gathered.at[0, at], gathered.at[bit, at], chip_partner(bit)))
-            far.append(wire.start(gathered.at[0, at], gathered.at[other, at], chip_partner(other)))
-        yield
-        last = []
-        for p in range(2):
-            at, bit, other = piece(p)
-            near[p].wait_recv()
-            last.append(wire.start(gathered.at[bit, at], gathered.at[3, at], chip_partner(other)))
-        yield
-        for copy in far + last:
-            copy.wait_recv()
-        for copy in sent + later + near + far + last:
-            copy.wait_send()
+        swap.wait_recv()
+        for rel in range(4):
+
+            def add(cols, _, rel=rel):
+                both = own[rel, :, cols].astype(F32) + swapped[rel, :, cols].astype(F32)
+                part[rel, :, cols] = both.astype(BF16)
+
+            over_tiles(own.shape[2], add)
+        yield from chip_sum(wire, part, first, second, outs[0])
+        swap.wait_send()
+
+
+def tensor_sum(weight, x, w, by_cols, wire, scratch):
+    part, first, second, summed = scratch
+    rows, width = summed.shape
+    r = rows // 4
+
+    def left(at):
+        return x[:, :, at].reshape(4 * rows, at.stop - at.start)
+
+    def store(to, value):
+        low = value.astype(BF16)
+        for c in range(4):
+            for z in range(4):
+                part[z, c * r : (c + 1) * r, to] = low[c * rows + z * r : c * rows + z * r + r]
+
+    weight.times(left, w, by_cols, store)
+    half = width // 2
+    halves = [slice(h * half, (h + 1) * half) for h in range(2)]
+    sent, later = [], []
+    for h in halves:
+        for i, z in ((1, 3), (0, 1)):
+            sent.append(wire.start(part.at[z, :, h], first.at[i, :, h], z_partner(1)))
+    yield
+    for n, h in enumerate(halves):
+        sent[2 * n].wait_recv()
+
+        def add(_, cols):
+            both = part[2, :, cols].astype(F32) + first[1, :, cols].astype(F32)
+            part[2, :, cols] = both.astype(BF16)
+
+        over_tiles(half, add, n * half)
+        later.append(wire.start(part.at[2, :, h], second.at[:, h], z_partner(2)))
+    yield
+    for n in range(2):
+        sent[2 * n + 1].wait_recv()
+        later[n].wait_recv()
+
+        def finish(_, cols):
+            both = part[0, :, cols].astype(F32) + first[0, :, cols].astype(F32)
+            summed[:, cols] = both + second[:, cols].astype(F32)
+
+        over_tiles(half, finish, n * half)
+    for copy in sent + later:
+        copy.wait_send()
+
+
+def sum_scratch(rows, width):
+    return [
+        pltpu.VMEM((4, rows, width), BF16),
+        pltpu.VMEM((2, rows, width), BF16),
+        pltpu.VMEM((rows, width), BF16),
+        pltpu.VMEM((rows, width), F32),
+    ]
+
+
+def true_slots(ref):
+    t = lax.axis_index("tensor")
+    own = [ref.at[xor(t, rel)] for rel in range(4)]
+    return own, [None, own[0], own[0], own[2]]
+
+
+def tensor_gather(wire, slots, there=None):
+    there = there or slots
+    far = wire.start(slots[0], there[2], z_partner(2))
+    near = wire.start(slots[0], there[1], z_partner(1))
+    yield
+    far.wait_recv()
+    last = wire.start(slots[2], there[3], z_partner(1))
+    yield
+    near.wait_recv()
+    last.wait_recv()
+    for copy in (far, near, last):
+        copy.wait_send()
 
 
 class ByTensor:
@@ -574,56 +803,23 @@
         self.by_cols, self.local, self.gather = by_cols, local, gather
         self.rows = x.shape[1]
         self.width = w.shape[0] if by_cols else w.shape[1]
-        self.args = (x, w) + tuple(args)
+        self.w = w
+        self.args = (x,) + w.args + tuple(args)
         shape = (4, 4, self.rows // 4, self.width)
         self.outs = (jax.ShapeDtypeStruct(shape, BF16),) if gather else ()
         self.outs += tuple(outs)
-        self.copies = 9 if gather else 6
-        self.scratch = [
-            pltpu.VMEM((4, self.rows, self.width), BF16),
-            pltpu.VMEM((2, self.rows, self.width), BF16),
-            pltpu.VMEM((self.rows, self.width), BF16),
-            pltpu.VMEM((self.rows, self.width), F32),
-            pltpu.VMEM((4, self.rows, 128), F32),
-        ]
+        self.copies = 12 if gather else 9
+        self.scratch = sum_scratch(self.rows, self.width)
+        self.scratch += [pltpu.VMEM((4, self.rows, 128), F32)]
         self.flops = 8 * self.rows * x.shape[2] * self.width
 
     def run(self, wire, args, outs, scratch):
-        x, w = args[:2]
-        part, first, second, summed, stats = scratch
-        rows, depth = self.rows, x.shape[2]
+        summed, stats = scratch[3:5]
+        rows = self.rows
         r = rows // 4
-        dims = BY_COLS if self.by_cols else PLAIN
-
-        def body(cols):
-            tile = w[cols, :] if self.by_cols else w[:, cols]
-            low = fast(x[...].reshape(4 * rows, depth), tile, dims).astype(BF16)
-            for c in range(4):
-                for z in range(4):
-                    part[z, c * r : (c + 1) * r, cols] = low[c * rows + z * r : c * rows + z * r + r]
-
-        over_tiles(self.width, body)
-        sent = [wire.start(part.at[z], first.at[i], z_partner(1)) for i, z in enumerate((1, 3))]
-        yield
-        sent[1].wait_recv()
-
-        def add(cols):
-            both = part[2, :, cols].astype(F32) + first[1, :, cols].astype(F32)
-            part[2, :, cols] = both.astype(BF16)
-
-        over_tiles(self.width, add)
-        later = wire.start(part.at[2], second, z_partner(2))
-        yield
-        sent[0].wait_recv()
-        later.wait_recv()
-
-        def finish(cols):
-            both = part[0, :, cols].astype(F32) + first[0, :, cols].astype(F32)
-            summed[:, cols] = both + second[:, cols].astype(F32)
-
-        over_tiles(self.width, finish)
-        rest = outs[1:] if self.gather else outs
-        local = self.local(summed, args[2:], rest)
+        yield from tensor_sum(self.w, args[0], args[1:3], self.by_cols, wire, scratch[:4])
+        rest = outs[1:] if self.gather else outs[:1]
+        local = self.local(summed, args[3:7], rest)
         stats[0] = jnp.broadcast_to(next(local), (rows, 128))
         sums = [
             wire.start(stats.at[0], stats.at[rel], chip_partner(rel)) for rel in range(1, 4)
@@ -647,9 +843,418 @@
             yield
             near.wait_recv()
             last.wait_recv()
-            sent += [far, near, last]
-        for copy in sent + [later] + sums:
+            sums += [far, near, last]
+        else:
+            yield from self.tail(wire, low, args, outs, scratch)
+        for copy in sums:
             copy.wait_send()
+
+
+class Leave(ByTensor):
+    def __init__(self, x, w, local, args, d_gain, theirs):
+        super().__init__(x, w, True, local, args, (d_gain,), gather=False)
+        r = self.rows // 4
+        self.args += (theirs,)
+        self.outs += (jax.ShapeDtypeStruct((4, r, 4 * self.width), BF16),)
+        self.copies = 15
+        self.scratch += [pltpu.VMEM((4, r, self.width), BF16)] * 2
+        self.scratch += [pltpu.VMEM((r, 4 * self.width), BF16)]
+
+    def tail(self, wire, low, args, outs, scratch):
+        theirs, out = args[-1], outs[-1]
+        mine, came, block_ref = scratch[5:]
+        r, width = self.rows // 4, self.width
+        half = width // 2
+        d, t = lax.axis_index("dp"), lax.axis_index("tensor")
+        for c in range(4):
+            mine[c] = low[c * r : (c + 1) * r]
+        sent = [
+            wire.start(mine.at[rel], came.at[rel], chip_partner(rel)) for rel in range(1, 4)
+        ]
+        yield
+        for rel in range(4):
+            if rel:
+                sent[rel - 1].wait_recv()
+            block = (came if rel else mine)[rel].astype(F32)
+            for j in range(2):
+                at = 2 * xor(d // 2, rel) + (d + j) % 2
+                at = pl.ds(pl.multiple_of(at * half, 128), half)
+                low = block[:, j * half : (j + 1) * half] + theirs[:, at]
+                block_ref[:, at] = low.astype(BF16)
+        out[t] = block_ref[...]
+        yield from tensor_gather(wire, *true_slots(out))
+        for copy in sent:
+            copy.wait_send()
+
+
+class FeedOut:
+    partners = [("tensor", 1), ("tensor", 2), ("dp", 1), ("dp", 2), ("dp", 3)]
+    copies = 12
+
+    def __init__(self, x, w, mid, proj):
+        self.w = w
+        self.rows, self.width = x.shape[1], w.shape[1]
+        self.cols = proj.shape[3]
+        r = self.rows // 4
+        self.args = (x,) + w.args + (mid, proj)
+        wide = 8 * self.cols
+        self.outs = (
+            jax.ShapeDtypeStruct((self.rows, self.width), BF16),
+            jax.ShapeDtypeStruct((4, r, wide), BF16),
+            jax.ShapeDtypeStruct((r, wide), BF16),
+        )
+        self.scratch = sum_scratch(self.rows, self.width)
+        self.scratch += [pltpu.VMEM((4, r, wide), BF16)] * 2
+        self.flops = 8 * self.rows * x.shape[2] * self.width
+
+    def run(self, wire, args, outs, scratch):
+        mid, proj = args[3:]
+        block, gathered, own = outs
+        summed, part, came = scratch[3:]
+        r = self.rows // 4
+        d = lax.axis_index("dp")
+        yield from tensor_sum(self.w, args[0], args[1:3], False, wire, scratch[:4])
+        block[...] = core_order((mid[...] + summed[...]).astype(BF16))
+        for x in range(4):
+            for y in range(2):
+                at = 2 * xor(d // 2, x) + (d + y) % 2
+                at = pl.ds(pl.multiple_of(at * self.cols, 128), self.cols)
+                value = fast(block[...], proj[x, y], PLAIN).astype(BF16)
+                part[:, :, at] = value.reshape(4, r, self.cols)
+        sent = [
+            wire.start(part.at[rel], came.at[rel], chip_partner(rel)) for rel in range(1, 4)
+        ]
+        yield
+        shared = part[0].astype(F32)
+        for rel in range(1, 4):
+            sent[rel - 1].wait_recv()
+            shared = shared + came[rel].astype(F32)
+        own[...] = shared.astype(BF16)
+        gathered[lax.axis_index("tensor")] = own[...]
+        yield from tensor_gather(wire, *true_slots(gathered))
+        for copy in sent:
+            copy.wait_send()
+
+
+class Settle:
+    partners = [("tensor", 1), ("tensor", 2), ("dp", 1), ("dp", 2), ("dp", 3)]
+    copies = 9
+
+    def __init__(self, terms, bc, mamba_in, gain, grad, proj):
+        self.args = (terms, bc, mamba_in, gain, grad, proj)
+        r, wide = mamba_in.shape
+        self.r, self.wide, self.cols = r, wide, proj.shape[3]
+        states, width = terms.shape[2] - wide, proj.shape[2]
+        self.outs = (
+            jax.ShapeDtypeStruct((4, 4, r, width), BF16),
+            jax.ShapeDtypeStruct((4, r, wide), BF16),
+            jax.ShapeDtypeStruct((r, wide), F32),
+            jax.ShapeDtypeStruct((r, states), BF16),
+            jax.ShapeDtypeStruct((4 * r, width), F32),
+            jax.ShapeDtypeStruct((1, wide), F32),
+        )
+        self.scratch = [
+            pltpu.VMEM((2, r, terms.shape[2]), BF16),
+            pltpu.VMEM((r, terms.shape[2]), BF16),
+            pltpu.VMEM((r, terms.shape[2]), BF16),
+        ]
+        self.flops = 16 * r * wide * width
+
+    def run(self, wire, args, outs, scratch):
+        terms, bc, mamba_in, gain, grad, proj = args
+        gathered, shared, d_mamba, state, d_block, d_gain = outs
+        first, middle, second = scratch
+        wide = self.wide
+        d = lax.axis_index("dp")
+        sent = [wire.start(terms.at[z], first.at[i], z_partner(1)) for i, z in enumerate((1, 3))]
+        yield
+        sent[1].wait_recv()
+        middle[...] = (terms[2].astype(F32) + first[1].astype(F32)).astype(BF16)
+        sent.append(wire.start(middle, second, z_partner(2)))
+        yield
+        sent[0].wait_recv()
+        sent[2].wait_recv()
+        summed = terms[0].astype(F32) + first[0].astype(F32) + second[...].astype(F32)
+        state[...] = summed[:, wide:].astype(BF16)
+        dy = summed[:, :wide] + fast(state[...], bc[...], BY_COLS)
+        v = mamba_in[...]
+        inv = lax.rsqrt(jnp.mean(v * v, axis=1, keepdims=True) + EPSILON)
+        scaled = dy * gain[...]
+        inner = jnp.mean(scaled * v, axis=1, keepdims=True)
+        d_gain[...] = jnp.sum(dy * v * inv, axis=0, keepdims=True)
+        d_mamba[...] = inv * scaled - v * (inv * inv * inv * inner) + grad[...].astype(F32)
+        shared[0] = d_mamba[...].astype(BF16)
+        more = [
+            wire.start(shared.at[0], shared.at[rel], chip_partner(rel)) for rel in range(1, 4)
+        ]
+        yield
+        for copy in more:
+            copy.wait_recv()
+        result = None
+        for x in range(4):
+            for y in range(2):
+                at = 2 * xor(d // 2, x) + (d + y) % 2
+                at = pl.ds(pl.multiple_of(at * self.cols, 128), self.cols)
+                left = shared[:, :, at].reshape(4 * self.r, self.cols)
+                value = fast(left, proj[x, y], BY_COLS)
+                result = value if result is None else result + value
+        d_block[...] = core_order(result)
+        for c in range(4):
+            gathered[c, 0] = d_block[c * self.r : (c + 1) * self.r].astype(BF16)
+        yield from tensor_gather(wire, [gathered.at[:, i] for i in range(4)])
+        for copy in sent + more:
+            copy.wait_send()
+
+
+class Spread:
+    partners = [("tensor", 1), ("tensor", 2), ("dp", 1), ("dp", 2), ("dp", 3), ("core", 1)]
+    copies = 7
+    flops = 0
+
+    def __init__(self, w):
+        self.args = (w,)
+        self.outs = (jax.ShapeDtypeStruct((4, 2) + w.shape, BF16),)
+        self.scratch = [pltpu.VMEM((4,) + w.shape, BF16)]
+
+    def run(self, wire, args, outs, scratch):
+        (out,), (rows,) = outs, scratch
+        rows[0] = args[0][...]
+        yield from tensor_gather(wire, [rows.at[i] for i in range(4)])
+        here = xor(lax.axis_index("dp") // 2, lax.axis_index("tensor"))
+        sent = [
+            wire.start(rows.at[xor(here, rel)], out.at[rel, 0], chip_partner(rel))
+            for rel in range(1, 4)
+        ]
+        out[0, 0] = rows[here]
+        yield
+        for copy in sent:
+            copy.wait_recv()
+        sent.append(wire.start(out.at[:, 0], out.at[:, 1], core_partner()))
+        yield
+        sent[3].wait_recv()
+        for copy in sent:
+            copy.wait_send()
+
+
+class Collect:
+    partners = Spread.partners
+    copies = 7
+    flops = 0
+
+    def __init__(self, own, other):
+        self.args = (own, other)
+        shape = own.shape[1:]
+        self.outs = (jax.ShapeDtypeStruct(shape, F32),)
+        self.scratch = [pltpu.VMEM((4,) + shape, BF16)] * 3
+        self.scratch += [pltpu.VMEM((2,) + shape, BF16), pltpu.VMEM(shape, BF16)]
+
+    def run(self, wire, args, outs, scratch):
+        own, other = args
+        (out,) = outs
+        swapped, mine, came, first, second = scratch
+        rows = own.shape[1]
+        tile = 128
+        sent = [wire.start(other, swapped, core_partner())]
+        yield
+        sent[0].wait_recv()
+        for rel in range(4):
+
+            def add(i, carry, rel=rel):
+                at = pl.ds(pl.multiple_of(i * tile, tile), tile)
+                both = own[rel, at, :] + swapped[rel, at, :].astype(F32)
+                (mine if rel else came)[rel, at, :] = both.astype(BF16)
+                return carry
+
+            lax.fori_loop(0, rows // tile, add, 0)
+            if rel:
+                sent.append(wire.start(mine.at[rel], came.at[rel], chip_partner(rel)))
+        yield
+        for copy in sent[1:]:
+            copy.wait_recv()
+        here = xor(lax.axis_index("dp") // 2, lax.axis_index("tensor"))
+        at = [xor(here, z) for z in range(4)]
+        more = [wire.start(came.at[at[z]], first.at[i], z_partner(1)) for i, z in enumerate((1, 3))]
+        yield
+        more[1].wait_recv()
+
+        def middle(i, carry):
+            to = pl.ds(pl.multiple_of(i * tile, tile), tile)
+            both = came[at[2], to, :].astype(F32) + first[1, to, :].astype(F32)
+            swapped[0, to, :] = both.astype(BF16)
+            return carry
+
+        lax.fori_loop(0, rows // tile, middle, 0)
+        more.append(wire.start(swapped.at[0], second, z_partner(2)))
+        yield
+        more[0].wait_recv()
+        more[2].wait_recv()
+
+        def finish(i, carry):
+            to = pl.ds(pl.multiple_of(i * tile, tile), tile)
+            both = came[at[0], to, :].astype(F32) + first[0, to, :].astype(F32)
+            out[to, :] = both + second[to, :].astype(F32)
+            return carry
+
+        lax.fori_loop(0, rows // tile, finish, 0)
+        for copy in sent + more:
+            copy.wait_send()
+
+
+class Outputs:
+    partners = [("tensor", 1), ("tensor", 2)]
+    copies = 6
+    flops = 0
+
+    def __init__(self, terms, base, valid):
+        self.args = (terms, base, valid)
+        self.outs = (jax.ShapeDtypeStruct(terms.shape, BF16),)
+        shape = terms.shape[1:]
+        self.scratch = [pltpu.VMEM((2,) + shape, BF16), pltpu.VMEM(shape, BF16)]
+        self.scratch += [pltpu.VMEM(shape, BF16)]
+
+    def run(self, wire, args, outs, scratch):
+        terms, base, valid = args
+        (gathered,) = outs
+        first, middle, second = scratch
+        sent = [wire.start(terms.at[z], first.at[i], z_partner(1)) for i, z in enumerate((1, 3))]
+        yield
+        sent[1].wait_recv()
+        middle[...] = (terms[2].astype(F32) + first[1].astype(F32)).astype(BF16)
+        sent.append(wire.start(middle, second, z_partner(2)))
+        yield
+        sent[0].wait_recv()
+        sent[2].wait_recv()
+        summed = terms[0].astype(F32) + first[0].astype(F32) + second[...].astype(F32)
+        gathered[lax.axis_index("tensor")] = ((base[...] + summed) * valid[...]).astype(BF16)
+        yield from tensor_gather(wire, *true_slots(gathered))
+        for copy in sent:
+            copy.wait_send()
+
+
+class Enter:
+    partners = [("dp", 1), ("dp", 2), ("dp", 3)]
+    copies = 9
+    flops = 0
+
+    def __init__(self, hid, emb, gain):
+        self.args = (hid, emb, gain)
+        self.rows, self.half = hid.shape[0], gain.shape[1] // 2
+        rows, width = self.rows, gain.shape[1]
+        self.outs = (
+            jax.ShapeDtypeStruct((4, rows, width), BF16),
+            jax.ShapeDtypeStruct((rows, width), F32),
+            jax.ShapeDtypeStruct((rows, 1), F32),
+        )
+        self.scratch = [
+            pltpu.VMEM((rows, 4 * width), BF16),
+            pltpu.VMEM((4, rows, width), BF16),
+            pltpu.VMEM((4, rows, 128), F32),
+        ]
+
+    def run(self, wire, args, outs, scratch):
+        hid, emb, gain = args
+        attn_in, joined_z, inv_z = outs
+        joined, came, stats = scratch
+        rows, half = self.rows, self.half
+        r, wide = rows // 4, hid.shape[1]
+        d, t = lax.axis_index("dp"), lax.axis_index("tensor")
+        for i in range(4):
+            at = pl.ds(pl.multiple_of(xor(t, i) * r, r), r)
+            to = slice(i * r, (i + 1) * r)
+            left, right = hid[at, :], emb[at, :]
+            joined[to, :wide] = left
+            joined[to, wide:] = right
+            left, right = left.astype(F32), right.astype(F32)
+            squares = jnp.sum(left * left, axis=1, keepdims=True)
+            squares = squares + jnp.sum(right * right, axis=1, keepdims=True)
+            inverse = lax.rsqrt(squares / (2 * wide) + EPSILON)
+            stats[0, to, :] = jnp.broadcast_to(inverse, (r, 128))
+        sent = []
+        for rel in (3, 1, 2):
+            sent.append(wire.start(stats.at[0], stats.at[rel], chip_partner(rel)))
+        for rel in (3, 1, 2, 0):
+            for j in range(2):
+                at = 2 * xor(d // 2, rel) + (d + j) % 2
+                at = pl.ds(pl.multiple_of(at * half, 128), half)
+                to = slice(j * half, (j + 1) * half)
+                if rel:
+                    src, dst = joined.at[:, at], came.at[rel, :, to]
+                    sent.append(wire.start(src, dst, chip_partner(rel)))
+                else:
+                    came[0, :, to] = joined[:, at]
+        yield
+        for copy in sent:
+            copy.wait_recv()
+        for c in range(4):
+            block = came[c].astype(F32)
+            inverse = stats[c][:, 0:1]
+            attn_in[c] = (block * inverse * gain[...]).astype(BF16)
+            joined_z[c * r : (c + 1) * r] = block[:r]
+            inv_z[c * r : (c + 1) * r] = inverse[:r]
+        for copy in sent:
+            copy.wait_send()
+
+
+class WeightGrad:
+    partners = [("core", 1)]
+    copies = 1
+
+    def __init__(self, a, b, by_rows, parts=1):
+        self.count, self.by_rows, self.parts = len(a), by_rows, parts
+        self.args = tuple(a) + tuple(b)
+        self.height, self.width = a[0].shape[2], b[0].shape[2]
+        if by_rows:
+            self.height //= 2
+        else:
+            self.width //= 2
+        self.cols = self.width // parts
+        shape = (self.height, self.cols)
+        shape = (parts,) + shape if parts > 1 else shape
+        self.outs = (jax.ShapeDtypeStruct(shape, F32),)
+        self.step = min(self.height, 512)
+        self.scratch = [pltpu.VMEM(shape, BF16)] * 2
+        self.scratch += [pltpu.VMEM((self.count, self.step, 4 * a[0].shape[1]), BF16)]
+        self.flops = 4 * self.count * a[0].shape[1] * self.height * self.width * 2
+
+    def run(self, wire, args, outs, scratch):
+        (out,) = outs
+        other, got, turned = scratch
+        a, b = args[: self.count], args[self.count :]
+        step = self.step
+        tokens = 4 * a[0].shape[1]
+
+        def work(half, ref):
+            row, col = (half * self.height, 0) if self.by_rows else (0, half * self.width)
+            for low in range(0, self.height, step):
+                rows = slice(row + low, row + low + step)
+                for i, x in enumerate(a):
+                    turned[i] = x[:, :, rows].reshape(tokens, step).T
+                for part in range(self.parts):
+                    to_ref = ref if self.parts == 1 else ref.at[part]
+
+                    def body(to, at, low=low, to_ref=to_ref):
+                        terms = [
+                            fast(turned[i], y[:, :, at].reshape(tokens, at.size), PLAIN)
+                            for i, y in enumerate(b)
+                        ]
+                        to_ref[low : low + step, to] = total(terms).astype(to_ref.dtype)
+
+                    over_tiles(self.cols, body, col + part * self.cols)
+                    yield
+
+        yield
+        yield from work(1, other)
+        swap = wire.start(other, got, core_partner())
+        yield from work(0, out)
+        swap.wait_recv()
+        for part in range(self.parts):
+            to_ref, got_ref = (out, got) if self.parts == 1 else (out.at[part], got.at[part])
+
+            def add(cols, _, to_ref=to_ref, got_ref=got_ref):
+                to_ref[:, cols] += got_ref[:, cols].astype(F32)
+
+            over_tiles(self.cols, add)
+        swap.wait_send()
 
 
 def together(groups, collective_id):
@@ -669,9 +1274,11 @@
         wires = [Wire(*take(2)) for g in groups]
         barrier = pltpu.get_barrier_semaphore()
         for axis, rel in partners:
-            partner = chip_partner(rel) if axis == "dp" else z_partner(rel)
             pl.semaphore_signal(
-                barrier, inc=1, device_id=partner, device_id_type=pl.DeviceIdType.MESH
+                barrier,
+                inc=1,
+                device_id=partner_of(axis, rel),
+                device_id_type=pl.DeviceIdType.MESH,
             )
         pl.semaphore_wait(barrier, len(partners))
         running = [
@@ -697,7 +1304,7 @@
         out_specs=[pl.BlockSpec(memory_space=pltpu.VMEM)] * len(outs),
         scratch_shapes=scratch,
         compiler_params=pltpu.CompilerParams(
-            collective_id=collective_id, has_side_effects=True, vmem_limit_bytes=58 * 2**20
+            collective_id=collective_id, has_side_effects=True, vmem_limit_bytes=62 * 2**20
         ),
         cost_estimate=pl.CostEstimate(
             flops=sum(g.flops for g in groups), bytes_accessed=size, transcendentals=0
@@ -730,7 +1337,7 @@
     low = summed[:, 2 * units :].astype(BF16)
     adapter[...] = low
 
-    def widen(cols):
+    def widen(cols, _):
         gate_up[:, cols] = summed[:, cols] + fast(low, up[:, cols], PLAIN)
 
     over_tiles(2 * units, widen)
@@ -786,14 +1393,15 @@
 
 def norm_back_local(width, summed, args, outs):
     value, inverse, gain, skip = args
-    d_value, d_gain = outs
+    d_gain = outs[-1]
     dy = summed[...]
     scaled = dy * gain[...]
     v, inv = value[...], inverse[...]
     weighted = yield jnp.sum(scaled * v, axis=1, keepdims=True)
     d_gain[...] = jnp.sum(dy * v * inv, axis=0, keepdims=True)
     result = scaled * inv - v * (inv * inv * inv * weighted / width) + skip[...]
-    d_value[...] = result
+    if len(outs) == 2:
+        outs[0][...] = result
     yield result.astype(BF16)
 
 
@@ -816,7 +1424,7 @@
 
 def proj_collect(links, own, other):
     mine = (own + links.core_swap(other).astype(F32)).astype(BF16)
-    blocks = [mine[:, rel] for rel in range(links.chips)]
+    blocks = [mine[rel] for rel in range(links.chips)]
     rows = jnp.stack(links.chip_a2a(blocks), 0)
     if links.chips == links.n_t:
         rows = links.by_index(rows, 0, links.chip ^ links.t)
@@ -1071,38 +1679,62 @@
     return jax.ShapeDtypeStruct(shape, dtype)
 
 
+def mixer_rows(links, m):
+    whole = m.shared_all.reshape(-1, m.shared_all.shape[2])
+    m.mamba_in = m.hid.astype(F32) + whole.astype(F32)
+    m.mamba_in_z = own_rows(links, m.hid).astype(F32) + m.shared_z.astype(F32)
+
+
+def projection_grads(links, micro):
+    block = jnp.concatenate([m.block for m in micro], axis=0)
+    low = jnp.concatenate([m.shared_low for m in micro], axis=0)
+    cols = links.dp_order(low, 2).reshape(low.shape[:2] + (links.chips, 2, -1))
+    spec = "crd,crxn->xdn"
+    return dotf(spec, block, cols[:, :, :, 0]), dotl(spec, block, cols[:, :, :, 1])
+
+
+def enter_group(links, w, m):
+    rows = m.hid.shape[0]
+    places = jnp.arange(rows, dtype=jnp.int32)
+    m.true = layout(m.lens, places)
+    _, position, _, allowed = layout(m.lens, links.rows_by_t(places))
+    m.allowed_rel = allowed.astype(F32)
+    m.cos, m.sin = rope_tables(position)
+    return Enter(m.hid, m.emb, w.g_attn[None, :])
+
+
+def take_enter(m, got):
+    m.attn_in, m.joined_z, m.inv_attn_z = got
+
+
 def attend_group(links, w, m):
-    wide = m.joined.astype(F32) * m.inv_attn[:, :, None]
-    m.attn_in = (wide * w.g_attn).astype(BF16)
-    rows, width = m.attn_in.shape[1], w.qkv.shape[1]
+    rows, width = m.attn_in.shape[1], w.qkv_pair.shape[1]
     args = (m.cos, m.sin, m.allowed_rel)
     outs = (sds((rows, width), BF16),)
-    return ByChips(m.attn_in, w.qkv, False, width // 3, attend_local, args, outs)
+    return ByChips(m.attn_in, w.qkv_pair, False, width // 3, attend_local, args, outs)
 
 
 def attend_out_group(links, w, m):
-    r, width = m.joined.shape[1] // links.n_t, m.joined.shape[2]
-    m.joined_z = m.joined[:, :r].astype(F32).reshape(-1, width)
-    m.inv_attn_z = m.inv_attn[:, :r].reshape(-1, 1)
+    width = m.joined_z.shape[1]
     outs = (sds(m.joined_z.shape), sds(m.inv_attn_z.shape))
     args = (m.joined_z, w.g_mlp[None, :])
     work = partial(norm_local, width * links.chips)
-    return ByTensor(m.attended, w.out, False, work, args, outs)
+    return ByTensor(m.attended, w.out_pair, False, work, args, outs)
 
 
 def feed_group(links, w, m):
-    rows, units = m.mlp_in.shape[1], w.down.shape[0]
-    outs = (sds((rows, 2 * units)), sds((rows, w.gate_up.shape[1] - 2 * units), BF16))
+    rows, units = m.mlp_in.shape[1], w.down_pair.shape[0]
+    outs = (sds((rows, 2 * units)), sds((rows, w.gate_up_pair.shape[1] - 2 * units), BF16))
     args = (w.adapter_up,)
-    return ByChips(m.mlp_in, w.gate_up, False, units, feed_local, args, outs)
+    return ByChips(m.mlp_in, w.gate_up_pair, False, units, feed_local, args, outs)
 
 
 def feed_back_group(links, w, m):
     args = (m.gate_up, w.adapter_up)
-    rank = w.gate_up.shape[1] - m.gate_up.shape[1]
+    rank = w.gate_up_pair.shape[1] - m.gate_up.shape[1]
     scratch = (pltpu.VMEM((m.gate_up.shape[0], rank), F32),)
-    width = w.gate_up.shape[1]
-    return ByChips(m.mlp_low, w.down, True, width, feed_back_local, args, (), scratch)
+    width = w.gate_up_pair.shape[1]
+    return ByChips(m.mlp_low, w.down_pair, True, width, feed_back_local, args, (), scratch)
 
 
 def feed_back_out_group(links, w, m):
@@ -1110,21 +1742,54 @@
     args = (m.mid_z, m.inv_mlp, w.g_mlp[None, :], m.d_block.reshape(m.mid_z.shape))
     outs = (sds(m.mid_z.shape), sds((1, width)))
     work = partial(norm_back_local, width * links.chips)
-    return ByTensor(m.gate_up_low, w.gate_up, True, work, args, outs)
+    return ByTensor(m.gate_up_low, w.gate_up_pair, True, work, args, outs)
 
 
 def attend_back_group(links, w, m):
     args = (m.qkv_low, m.cos, m.sin, m.allowed_rel)
-    width = w.qkv.shape[1]
-    return ByChips(m.attn_low, w.out, True, width, attend_back_local, args, ())
+    width = w.qkv_pair.shape[1]
+    return ByChips(m.attn_low, w.out_pair, True, width, attend_back_local, args, ())
 
 
 def leave_group(links, w, m):
     width = m.joined_z.shape[1]
     args = (m.joined_z, m.inv_attn_z, w.g_attn[None, :], m.d_mid)
-    outs = (sds(m.joined_z.shape), sds((1, width)))
     work = partial(norm_back_local, width * links.chips)
-    return ByTensor(m.d_qkv, w.qkv, True, work, args, outs, gather=False)
+    theirs = jnp.concatenate([m.d_mamba, jnp.zeros_like(m.d_mamba)], axis=1)
+    return Leave(m.d_qkv, w.qkv_pair, work, args, sds((1, width)), theirs)
+
+
+def feed_out_group(links, w, m):
+    return FeedOut(m.hidden, w.down_pair, m.mid_z, w.proj)
+
+
+def settle_group(links, w, m):
+    grad = own_rows(links, m.grad_low)
+    return Settle(m.terms, w.bc, m.mamba_in_z, w.g_mamba[None, :], grad, w.proj)
+
+
+def spread_group(links, w, m):
+    return Spread(w.proj_own)
+
+
+def outputs_group(links, w, micro):
+    terms = [z_split(links, links.rows_by_t(m.mamba_out), 0) for m in micro]
+    base = [m.mamba_in_z for m in micro]
+    valid = [own_rows(links, m.true[2])[:, None].astype(F32) for m in micro]
+    args = (jnp.concatenate(terms, 1), jnp.concatenate(base, 0), jnp.concatenate(valid, 0))
+    return Outputs(*args)
+
+
+def take_feed_out(m, got):
+    m.block, m.shared_all, m.shared_z = got
+    m.block = m.block.reshape(4, -1, m.block.shape[1])
+
+
+def take_settle(m, got):
+    gathered, m.shared_low, m.d_mamba, m.state_low, d_block, d_gain = got
+    m.mlp_low = z_join(gathered, 1)
+    m.d_block = d_block
+    m.sums_all = (m.d_taps_bc, d_gain[0])
 
 
 def take_attend(m, got):
@@ -1157,9 +1822,8 @@
 
 
 def take_leave(m, got):
-    d_joined, d_gain = got
+    d_gain, m.left = got
     m.grad_g_attn = d_gain[0]
-    m.d_joined = d_joined.astype(BF16)
 
 
 def fused(links, w, number, *work):
@@ -1168,6 +1832,7 @@
         taker(m, got)
 
 
+ENTER = (enter_group, take_enter)
 ATTEND = (attend_group, take_attend)
 ATTEND_OUT = (attend_out_group, take_attend_out)
 FEED = (feed_group, take_feed)
@@ -1175,6 +1840,16 @@
 FEED_BACK_OUT = (feed_back_out_group, take_feed_back_out)
 ATTEND_BACK = (attend_back_group, take_attend_back)
 LEAVE = (leave_group, take_leave)
+FEED_OUT = (feed_out_group, take_feed_out)
+SETTLE = (settle_group, take_settle)
+
+
+WEIGHT_GRADS = {
+    "down": ("crn,crd->nd", "hidden", "mlp_low", False, 1),
+    "gate_up": ("crd,crn->dn", "mlp_in", "gate_up_low", True, 1),
+    "out": ("crn,crd->nd", "attended", "attn_low", False, 1),
+    "qkv": ("crd,crn->dn", "attn_in", "d_qkv", True, 3),
+}
 
 
 def local(
@@ -1223,39 +1898,32 @@
     w = SimpleNamespace()
     gains = core_pair(links, jnp.stack([attention_gain, feedforward_gain], 0), 1).astype(F32)
     w.g_attn, w.g_mlp = gains[0], gains[1]
-    flat = jnp.concatenate([query_key_value_weight[:, i] for i in range(3)], axis=1)
-    w.qkv = lax.optimization_barrier(core_pair(links, flat, 0))
+    parts = query_key_value_weight.transpose(1, 0, 2)
+    w.qkv_pair = RowPair(parts, links.core_swap(parts))
     def stage(work, m):
         with jax.named_scope(f"{work.__name__}_micro{micro.index(m)}"):
             work(links, w, m)
 
-    for m in micro:
-        stage(enter, m)
-    inverses = jnp.stack([m.inverse for m in micro], 0)
-    inverses = jnp.stack(links.chip_a2a([inverses] * links.chips), 1)
-    for b, m in enumerate(micro):
-        m.inv_attn = inverses[b]
-    first = micro[0]
     units = gate_up_weight.shape[2]
     up_own = adapter_up.reshape(adapter_up.shape[0], 2 * units)
     cols = jnp.concatenate([gate_up_weight[:, 0], gate_up_weight[:, 1], adapter_down], axis=1)
-    w.out = lax.optimization_barrier(core_pair(links, attention_output_weight, 1))
-    w.gate_up = lax.optimization_barrier(core_pair(links, cols, 0))
-    w.down = lax.optimization_barrier(core_pair(links, down_weight, 1))
+    w.out_pair = ColPair(attention_output_weight, links.core_swap(attention_output_weight))
+    w.gate_up_pair = RowPair(cols, links.core_swap(cols))
+    w.down_pair = ColPair(down_weight, links.core_swap(down_weight))
+    w.proj_own = shared_projection_weight
     state_cols, step_cols = state_map_weight.shape[1], step_weight.shape[1]
     packed = jnp.concatenate([state_map_weight, step_weight, mixer_gain[:, None]], axis=1)
 
     w.smalls = smalls
     def gather_mixer():
-        w.adapter_up = lax.all_gather(after(up_own, first.joined), "dp", axis=0, tiled=True)
-        w.proj = proj_spread(links, shared_projection_weight)
-        whole = lax.all_gather(after(packed, first.attended), "dp", axis=0, tiled=True)
+        w.adapter_up = lax.all_gather(after(up_own, w.begun), "dp", axis=0, tiled=True)
+        whole = lax.all_gather(after(packed, w.begun), "dp", axis=0, tiled=True)
         w.bc = whole[:, :state_cols]
         w.dt = whole[:, state_cols : state_cols + step_cols]
         w.g_mamba = whole[:, state_cols + step_cols].astype(F32)
-        shard = after(mixer_input_weight.transpose(1, 0, 2), first.attended)
+        shard = after(mixer_input_weight.transpose(1, 0, 2), w.begun)
         w.w_in = lax.all_gather(shard, "dp", axis=1, tiled=True)
-        shard = after(mixer_output_weight, first.attended)
+        shard = after(mixer_output_weight, w.begun)
         w.mout = lax.all_gather(shard, "dp", axis=1, tiled=True)
 
     def run(*works):
@@ -1263,44 +1931,91 @@
             for m in micro:
                 stage(work, m)
 
+    def both(get, axis=0):
+        return jnp.concatenate([get(m) for m in micro], axis=axis)
+
+    def mixer_grads(done=None):
+        ssm_in = both(lambda m: m.ssm_in)
+        grad_in = dotl("td,ktc->kdc", ssm_in, both(lambda m: m.gate_x_low, 1))
+        begun = grad_in
+        grad_in = grad_in if done is None else after(grad_in, done)
+        grad_in = lax.psum_scatter(grad_in, "dp", scatter_dimension=1, tiled=True)
+        grad_mout = dotl("tn,ti->ni", both(lambda m: m.grad_low), both(lambda m: m.gated_norm))
+        grad_mout = grad_mout if done is None else after(grad_mout, done)
+        grad_mout = lax.psum_scatter(grad_mout, "dp", scatter_dimension=0, tiled=True)
+        grad_bc = dotl("td,tn->dn", both(lambda m: m.ssm_in_z), both(lambda m: m.state_low))
+        grad_dt = dotl("td,tn->dn", ssm_in, both(lambda m: m.step_low))
+        grad_small = jnp.concatenate([grad_bc, grad_dt], axis=1)
+        grad_small = lax.psum_scatter(grad_small, "dp", scatter_dimension=0, tiled=True)
+        grad_up = dotl("ra,rn->an", both(lambda m: m.adapter), both(lambda m: m.gate_up_own))
+        grad_up = lax.psum_scatter(grad_up, "dp", scatter_dimension=0, tiled=True)
+        return begun, grad_in, grad_mout, grad_small, grad_up
+
+    def weight_grad(name):
+        _, a, b, by_rows, parts = WEIGHT_GRADS[name]
+
+        def make(*_):
+            return WeightGrad([getattr(m, a) for m in micro], [getattr(m, b) for m in micro], by_rows, parts)
+
+        return (make, lambda _, got: setattr(w, "grad_" + name, got[0]), None)
+
     if links.chips == 4 and links.n_t == 4 and len(micro) == 2:
         a, b = micro
-        fused(links, w, 1, (*ATTEND, a))
+        spread = (spread_group, lambda _, got: setattr(w, "proj", got[0]), None)
+        fused(links, w, 1, (*ENTER, a))
+        fused(links, w, 2, (*ATTEND, a), spread, (*ENTER, b))
+        w.begun = a.attended
         gather_mixer()
-        fused(links, w, 2, (*ATTEND, b), (*ATTEND_OUT, a))
-        fused(links, w, 3, (*FEED, a), (*ATTEND_OUT, b))
-        fused(links, w, 4, (*FEED, b))
-        run(feed_out, mix, settle)
-        fused(links, w, 5, (*FEED_BACK, a))
-        fused(links, w, 6, (*FEED_BACK, b), (*FEED_BACK_OUT, a))
-        fused(links, w, 7, (*ATTEND_BACK, a), (*FEED_BACK_OUT, b))
-        fused(links, w, 8, (*ATTEND_BACK, b), (*LEAVE, a))
-        fused(links, w, 9, (*LEAVE, b))
+        fused(links, w, 3, (*ATTEND_OUT, a), (*ATTEND, b))
+        fused(links, w, 4, (*FEED, a), (*ATTEND_OUT, b))
+        fused(links, w, 5, (*FEED, b), (*FEED_OUT, a))
+        mixer_rows(links, a)
+        stage(mix, a)
+        fused(links, w, 6, (*FEED_OUT, b), (*SETTLE, a))
+        mixer_rows(links, b)
+        stage(mix, b)
+        outputs = (outputs_group, lambda _, got: setattr(w, "results", got[0]), micro)
+        fused(links, w, 7, (*FEED_BACK, a), (*SETTLE, b), outputs)
+        collect = (lambda *_: Collect(*projection_grads(links, micro)), lambda _, got: setattr(w, "grad_proj", got[0]), None)
+        fused(links, w, 8, (*FEED_BACK_OUT, a), (*FEED_BACK, b))
+        fused(links, w, 9, (*FEED_BACK_OUT, b), (*ATTEND_BACK, a), weight_grad("gate_up"))
+        fused(links, w, 10, (*LEAVE, a), (*ATTEND_BACK, b), weight_grad("down"))
+        mixed = mixer_grads(b.d_qkv)
+        fused(links, w, 11, (*LEAVE, b), weight_grad("qkv"), weight_grad("out"), collect)
+        grad_down, grad_cols, grad_out = w.grad_down, w.grad_gate_up, w.grad_out
+        grad_qkv = w.grad_qkv.transpose(1, 0, 2)
+        grad_proj = w.grad_proj
         for m in micro:
-            leave_rows(links, m)
+            m.d_hid, m.d_emb = jnp.split(m.left.reshape(-1, m.left.shape[2]), 2, axis=1)
+        results = w.results.reshape(links.n_t, len(micro), -1, w.results.shape[2])
+        results = z_join(results.transpose(1, 0, 2, 3), 1)
     else:
+        for m in micro:
+            stage(enter, m)
+        inverses = jnp.stack([m.inverse for m in micro], 0)
+        inverses = jnp.stack(links.chip_a2a([inverses] * links.chips), 1)
+        for b, m in enumerate(micro):
+            m.inv_attn = inverses[b]
+        w.qkv, w.out = w.qkv_pair.whole(), w.out_pair.whole()
+        w.gate_up, w.down = w.gate_up_pair.whole(), w.down_pair.whole()
+        w.proj = proj_spread(links, shared_projection_weight)
         run(attend)
+        w.begun = micro[0].attended
         gather_mixer()
         run(attend_out, feed, feed_out, mix, settle)
         run(feed_back, feed_back_out, attend_back, leave)
-    with jax.named_scope("outputs"):
         results = finish_output(links, micro)
-
-    def both(get, axis=0):
-        return jnp.concatenate([get(m) for m in micro], axis=axis)
-
-    ssm_in = both(lambda m: m.ssm_in)
-    grad_in = dotl("td,ktc->kdc", ssm_in, both(lambda m: m.gate_x_low, 1))
-    grad_in = lax.psum_scatter(grad_in, "dp", scatter_dimension=1, tiled=True)
-    grad_mout = dotl("tn,ti->ni", both(lambda m: m.grad_low), both(lambda m: m.gated_norm))
-    grad_mout = lax.psum_scatter(grad_mout, "dp", scatter_dimension=0, tiled=True)
-    grad_bc = dotl("td,tn->dn", both(lambda m: m.ssm_in_z), both(lambda m: m.state_low))
-    grad_dt = dotl("td,tn->dn", ssm_in, both(lambda m: m.step_low))
-    grad_small = jnp.concatenate([grad_bc, grad_dt], axis=1)
-    grad_small = lax.psum_scatter(grad_small, "dp", scatter_dimension=0, tiled=True)
-    grad_up = dotl("ra,rn->an", both(lambda m: m.adapter), both(lambda m: m.gate_up_own))
-    grad_up = lax.psum_scatter(grad_up, "dp", scatter_dimension=0, tiled=True)
-
+        grad_proj = proj_collect(links, *projection_grads(links, micro))
+        mixed = mixer_grads()
+
+        def grad(name, axis):
+            spec, a, b = WEIGHT_GRADS[name][:3]
+            terms = [dotf(spec, getattr(m, a), getattr(m, b)) for m in micro]
+            return core_rs(links, total(terms), axis)
+
+        grad_down, grad_cols, grad_out = grad("down", 1), grad("gate_up", 0), grad("out", 1)
+        grad_qkv = jnp.stack(jnp.split(grad("qkv", 0), 3, axis=1), 1)
+    _, grad_in, grad_mout, grad_small, grad_up = mixed
     sums_dp = jax.tree.map(lambda *v: total(v), *[m.sums_dp for m in micro])
     sums_all = jax.tree.map(lambda *v: total(v), *[m.sums_all for m in micro])
     flat_all = links.z_sum(jnp.concatenate([v.reshape(-1) for v in sums_all]))
@@ -1317,20 +2032,6 @@
     g_rows = g_rows[:, :half] + links.core_swap(g_rows[:, half:])
     g_rows = links.z_sum(g_rows)
 
-    def grad(spec, get_a, get_b, axis):
-        return core_rs(links, total([dotf(spec, get_a(m), get_b(m)) for m in micro]), axis)
-
-    block = both(lambda m: m.block)
-    cols = both(lambda m: m.shared_cols)
-    spec = "crd,crxn->dxn"
-    grad_proj = proj_collect(
-        links, dotf(spec, block, cols[:, :, :, 0]), dotl(spec, block, cols[:, :, :, 1])
-    )
-    grad_down = grad("crn,crd->nd", lambda m: m.hidden, lambda m: m.mlp_low, 1)
-    grad_cols = grad("crd,crn->dn", lambda m: m.mlp_in, lambda m: m.gate_up_low, 0)
-    grad_out = grad("crn,crd->nd", lambda m: m.attended, lambda m: m.attn_low, 1)
-    grad_qkv = grad("crd,crn->dn", lambda m: m.attn_in, lambda m: m.d_qkv, 0)
-    grad_qkv = jnp.stack(jnp.split(grad_qkv, 3, axis=1), 1)
     grad_gate_up = jnp.stack([grad_cols[:, :units], grad_cols[:, units : 2 * units]], 1)
     partial_t = [grad_cols[:, 2 * units :].astype(BF16), grad_small[:, :state_cols]]
     sizes = [v.size for v in partial_t]

time: 1400 us -> 1180 us (0.84)
  Pallas kernels: 633 us -> 911 us
  waiting for transfers between devices: 185 us -> 23.8 us
  other arithmetic: 173 us -> 41.7 us
  matrix products: 138 us -> 55 us
  starting transfers between devices: 105 us -> 32 us
  local copies, waits for them, and re-layouts: 141 us -> 84.7 us
    pallas_call x9 -> x11, Pallas kernels: 619 us -> 898 us  [together(): pl.pallas_call(kernel, out_shape=outs, in_specs=[pl.BlockSpec(memory_spac...]
    ppermute x51 -> x15, waiting for transfers between devices: 113 us -> 17.4 us  [z_swap(): return lax.ppermute(x, 'tensor', [(i, i ^ rel) for i in range(self.n_t)])]
    ppermute x36 -> x3, waiting for transfers between devices: 70.2 us -> 1.98 us  [chip_swap(): return lax.ppermute(x, 'dp', [(i, i ^ rel << 1) for i in range(self.n_dp)])]
    dot_general x25 -> x13, matrix products: 103 us -> 34.8 us  [dotf(): return jnp.einsum(spec, a, b, preferred_element_type=F32)]
    concatenate x17 -> x5, other arithmetic: 65.5 us -> 3.15 us  [the longest x1 1.08 us: outputs_group(): jnp.concatenate(terms, 1)]
    ppermute x36 -> x3, starting transfers between devices: 45.3 us -> 7.59 us  [chip_swap(): return lax.ppermute(x, 'dp', [(i, i ^ rel << 1) for i in range(self.n_dp)])]
    ppermute x51 -> x15, starting transfers between devices: 57.2 us -> 22.3 us  [z_swap(): return lax.ppermute(x, 'tensor', [(i, i ^ rel) for i in range(self.n_t)])]
    add x13 -> x2, other arithmetic: 23.9 us -> 1.74 us  [mixer_rows(): m.mamba_in_z = own_rows(links, m.hid).astype(F32) + m.shared_z.astype(F32)]
  transfers between devices with their start and end apart: 108 -> 33, of which waited for: 42 -> 8; matrix products, arithmetic and copies ran while one was open for 30% -> 10% of each run, Pallas kernels for 45% -> 56%
where the time goes in v3:
time: 1180 us; the launch traced here: 1170 us
  Pallas kernels  911 us (77%)
  local copies, waits for them, and re-layouts  84.7 us (7%)
  matrix products  55 us (5%)
  other arithmetic  41.7 us (4%)
  starting transfers between devices  32 us (3%)
  waiting for transfers between devices  23.8 us (2%)
  between operations  17.4 us (1%)
    pallas_call x11, Pallas kernels, together(): pl.pallas_call(kernel, out_shape=outs, in_specs=[pl.BlockSpec(memory_spac...  898 us
    dot_general x13, matrix products, dotf(): return jnp.einsum(spec, a, b, preferred_element_type=F32)  34.8 us
    unnamed x177, local copies, waits for them, and re-layouts  33.4 us
  transfers between devices with their start and end apart: 33, of which 8 were waited for; matrix products, arithmetic and copies ran while one was open for 10% of the time, Pallas kernels for 56%

profile of v3, /device:TPU:0, one launch (start us, length us, event | category | flops | bytes accessed | tf_op | source)
XLA Modules:
  0.0 1165.5 jit_solution(11587886962943937134)
XLA Ops:
  17.0 22.3 %shard_map.407 = (bf16[4,128,1024]{2,1,0:T(8,128)(2,1)}, f32[128,1024]{1,0:T(8,128)}, f32[128,1]{1,0:T(8,128)}) custom-call(bf16[128,2048]{1,0:T(8,128)(2,1)} %get-tuple-element.325.refs_0_, bf16[128,2048]{1,0:T(8,128)(2,1)} %get-tuple-element.331.refs_1_, f32[1,1024]{1,0:T(1,128)} %get-tuple-element.368.refs_2_.refs_9_.refs_5_), custom_call_target="tpu_custom_call" | custom-call | bytes 2626048 | tf_op jit(solution)/shard_map/pallas_call | solution.py:1300
  39.4 93.7 %shard_map.408 = (bf16[4,128,1024]{2,1,0:T(8,128)(2,1)}, bf16[128,3072]{1,0:T(8,128)(2,1)}, bf16[4,2,1024,256]{3,2,1,0:T(8,128)(2,1)}, bf16[4,128,1024]{2,1,0:T(...) custom-call(bf16[4,128,1024]{2,1,0:T(8,128)(2,1)} %get-tuple-element.104.refs_0_.refs_8_, ...), custom_call_target="tpu_custom_call" | custom-call | flops 3221225472 | bytes 16716288 | tf_op jit(solution)/shard_map/pallas_call | solution.py:1300
  141.0 9.1 fusion.89
  160.5 4.2 collective-permute-done.2.refs_2_.refs_6_.refs_9_.refs_10_
  164.6 71.2 %shard_map.409 = (bf16[4,4,32,1024]{3,2,1,0:T(8,128)(2,1)}, f32[128,1024]{1,0:T(8,128)}, f32[128,1]{1,0:T(8,128)}, bf16[4,128,1024]{2,1,0:T(8,128)(2,1)}, bf16[128,3072]{1,0:T(8,128)(2,1)}) custom-call(bf16[4,128,1024]{2,1,0:T(8,128)(2,1)} %get-tuple-element.105.refs_0_.refs_12_, bf16[1024,512]{1,0:T(8,128)(2,1)} %refs_9_.1, ...), custom_call_target="tpu_custom_call" | custom-call | flops 4294967296 | bytes 14619136 | tf_op jit(solution)/shard_map/pallas_call | solution.py:1300
  235.8 117.5 %shard_map.410 = (bf16[4,128,2048]{2,1,0:T(8,128)(2,1)}, f32[128,4096]{1,0:T(8,128)}, bf16[128,128]{1,0:T(8,128)(2,1)}, bf16[4,4,32,1024]{3,2,1,0:T(8,128)(2,1)}, f32[128,1024]{1,0:T(8,128)}, /*index=5*/f32[128,1]{1,0:T(8,128)}) custom-call(bf16[4,128,1024]{2,1,0:T(8,128)(2,1)} %bitcast.252, bf16[512,4224]{1,0:T(8,128)(2,1)} %pad_maximum_fusion.1.refs_1_, ...), custom_call_target="tpu_custom_call" | custom-call | flops 5502926848 | bytes 20222464 | tf_op jit(solution)/shard_map/pallas_call | solution.py:1300
  353.3 82.4 %shard_map.411 = (bf16[4,128,2048]{2,1,0:T(8,128)(2,1)}, f32[128,4096]{1,0:T(8,128)}, bf16[128,128]{1,0:T(8,128)(2,1)}, bf16[128,1024]{1,0:T(8,128)(2,1)}, bf16[...) custom-call(bf16[4,128,1024]{2,1,0:T(8,128)(2,1)} %bitcast.254, bf16[512,4224]{1,0:T(8,128)(2,1)} %pad_maximum_fusion.1.refs_1_, ...), custom_call_target="tpu_custom_call" | custom-call | flops 6576668672 | bytes 26902528 | tf_op jit(solution)/shard_map/pallas_call | solution.py:1300
  444.8 4.5 broadcast_multiply_fusion.1
  449.4 6.4 convolution_bitcast_fusion.4.gate_ref
  465.7 4.9 mix_micro0.3
  473.5 63.4 %shard_map.412 = (bf16[128,1024]{1,0:T(8,128)(2,1)}, bf16[4,32,2048]{2,1,0:T(8,128)(2,1)}, bf16[32,2048]{1,0:T(8,128)(2,1)}, bf16[4,4,32,1024]{3,2,1,0:T(8,128)(...) custom-call(bf16[4,128,2048]{2,1,0:T(8,128)(2,1)} %get-tuple-element, ...), custom_call_target="tpu_custom_call" | custom-call | flops 3221225472 | bytes 20545536 | tf_op jit(solution)/shard_map/pallas_call | solution.py:1300
  539.9 6.5 convolution_bitcast_fusion.3.gate_ref
  547.1 3.0 multiply_reduce_fusion.3
  557.4 3.0 convolution_convert_fusion.3
  568.1 5.3 mix_micro1.3
  575.2 4.7 convolution_bitcast_fusion
  585.4 91.6 %shard_map.413 = (bf16[4,128,4224]{2,1,0:T(8,128)(2,1)}, bf16[4,4,32,1024]{3,2,1,0:T(8,128)(2,1)}, bf16[4,32,2048]{2,1,0:T(8,128)(2,1)}, f32[32,2048]{1,0:T(8,12...) custom-call(bf16[4,128,1024]{2,1,0:T(8,128)(2,1)} %bitcast.222, ...), custom_call_target="tpu_custom_call" | custom-call | flops 3221225472 | bytes 23953664 | tf_op jit(solution)/shard_map/pallas_call | solution.py:1300
  681.7 77.8 %shard_map.414 = (bf16[4,4,32,1024]{3,2,1,0:T(8,128)(2,1)}, f32[128,1024]{1,0:T(8,128)}, f32[1,1024]{1,0:T(1,128)}, bf16[4,128,4224]{2,1,0:T(8,128)(2,1)}) custom-call(bf16[4,128,4224]{2,1,0:T(8,128)(2,1)} %get-tuple-element.134.refs_0_.refs_16_, bf16[512,4224]{1,0:T(8,128)(2,1)} %pad_maximum_fusion.1.refs_1_, ...), custom_call_target="tpu_custom_call" | custom-call | flops 6576668672 | bytes 28320256 | tf_op jit(solution)/shard_map/pallas_call | solution.py:1300
  763.6 74.6 %shard_map.415 = (bf16[4,4,32,1024]{3,2,1,0:T(8,128)(2,1)}, f32[128,1024]{1,0:T(8,128)}, f32[1,1024]{1,0:T(1,128)}, bf16[4,128,3072]{2,1,0:T(8,128)(2,1)}, f32[512,4224]{1,0:T(8,128)}) custom-call(bf16[4,128,4224]{2,1,0:T(8,128)(2,1)} %get-tuple-element.139.refs_0_.refs_17_, bf16[512,4224]{1,0:T(8,128)(2,1)} %pad_maximum_fusion.1.refs_1_, ...), custom_call_target="tpu_custom_call" | custom-call | flops 9932111872 | bytes 42279424 | tf_op jit(solution)/shard_map/pallas_call | solution.py:1300
  838.2 84.0 %shard_map.416 = (f32[1,1024]{1,0:T(1,128)}, bf16[4,32,4096]{2,1,0:T(8,128)(2,1)}, bf16[4,128,3072]{2,1,0:T(8,128)(2,1)}, f32[2048,512]{1,0:T(8,128)}) custom-call(bf16[4,128,3072]{2,1,0:T(8,128)(2,1)} %get-tuple-element.144.refs_0_.refs_10_, bf16[3,512,1024]{2,1,0:T(8,128)(2,1)} %bitcast.212, bf16[3,512,1024]{2,1,0:T(8,128)(2,1)} %collective-permute-done.1.refs_2_.refs_7_, ...), custom_call_target="tpu_custom_call" | custom-call | flops 6442450944 | bytes 29827584 | tf_op jit(solution)/shard_map/pallas_call | solution.py:1300
  924.2 4.4 convert_add_fusion
  929.8 5.9 add_bitcast_fusion
  942.8 2.8 convolution_bitcast_fusion.2.refs_16_
  947.7 119.1 %shard_map.417 = (f32[1,1024]{1,0:T(1,128)}, bf16[4,32,4096]{2,1,0:T(8,128)(2,1)}, f32[3,512,1024]{2,1,0:T(8,128)}, f32[1024,512]{1,0:T(8,128)}, f32[1024,256]{1,0:T(8,128)}) custom-call(bf16[4,128,3072]{2,1,0:T(8,128)(2,1)} %get-tuple-element.151.refs_0_.refs_11_, bf16[3,512,1024]{2,1,0:T(8,128)(2,1)} %bitcast.213, ...), custom_call_target="tpu_custom_call" | custom-call | flops 7516192768 | bytes 40378880 | tf_op jit(solution)/shard_map/pallas_call | solution.py:1300
  1071.3 4.0 slice_bitcast_fusion.1
  1077.4 3.6 collective-permute-start.20
  1082.9 11.0 copy.205
  1094.9 3.6 collective-permute-start.14
  1100.3 2.7 collective-permute-done.13
  1103.0 3.7 collective-permute-start.24
  1126.1 11.9 %collective-permute-done.16 = bf16[1024,128]{1,0:T(8,128)(2,1)S(1)} collective-permute-done((bf16[1024,128]{1,0:T(8,128)(2,1)S(1)}, bf16[1024,128]{1,0:T(8,128)(2,1)S(1)}, u32[]{:S(2)}, u32[]{:S(2)}) %collective-permute-start.16) | collective-permute-done | bytes 262176 | tf_op jit(solution)/shard_map/ppermute | solution.py:314
  1145.8 6.8 copy.237
  (408 shorter events, 138.3 us)
Async XLA Ops:
  7.2 228.6 %all-gather.5.cloned.1.call-start = ((), (), s32[]{:S(2)}) async-start(), calls=%async_computation.4 | async-start | bytes 1179648 | tf_op jit(solution)/shard_map/all_gather | solution.py:1919
  8.7 7.6 collective-permute-start
  9.2 30.1 %collective-permute-start.1 = (bf16[3,512,1024]{2,1,0:T(8,128)(2,1)}, bf16[3,512,1024]{2,1,0:T(8,128)(2,1)}, u32[]{:S(2)}, u32[]{:S(2)}) collective-permute-start(bf16[3,512,1024]{2,1,0:T(8,128)(2,1)} %bitcast.209), channel_id=1, source_target_pairs={{0,4},{4,0},{8,12},{12,8},{16,20},{20,16},{24,28},{28,24},{1,5},{5... | collective-permute-start | bytes 9437192 | tf_op jit(solution)/shard_map/ppermute | solution.py:308
  135.7 303.2 %all-gather.9.cloned.1.call-start = ((), (), s32[]{:S(2)}) async-start(), calls=%async_computation.6 | async-start | bytes 1769472 | tf_op jit(solution)/shard_map/all_gather | solution.py:1920
  137.7 307.1 %all-gather.11.cloned.1.call-start = ((), (), s32[]{:S(2)}) async-start(), calls=%async_computation.7 | async-start | bytes 4718592 | tf_op jit(solution)/shard_map/all_gather | solution.py:1927
  138.6 310.8 %all-gather.7.cloned.1.call-start = ((), (), s32[]{:S(2)}) async-start(), calls=%async_computation.5 | async-start | bytes 9437184 | tf_op jit(solution)/shard_map/all_gather | solution.py:1925
  140.8 973.0 %reduce-scatter.5.cloned.1.call-start = ((), (), s32[]{:S(2)}) async-start(), calls=%async_computation.8 | async-start | bytes 1253376 | tf_op jit(solution)/shard_map/reduce_scatter | solution.py:1949
  155.1 80.7 %collective-permute-start.3 = (bf16[512,4224]{1,0:T(8,128)(2,1)}, bf16[512,4224]{1,0:T(8,128)(2,1)}, u32[]{:S(2)}, u32[]{:S(2)}) collective-permute-start(bf16[512,4224]{1,0:T(8,128)(2,1)} %pad_maximum_fusion.1.refs_1_), channel_id=1, source_target_pairs={{0,4},{4,0},{8,12},{12,8},{16,20},{20,16},{24,28},{28,24},{1,5},{5... | collective-permute-start | bytes 12976136 | tf_op jit(solution)/shard_map/ppermute | solution.py:308
  155.5 9.2 collective-permute-start.2
  155.6 197.7 %collective-permute-start.4 = (bf16[2048,512]{1,0:T(8,128)(2,1)}, bf16[2048,512]{1,0:T(8,128)(2,1)}, u32[]{:S(2)}, u32[]{:S(2)}) collective-permute-start(bf16[2048,512]{1,0:T(8,128)(2,1)} %refs_8_.2), channel_id=1, source_target_pairs={{0,4},{4,0},{8,12},{12,8},{16,20},{20,16},{24,28},{28,24},{1,5},{5... | collective-permute-start | bytes 6291464 | tf_op jit(solution)/shard_map/ppermute | solution.py:308
  457.4 7.1 collective-permute-start.7
  459.8 5.3 collective-permute-start.6
  460.5 5.0 collective-permute-start.5
  551.6 14.9 %collective-permute-start.10 = (f32[128,2]{1,0:T(8,128)S(1)}, f32[128,2]{1,0:T(8,128)}, u32[]{:S(2)}, u32[]{:S(2)}) collective-permute-start(f32[128,2]{1,0:T(8,128)S(1)} %get-tuple-element.128), channel_id=1, source_target_pairs={{0,3},{1,2},{2,1},{3,0},{4,7},{5,6},{6,5},{7,4},{8,11},{9,10},{10,... | collective-permute-start | bytes 3080 | tf_op jit(solution)/shard_map/mix_micro1/ppermute | solution.py:314
  553.7 12.8 %collective-permute-start.9 = (f32[128,2]{1,0:T(8,128)S(1)}, f32[128,2]{1,0:T(8,128)}, u32[]{:S(2)}, u32[]{:S(2)}) collective-permute-start(f32[128,2]{1,0:T(8,128)S(1)} %get-tuple-element.128), channel_id=1, source_target_pairs={{0,2},{1,3},{2,0},{3,1},{4,6},{5,7},{6,4},{7,5},{8,10},{9,11},{10,... | collective-permute-start | bytes 3080 | tf_op jit(solution)/shard_map/mix_micro1/ppermute | solution.py:314
  553.7 12.8 %collective-permute-start.8 = (f32[128,2]{1,0:T(8,128)S(1)}, f32[128,2]{1,0:T(8,128)}, u32[]{:S(2)}, u32[]{:S(2)}) collective-permute-start(f32[128,2]{1,0:T(8,128)S(1)} %get-tuple-element.128), channel_id=1, source_target_pairs={{0,1},{1,0},{2,3},{3,2},{4,5},{5,4},{6,7},{7,6},{8,9},{9,8},{10,11... | collective-permute-start | bytes 3080 | tf_op jit(solution)/shard_map/mix_micro1/ppermute | solution.py:314
  679.4 442.5 %reduce-scatter.7.cloned.1.call-start = ((), (), s32[]{:S(2)}) async-start(), calls=%async_computation.9 | async-start | bytes 1179648 | tf_op jit(solution)/shard_map/reduce_scatter | solution.py:1951
  763.5 376.1 %reduce-scatter.11.cloned.1.call-start = ((), (), s32[]{:S(2)}) async-start(), calls=%async_computation.11 | async-start | bytes 4718592 | tf_op jit(solution)/shard_map/reduce_scatter | solution.py:1945
  928.7 213.4 %reduce-scatter.9.cloned.1.call-start = ((), (), s32[]{:S(2)}) async-start(), calls=%async_computation.10 | async-start | bytes 9437184 | tf_op jit(solution)/shard_map/reduce_scatter | solution.py:1942
  1067.6 27.3 %collective-permute-start.11 = (f32[2,512]{1,0:T(2,128)S(1)}, f32[2,512]{1,0:T(2,128)S(1)}, u32[]{:S(2)}, u32[]{:S(2)}) collective-permute-start(f32[2,512]{1,0:T(2,128)S(1)} %slice.240), channel_id=1, source_target_pairs={{0,4},{4,0},{8,12},{12,8},{16,20},{20,16},{24,28},{28,24},{1,5},{5... | collective-permute-start | bytes 12296 | tf_op jit(solution)/shard_map/ppermute | solution.py:308
  1077.4 21.1 %collective-permute-start.20 = (f32[3072]{0:T(1024)S(1)}, f32[3072]{0:T(1024)S(1)}, u32[]{:S(2)}, u32[]{:S(2)}) collective-permute-start(f32[3072]{0:T(1024)S(1)} %pad_maximum_fusion.22), channel_id=1, source_target_pairs={{0,3},{1,2},{2,1},{3,0},{4,7},{5,6},{6,5},{7,4},{8,11},{9,10},{10,... | collective-permute-start | bytes 36872 | tf_op jit(solution)/shard_map/ppermute | solution.py:314
  1081.1 18.2 %collective-permute-start.19 = (f32[3072]{0:T(1024)S(1)}, f32[3072]{0:T(1024)S(1)}, u32[]{:S(2)}, u32[]{:S(2)}) collective-permute-start(f32[3072]{0:T(1024)S(1)} %pad_maximum_fusion.22), channel_id=1, source_target_pairs={{0,2},{1,3},{2,0},{3,1},{4,6},{5,7},{6,4},{7,5},{8,10},{9,11},{10,... | collective-permute-start | bytes 36872 | tf_op jit(solution)/shard_map/ppermute | solution.py:314
  1081.4 17.9 %collective-permute-start.18 = (f32[3072]{0:T(1024)S(1)}, f32[3072]{0:T(1024)S(1)}, u32[]{:S(2)}, u32[]{:S(2)}) collective-permute-start(f32[3072]{0:T(1024)S(1)} %pad_maximum_fusion.22), channel_id=1, source_target_pairs={{0,1},{1,0},{2,3},{3,2},{4,5},{5,4},{6,7},{7,6},{8,9},{9,8},{10,11... | collective-permute-start | bytes 36872 | tf_op jit(solution)/shard_map/ppermute | solution.py:314
  1094.9 5.5 collective-permute-start.14
  1098.5 4.5 collective-permute-start.13
  1098.5 4.5 collective-permute-start.12
  1103.0 8.2 collective-permute-start.24
  1106.7 4.5 collective-permute-start.23
  1109.2 4.0 collective-permute-start.22
  1114.9 11.1 collective-permute-start.17
  1116.7 21.3 %collective-permute-start.16 = (bf16[1024,128]{1,0:T(8,128)(2,1)S(1)}, bf16[1024,128]{1,0:T(8,128)(2,1)S(1)}, u32[]{:S(2)}, u32[]{:S(2)}) collective-permute-start(bf16[1024,128]{1,0:T(8,128)(2,1)S(1)} %pad_maximum_fusion.15), channel_id=1, source_target_pairs={{0,2},{1,3},{2,0},{3,1},{4,6},{5,7},{6,4},{7,5},{8,10},{9,11},{10,... | collective-permute-start | bytes 786440 | tf_op jit(solution)/shard_map/ppermute | solution.py:314
  1117.8 20.2 %collective-permute-start.15 = (bf16[1024,128]{1,0:T(8,128)(2,1)S(1)}, bf16[1024,128]{1,0:T(8,128)(2,1)S(1)}, u32[]{:S(2)}, u32[]{:S(2)}) collective-permute-start(bf16[1024,128]{1,0:T(8,128)(2,1)S(1)} %pad_maximum_fusion.15), channel_id=1, source_target_pairs={{0,1},{1,0},{2,3},{3,2},{4,5},{5,4},{6,7},{7,6},{8,9},{9,8},{10,11... | collective-permute-start | bytes 786440 | tf_op jit(solution)/shard_map/ppermute | solution.py:314
  (83 other events, 2714.7 us)
Sparse Core Ops, SparseCore 0:
  135.8 25.1 all-gather.4
  163.5 31.3 all-gather.8
  197.3 43.5 all-gather.10
  243.3 85.6 all-gather.6
  679.5 39.4 reduce-scatter.4
  763.6 39.2 reduce-scatter.6
  928.8 49.7 reduce-scatter.10
  982.5 73.2 reduce-scatter.8

commit v4 on v3

--- a/solution.py
+++ b/solution.py
@@ -447,7 +447,11 @@
 
 
 def z_partner(rel):
-    return {"tensor": flip(lax.axis_index("tensor"), rel)}
+    t = lax.axis_index("tensor")
+    for bit in (1, 2):
+        if rel & bit:
+            t = flip(t, bit)
+    return {"tensor": t}
 
 
 def core_partner():
@@ -492,17 +496,18 @@
 TILE = 256
 
 
-def over_tiles(width, body, offset=0):
+def over_tiles(width, body, *offsets):
+    offsets = (0,) + (offsets or (0,))
+
     def step(i, carry):
-        at = pl.ds(pl.multiple_of(i * TILE, 128), TILE)
-        body(at, pl.ds(pl.multiple_of(offset + i * TILE, 128), TILE))
+        starts = [pl.multiple_of(offset + i * TILE, 128) for offset in offsets]
+        body(*[pl.ds(start, TILE) for start in starts])
         return carry
 
     count = width // TILE
     lax.fori_loop(0, count, step, 0)
     if width % TILE:
-        low, left = count * TILE, width % TILE
-        body(pl.ds(low, left), pl.ds(offset + low, left))
+        body(*[pl.ds(offset + count * TILE, width % TILE) for offset in offsets])
 
 
 class RowPair:
@@ -519,32 +524,37 @@
     def pick(self, ref, part):
         return ref if self.parts == 1 else ref.at[part]
 
-    def times(self, x, refs, by_cols, store):
+    def chunks(self, by_cols):
+        if by_cols:
+            return [(0, self.half), (self.half, self.half)]
+        if self.parts > 1:
+            return [(i * self.cols, self.cols) for i in range(self.parts)]
+        low = self.cols // 2 // TILE * TILE
+        return [(0, low), (low, self.cols - low)]
+
+    def times(self, x, refs, by_cols, store, chunk):
         half, cols = self.half, self.cols
+        start, width = self.chunks(by_cols)[chunk]
         if by_cols:
-            for h, ref in enumerate(refs):
-
-                def body(at, to, ref=ref):
-                    store(
-                        to,
-                        total(
-                            [
-                                fast(x(slice(i * cols, i * cols + cols)), self.pick(ref, i)[at, :], BY_COLS)
-                                for i in range(self.parts)
-                            ]
-                        ),
-                    )
-
-                over_tiles(half, body, h * half)
+            ref = refs[chunk]
+
+            def body(at, to):
+                terms = [
+                    fast(x(slice(i * cols, i * cols + cols)), self.pick(ref, i)[at, :], BY_COLS)
+                    for i in range(self.parts)
+                ]
+                store(to, total(terms))
+
+            over_tiles(width, body, start)
             return
-        for i in range(self.parts):
-
-            def body(at, to, i=i):
-                own, other = (self.pick(ref, i)[:, at] for ref in refs)
-                left, right = x(slice(0, half)), x(slice(half, 2 * half))
-                store(to, fast(left, own, PLAIN) + fast(right, other, PLAIN))
-
-            over_tiles(cols, body, i * cols)
+        part, low = (chunk, 0) if self.parts > 1 else (0, start)
+
+        def body(_, at, to):
+            own, other = (self.pick(ref, part)[:, at] for ref in refs)
+            left, right = x(slice(0, half)), x(slice(half, 2 * half))
+            store(to, fast(left, own, PLAIN) + fast(right, other, PLAIN))
+
+        over_tiles(width, body, low, start)
 
 
 class ColPair:
@@ -556,27 +566,31 @@
     def whole(self):
         return jnp.concatenate(self.args, axis=1)
 
-    def times(self, x, refs, by_cols, store):
+    def chunks(self, by_cols):
+        width = self.rows // 2 if by_cols else self.half
+        return [(0, width), (width, width)]
+
+    def times(self, x, refs, by_cols, store, chunk):
         half = self.half
+        start, width = self.chunks(by_cols)[chunk]
         if by_cols:
             own, other = refs
 
-            def body(at, to):
+            def body(_, at):
                 left, right = x(slice(0, half)), x(slice(half, 2 * half))
-                store(to, fast(left, own[at, :], BY_COLS) + fast(right, other[at, :], BY_COLS))
-
-            over_tiles(self.rows, body)
+                store(at, fast(left, own[at, :], BY_COLS) + fast(right, other[at, :], BY_COLS))
+
+            over_tiles(width, body, start)
             return
-        for h, ref in enumerate(refs):
-
-            def body(at, to, ref=ref):
-                store(to, fast(x(slice(0, self.rows)), ref[:, at], PLAIN))
-
-            over_tiles(half, body, h * half)
+        ref = refs[chunk]
+
+        def body(at, to):
+            store(to, fast(x(slice(0, self.rows)), ref[:, at], PLAIN))
+
+        over_tiles(width, body, start)
 
 
 class ByChips:
-    copies = 12
     partners = [("dp", 1), ("dp", 2)]
 
     def __init__(self, x, w, by_cols, out_width, local, args, outs, scratch=()):
@@ -586,6 +600,8 @@
         self.w = w
         self.args = (x,) + w.args + tuple(args)
         self.outs = (jax.ShapeDtypeStruct((4, self.rows, out_width), BF16),) + tuple(outs)
+        self.chunks = w.chunks(by_cols)
+        self.copies = 6 * len(self.chunks) + 12
         self.scratch = chip_scratch(self.rows, self.width)
         self.scratch += [pltpu.VMEM((self.rows, self.width), F32)] + list(scratch)
         self.flops = 8 * self.rows * x.shape[2] * self.width
@@ -596,19 +612,18 @@
         gathered = outs[0]
         rows = self.rows
 
-        def dot(low, high):
+        def dot(low, high, chunk):
             def left(at):
                 return x[low:high, :, at].reshape((high - low) * rows, at.stop - at.start)
 
             def store(to, value):
                 part[low:high, :, to] = value.astype(BF16).reshape(high - low, rows, value.shape[1])
 
-            self.w.times(left, w, self.by_cols, store)
-
-        dot(1, 4)
-        yield from chip_sum(wire, part, first, second, summed, lambda: dot(0, 1))
+            self.w.times(left, w, self.by_cols, store, chunk)
+
+        yield from chip_sum(wire, part, first, second, summed, self.chunks, dot)
         self.local(summed, gathered.at[0], args[3:], outs[1:], scratch[4:])
-        yield from chip_gather(wire, [gathered.at[rel] for rel in range(4)], rows)
+        yield from chip_gather(wire, gathered)
 
 
 def pieces(rows):
@@ -616,51 +631,66 @@
     return [(p, slice(p * half, (p + 1) * half), 1 << p, 1 << (1 - p)) for p in range(2)]
 
 
-def chip_sum(wire, part, first, second, summed, meanwhile=None):
-    rows, width = summed.shape
-    sent, later = [], []
-    for p, at, bit, _ in pieces(rows):
-        for i, rel in enumerate((bit, 3)):
-            sent.append(wire.start(part.at[rel, at], first.at[p, i], chip_partner(bit)))
-    if meanwhile:
-        meanwhile()
+def chip_sum(wire, part, first, second, summed, chunks, dot):
+    halves = pieces(summed.shape[0])
+    sent, later = {}, {}
+    for n, (start, width) in enumerate(chunks):
+        cols = slice(start, start + width)
+        dot(1, 4, n)
+        for p, at, bit, _ in halves:
+            for i, rel in ((1, 3), (0, bit)):
+                src, dst = part.at[rel, at, cols], first.at[p, i, :, cols]
+                sent[n, p, i] = wire.start(src, dst, chip_partner(bit))
+        yield
+    for n in range(len(chunks)):
+        dot(0, 1, n)
+    for n, (start, width) in enumerate(chunks):
+        cols = slice(start, start + width)
+        for p, at, _, other in halves:
+            sent[n, p, 1].wait_recv()
+
+            def add(_, cols, p=p, at=at, other=other):
+                both = part[other, at, cols].astype(F32) + first[p, 1, :, cols].astype(F32)
+                part[other, at, cols] = both.astype(BF16)
+
+            over_tiles(width, add, start)
+            src, dst = part.at[other, at, cols], second.at[p, :, cols]
+            later[n, p] = wire.start(src, dst, chip_partner(other))
+        yield
+    for n, (start, width) in enumerate(chunks):
+        for p, at, _, _ in halves:
+            sent[n, p, 0].wait_recv()
+            later[n, p].wait_recv()
+
+            def finish(_, cols, p=p, at=at):
+                both = part[0, at, cols].astype(F32) + first[p, 0, :, cols].astype(F32)
+                summed[at, cols] = both + second[p, :, cols].astype(F32)
+
+            over_tiles(width, finish, start)
+    for copy in list(sent.values()) + list(later.values()):
+        copy.wait_send()
+
+
+def chip_gather(wire, out):
+    _, rows, width = out.shape
+    low = width // 2 // 128 * 128
+    ranges = [slice(0, low), slice(low, width)]
+    near, far, last = {}, [], []
+    for n, cols in enumerate(ranges):
+        for p, at, bit, other in pieces(rows):
+            src = out.at[0, at, cols]
+            near[n, p] = wire.start(src, out.at[bit, at, cols], chip_partner(bit))
+            far.append(wire.start(src, out.at[other, at, cols], chip_partner(other)))
     yield
-    for p, at, _, other in pieces(rows):
-        sent[2 * p + 1].wait_recv()
-
-        def add(cols, _, p=p, at=at, other=other):
-            both = part[other, at, cols].astype(F32) + first[p, 1, :, cols].astype(F32)
-            part[other, at, cols] = both.astype(BF16)
-
-        over_tiles(width, add)
-        later.append(wire.start(part.at[other, at], second.at[p], chip_partner(other)))
-    yield
-    for p, at, _, _ in pieces(rows):
-        sent[2 * p].wait_recv()
-        later[p].wait_recv()
-
-        def finish(cols, _, p=p, at=at):
-            both = part[0, at, cols].astype(F32) + first[p, 0, :, cols].astype(F32)
-            summed[at, cols] = both + second[p, :, cols].astype(F32)
-
-        over_tiles(width, finish)
-    for copy in sent + later:
-        copy.wait_send()
-
-
-def chip_gather(wire, slots, rows):
-    near, far, last = [], [], []
-    for _, at, bit, other in pieces(rows):
-        near.append(wire.start(slots[0].at[at], slots[bit].at[at], chip_partner(bit)))
-        far.append(wire.start(slots[0].at[at], slots[other].at[at], chip_partner(other)))
-    yield
-    for p, at, bit, other in pieces(rows):
-        near[p].wait_recv()
-        last.append(wire.start(slots[bit].at[at], slots[3].at[at], chip_partner(other)))
-    yield
+    for n, cols in enumerate(ranges):
+        for p, at, bit, other in pieces(rows):
+            near[n, p].wait_recv()
+            src, dst = out.at[bit, at, cols], out.at[3, at, cols]
+            last.append(wire.start(src, dst, chip_partner(other)))
+        yield
     for copy in far + last:
         copy.wait_recv()
-    for copy in near + far + last:
+    for copy in list(near.values()) + far + last:
         copy.wait_send()
 
 
@@ -673,54 +703,6 @@
     ]
 
 
-class GatherDp:
-    partners = [("dp", 1), ("dp", 2), ("core", 1)]
-    copies = 7
-    flops = 0
-
-    def __init__(self, x):
-        self.args, self.rows = (x,), x.shape[0]
-        self.outs = (jax.ShapeDtypeStruct((4, 2) + x.shape, BF16),)
-        self.scratch = []
-
-    def run(self, wire, args, outs, scratch):
-        (out,) = outs
-        out[0, 0] = args[0][...]
-        yield from chip_gather(wire, [out.at[rel, 0] for rel in range(4)], self.rows)
-        swap = wire.start(out.at[:, 0], out.at[:, 1], core_partner())
-        yield
-        swap.wait_recv()
-        swap.wait_send()
-
-
-class ScatterDp:
-    partners = GatherDp.partners
-    copies = 7
-    flops = 0
-
-    def __init__(self, own, other):
-        self.args = (own, other)
-        shape = own.shape[1:]
-        self.outs = (jax.ShapeDtypeStruct(shape, F32),)
-        self.scratch = [pltpu.VMEM(own.shape, BF16)] + chip_scratch(*shape)
-
-    def run(self, wire, args, outs, scratch):
-        own, other = args
-        swapped, part, first, second = scratch
-        swap = wire.start(other, swapped, core_partner())
-        yield
-        swap.wait_recv()
-        for rel in range(4):
-
-            def add(cols, _, rel=rel):
-                both = own[rel, :, cols].astype(F32) + swapped[rel, :, cols].astype(F32)
-                part[rel, :, cols] = both.astype(BF16)
-
-            over_tiles(own.shape[2], add)
-        yield from chip_sum(wire, part, first, second, outs[0])
-        swap.wait_send()
-
-
 def tensor_sum(weight, x, w, by_cols, wire, scratch):
     part, first, second, summed = scratch
     rows, width = summed.shape
@@ -735,14 +717,14 @@
             for z in range(4):
                 part[z, c * r : (c + 1) * r, to] = low[c * rows + z * r : c * rows + z * r + r]
 
-    weight.times(left, w, by_cols, store)
     half = width // 2
     halves = [slice(h * half, (h + 1) * half) for h in range(2)]
     sent, later = [], []
-    for h in halves:
+    for n, h in enumerate(halves):
+        weight.times(left, w, by_cols, store, n)
         for i, z in ((1, 3), (0, 1)):
             sent.append(wire.start(part.at[z, :, h], first.at[i, :, h], z_partner(1)))
-    yield
+        yield
     for n, h in enumerate(halves):
         sent[2 * n].wait_recv()
 
@@ -752,7 +734,7 @@
 
         over_tiles(half, add, n * half)
         later.append(wire.start(part.at[2, :, h], second.at[:, h], z_partner(2)))
-    yield
+        yield
     for n in range(2):
         sent[2 * n + 1].wait_recv()
         later[n].wait_recv()
@@ -1007,6 +989,8 @@
 
 
 class Spread:
+    every = 2
+
     partners = [("tensor", 1), ("tensor", 2), ("dp", 1), ("dp", 2), ("dp", 3), ("core", 1)]
     copies = 7
     flops = 0
@@ -1037,6 +1021,8 @@
 
 
 class Collect:
+    every = 2
+
     partners = Spread.partners
     copies = 7
     flops = 0
@@ -1128,6 +1114,45 @@
         gathered[lax.axis_index("tensor")] = ((base[...] + summed) * valid[...]).astype(BF16)
         yield from tensor_gather(wire, *true_slots(gathered))
         for copy in sent:
+            copy.wait_send()
+
+
+class SmallSum:
+    partners = [("tensor", 1), ("tensor", 2), ("tensor", 3)]
+    partners += [("dp", 1), ("dp", 2), ("dp", 3), ("core", 1)]
+    copies = 7
+    flops = 0
+
+    def __init__(self, x, rows_all):
+        self.args, self.rows_all = (x,), rows_all
+        self.outs = (jax.ShapeDtypeStruct(x.shape, F32),)
+        self.scratch = [pltpu.VMEM(x.shape, F32)] * 3
+        self.scratch += [pltpu.VMEM((3,) + x.shape, F32), pltpu.VMEM((3, rows_all, 128), F32)]
+
+    def run(self, wire, args, outs, scratch):
+        (x,), (out,) = args, outs
+        from_core, mine, whole, from_chips, from_z = scratch
+        top = slice(0, self.rows_all)
+        swap = wire.start(x, from_core, core_partner())
+        yield
+        swap.wait_recv()
+        mine[...] = x[...] + from_core[...]
+        sent = [
+            wire.start(mine, from_chips.at[rel - 1], chip_partner(rel)) for rel in range(1, 4)
+        ]
+        yield
+        for copy in sent:
+            copy.wait_recv()
+        whole[...] = total([mine[...]] + [from_chips[i] for i in range(3)])
+        more = [
+            wire.start(whole.at[top], from_z.at[rel - 1], z_partner(rel)) for rel in range(1, 4)
+        ]
+        yield
+        for copy in more:
+            copy.wait_recv()
+        out[...] = whole[...]
+        out[top] = total([whole[top]] + [from_z[i] for i in range(3)])
+        for copy in [swap] + sent + more:
             copy.wait_send()
 
 
@@ -1282,14 +1307,19 @@
             )
         pl.semaphore_wait(barrier, len(partners))
         running = [
-            g.run(wire, a, o, s) for g, wire, a, o, s in zip(groups, wires, args, outs, scratch)
+            (g, g.run(wire, a, o, s))
+            for g, wire, a, o, s in zip(groups, wires, args, outs, scratch)
         ]
+        turn = 0
         while running:
             left = []
-            for run in running:
-                if next(run, running) is not running:
-                    left.append(run)
+            slow_alone = all(getattr(g, "every", 1) > 1 for g, _ in running)
+            for g, run in running:
+                waits = turn % getattr(g, "every", 1) and not slow_alone
+                if waits or next(run, running) is not running:
+                    left.append((g, run))
             running = left
+            turn += 1
 
     args = [x for g in groups for x in g.args]
     outs = [x for g in groups for x in g.outs]
@@ -1940,16 +1970,32 @@
         begun = grad_in
         grad_in = grad_in if done is None else after(grad_in, done)
         grad_in = lax.psum_scatter(grad_in, "dp", scatter_dimension=1, tiled=True)
-        grad_mout = dotl("tn,ti->ni", both(lambda m: m.grad_low), both(lambda m: m.gated_norm))
-        grad_mout = grad_mout if done is None else after(grad_mout, done)
-        grad_mout = lax.psum_scatter(grad_mout, "dp", scatter_dimension=0, tiled=True)
         grad_bc = dotl("td,tn->dn", both(lambda m: m.ssm_in_z), both(lambda m: m.state_low))
         grad_dt = dotl("td,tn->dn", ssm_in, both(lambda m: m.step_low))
         grad_small = jnp.concatenate([grad_bc, grad_dt], axis=1)
         grad_small = lax.psum_scatter(grad_small, "dp", scatter_dimension=0, tiled=True)
         grad_up = dotl("ra,rn->an", both(lambda m: m.adapter), both(lambda m: m.gate_up_own))
         grad_up = lax.psum_scatter(grad_up, "dp", scatter_dimension=0, tiled=True)
-        return begun, grad_in, grad_mout, grad_small, grad_up
+        return begun, grad_in, grad_small, grad_up
+
+    def mout_grad(done=None):
+        grad_mout = dotl("tn,ti->ni", both(lambda m: m.grad_low), both(lambda m: m.gated_norm))
+        grad_mout = grad_mout if done is None else after(grad_mout, done)
+        grad_mout = lax.psum_scatter(grad_mout, "dp", scatter_dimension=0, tiled=True)
+        return grad_mout
+
+    def lines(values):
+        flat = jnp.concatenate([v.reshape(-1) for v in values])
+        return jnp.pad(flat, (0, -flat.size % 1024)).reshape(-1, 128)
+
+    def small_terms():
+        sums = [jax.tree.map(lambda *v: total(v), *[m.sums_all for m in micro])]
+        sums += [jax.tree.map(lambda *v: total(v), *[m.sums_dp for m in micro])]
+        return [lines(values) for values in sums]
+
+    def tensor_terms():
+        terms = [grad_cols[:, 2 * units :].astype(BF16), grad_small[:, :state_cols]]
+        return jnp.concatenate([v.reshape(-1, HEAD) for v in terms], 0)
 
     def weight_grad(name):
         _, a, b, by_rows, parts = WEIGHT_GRADS[name]
@@ -1978,11 +2024,22 @@
         fused(links, w, 7, (*FEED_BACK, a), (*SETTLE, b), outputs)
         collect = (lambda *_: Collect(*projection_grads(links, micro)), lambda _, got: setattr(w, "grad_proj", got[0]), None)
         fused(links, w, 8, (*FEED_BACK_OUT, a), (*FEED_BACK, b))
-        fused(links, w, 9, (*FEED_BACK_OUT, b), (*ATTEND_BACK, a), weight_grad("gate_up"))
-        fused(links, w, 10, (*LEAVE, a), (*ATTEND_BACK, b), weight_grad("down"))
-        mixed = mixer_grads(b.d_qkv)
-        fused(links, w, 11, (*LEAVE, b), weight_grad("qkv"), weight_grad("out"), collect)
-        grad_down, grad_cols, grad_out = w.grad_down, w.grad_gate_up, w.grad_out
+        terms = small_terms()
+        rows_all = terms[0].shape[0]
+        sums = (
+            lambda *_: SmallSum(jnp.concatenate(terms, 0), rows_all),
+            lambda _, got: setattr(w, "flat", got[0]),
+            None,
+        )
+        fused(links, w, 9, (*FEED_BACK_OUT, b), (*ATTEND_BACK, a), weight_grad("gate_up"), sums)
+        flat, grad_cols = w.flat, w.grad_gate_up
+        fused(links, w, 10, (*LEAVE, a), (*ATTEND_BACK, b), weight_grad("down"), collect)
+        grad_mout = mout_grad(b.d_qkv)
+        _, grad_in, grad_small, grad_up = mixer_grads(b.d_qkv)
+
+        fused(links, w, 11, (*LEAVE, b), weight_grad("qkv"), weight_grad("out"))
+        whole_t = links.z_sum(tensor_terms())
+        grad_down, grad_out = w.grad_down, w.grad_out
         grad_qkv = w.grad_qkv.transpose(1, 0, 2)
         grad_proj = w.grad_proj
         for m in micro:
@@ -2007,6 +2064,7 @@
         results = finish_output(links, micro)
         grad_proj = proj_collect(links, *projection_grads(links, micro))
         mixed = mixer_grads()
+        grad_mout = mout_grad()
 
         def grad(name, axis):
             spec, a, b = WEIGHT_GRADS[name][:3]
@@ -2015,17 +2073,18 @@
 
         grad_down, grad_cols, grad_out = grad("down", 1), grad("gate_up", 0), grad("out", 1)
         grad_qkv = jnp.stack(jnp.split(grad("qkv", 0), 3, axis=1), 1)
-    _, grad_in, grad_mout, grad_small, grad_up = mixed
-    sums_dp = jax.tree.map(lambda *v: total(v), *[m.sums_dp for m in micro])
-    sums_all = jax.tree.map(lambda *v: total(v), *[m.sums_all for m in micro])
-    flat_all = links.z_sum(jnp.concatenate([v.reshape(-1) for v in sums_all]))
-    flat = links.dp_sum(jnp.concatenate([v.reshape(-1) for v in sums_dp] + [flat_all]))
-    small_sums = []
-    for v in sums_dp + sums_all:
-        small_sums.append(flat[: v.size].reshape(v.shape))
-        flat = flat[v.size :]
+        _, grad_in, grad_small, grad_up = mixed
+        flat_all, flat_dp = small_terms()
+        rows_all = flat_all.shape[0]
+        flat = links.dp_sum(jnp.concatenate([links.z_sum(flat_all), flat_dp], 0))
+        whole_t = links.z_sum(tensor_terms())
+    small_sums, flat = [], flat.reshape(-1)
+    for start, parts in ((0, micro[0].sums_all), (rows_all * 128, micro[0].sums_dp)):
+        for v in parts:
+            small_sums.append(flat[start : start + v.size].reshape(v.shape))
+            start += v.size
     own_gain = mixer_gain.shape[0]
-    grad_g_mamba = lax.dynamic_slice_in_dim(small_sums[6], links.d * own_gain, own_gain)
+    grad_g_mamba = lax.dynamic_slice_in_dim(small_sums[1], links.d * own_gain, own_gain)
 
     g_rows = total([jnp.stack([m.grad_g_attn, m.grad_g_mlp], 0) for m in micro])
     half = g_rows.shape[1] // 2
@@ -2033,12 +2092,9 @@
     g_rows = links.z_sum(g_rows)
 
     grad_gate_up = jnp.stack([grad_cols[:, :units], grad_cols[:, units : 2 * units]], 1)
-    partial_t = [grad_cols[:, 2 * units :].astype(BF16), grad_small[:, :state_cols]]
-    sizes = [v.size for v in partial_t]
-    whole_t = links.z_sum(jnp.concatenate([v.reshape(-1, HEAD) for v in partial_t], 0))
-    split = sizes[0] // HEAD
-    grad_adapter_down = whole_t[:split].reshape(partial_t[0].shape).astype(F32)
-    grad_bc = whole_t[split:].reshape(partial_t[1].shape).astype(F32)
+    split = grad_cols.shape[0] * (grad_cols.shape[1] - 2 * units) // HEAD
+    grad_adapter_down = whole_t[:split].reshape(grad_cols.shape[0], -1).astype(F32)
+    grad_bc = whole_t[split:].reshape(-1, state_cols).astype(F32)
 
     return (
         results,
@@ -2058,12 +2114,12 @@
         grad_bc,
         grad_small[:, state_cols:].astype(F32),
         grad_mout.T.astype(F32),
+        small_sums[2],
         small_sums[0],
+        small_sums[4],
         small_sums[5],
-        small_sums[2],
+        small_sums[6],
         small_sums[3],
-        small_sums[4],
-        small_sums[1],
     )
 
 

time: 1180 us -> 1070 us (0.907)
  Pallas kernels: 911 us -> 821 us
  starting transfers between devices: 32 us -> 19.3 us
    pallas_call x11, Pallas kernels: 898 us -> 807 us  [together(): pl.pallas_call(kernel, out_shape=outs, in_specs=[pl.BlockSpec(memory_spac...]
    unnamed x177 -> x179, local copies, waits for them, and re-layouts: 33.4 us -> 34.2 us
  transfers between devices with their start and end apart: 33 -> 26, of which waited for: 8 -> 5; matrix products, arithmetic and copies ran while one was open for 10% -> 11% of each run, Pallas kernels for 56% -> 55%
where the time goes in v4:
time: 1070 us; the launch traced here: 1060 us
  Pallas kernels  821 us (77%)
  local copies, waits for them, and re-layouts  86.1 us (8%)
  matrix products  54.3 us (5%)
  other arithmetic  45.8 us (4%)
  waiting for transfers between devices  19.5 us (2%)
  starting transfers between devices  19.3 us (2%)
  between operations  17.7 us (2%)
    pallas_call x11, Pallas kernels, together(): pl.pallas_call(kernel, out_shape=outs, in_specs=[pl.BlockSpec(memory_spac...  807 us
    dot_general x13, matrix products, dotf(): return jnp.einsum(spec, a, b, preferred_element_type=F32)  34.8 us
    unnamed x179, local copies, waits for them, and re-layouts  34.2 us
  transfers between devices with their start and end apart: 26, of which 5 were waited for; matrix products, arithmetic and copies ran while one was open for 11% of the time, Pallas kernels for 55%

profile of v4, /device:TPU:0, one launch (start us, length us, event | category | flops | bytes accessed | tf_op | source)
XLA Modules:
  0.0 1063.5 jit_solution(15293256409300192047)
XLA Ops:
  11.9 2.6 fusion.91
  16.9 22.3 %shard_map.407 = (bf16[4,128,1024]{2,1,0:T(8,128)(2,1)}, f32[128,1024]{1,0:T(8,128)}, f32[128,1]{1,0:T(8,128)}) custom-call(bf16[128,2048]{1,0:T(8,128)(2,1)} %get-tuple-element.327.refs_0_, bf16[128,2048]{1,0:T(8,128)(2,1)} %get-tuple-element.333.refs_1_, f32[1,1024]{1,0:T(1,128)} %get-tuple-element.370.refs_2_.refs_9_.refs_5_), custom_call_target="tpu_custom_call" | custom-call | bytes 2626048 | tf_op jit(solution)/shard_map/pallas_call | solution.py:1330
  39.3 89.7 %shard_map.408 = (bf16[4,128,1024]{2,1,0:T(8,128)(2,1)}, bf16[128,3072]{1,0:T(8,128)(2,1)}, bf16[4,2,1024,256]{3,2,1,0:T(8,128)(2,1)}, bf16[4,128,1024]{2,1,0:T(...) custom-call(bf16[4,128,1024]{2,1,0:T(8,128)(2,1)} %get-tuple-element.105.refs_0_.refs_8_, ...), custom_call_target="tpu_custom_call" | custom-call | flops 3221225472 | bytes 16716288 | tf_op jit(solution)/shard_map/pallas_call | solution.py:1330
  136.9 9.3 fusion.89
  146.2 2.6 copy_bitcast_fusion
  158.6 74.4 %shard_map.409 = (bf16[4,4,32,1024]{3,2,1,0:T(8,128)(2,1)}, f32[128,1024]{1,0:T(8,128)}, f32[128,1]{1,0:T(8,128)}, bf16[4,128,1024]{2,1,0:T(8,128)(2,1)}, bf16[128,3072]{1,0:T(8,128)(2,1)}) custom-call(bf16[4,128,1024]{2,1,0:T(8,128)(2,1)} %get-tuple-element.106.refs_0_.refs_12_, bf16[1024,512]{1,0:T(8,128)(2,1)} %refs_9_.1, ...), custom_call_target="tpu_custom_call" | custom-call | flops 4294967296 | bytes 14619136 | tf_op jit(solution)/shard_map/pallas_call | solution.py:1330
  233.0 110.0 %shard_map.410 = (bf16[4,128,2048]{2,1,0:T(8,128)(2,1)}, f32[128,4096]{1,0:T(8,128)}, bf16[128,128]{1,0:T(8,128)(2,1)}, bf16[4,4,32,1024]{3,2,1,0:T(8,128)(2,1)}, f32[128,1024]{1,0:T(8,128)}, /*index=5*/f32[128,1]{1,0:T(8,128)}) custom-call(bf16[4,128,1024]{2,1,0:T(8,128)(2,1)} %bitcast.258, bf16[512,4224]{1,0:T(8,128)(2,1)} %pad_maximum_fusion.1.refs_1_, ...), custom_call_target="tpu_custom_call" | custom-call | flops 5502926848 | bytes 20222464 | tf_op jit(solution)/shard_map/pallas_call | solution.py:1330
  343.0 72.0 %shard_map.411 = (bf16[4,128,2048]{2,1,0:T(8,128)(2,1)}, f32[128,4096]{1,0:T(8,128)}, bf16[128,128]{1,0:T(8,128)(2,1)}, bf16[128,1024]{1,0:T(8,128)(2,1)}, bf16[...) custom-call(bf16[4,128,1024]{2,1,0:T(8,128)(2,1)} %bitcast.260, bf16[512,4224]{1,0:T(8,128)(2,1)} %pad_maximum_fusion.1.refs_1_, ...), custom_call_target="tpu_custom_call" | custom-call | flops 6576668672 | bytes 26902528 | tf_op jit(solution)/shard_map/pallas_call | solution.py:1330
  424.1 4.5 broadcast_multiply_fusion.1
  428.7 6.4 convolution_bitcast_fusion.4.gate_ref
  445.9 4.9 mix_micro0.3
  453.7 63.8 %shard_map.412 = (bf16[128,1024]{1,0:T(8,128)(2,1)}, bf16[4,32,2048]{2,1,0:T(8,128)(2,1)}, bf16[32,2048]{1,0:T(8,128)(2,1)}, bf16[4,4,32,1024]{3,2,1,0:T(8,128)(...) custom-call(bf16[4,128,2048]{2,1,0:T(8,128)(2,1)} %get-tuple-element, ...), custom_call_target="tpu_custom_call" | custom-call | flops 3221225472 | bytes 20545536 | tf_op jit(solution)/shard_map/pallas_call | solution.py:1330
  520.4 6.5 convolution_bitcast_fusion.3.gate_ref
  527.5 3.0 multiply_reduce_fusion.3
  532.1 3.2 collective-permute-start.10
  537.9 3.0 convolution_convert_fusion.3
  550.5 5.3 mix_micro1.3
  557.5 4.7 convolution_bitcast_fusion
  568.5 67.3 %shard_map.413 = (bf16[4,128,4224]{2,1,0:T(8,128)(2,1)}, bf16[4,4,32,1024]{3,2,1,0:T(8,128)(2,1)}, bf16[4,32,2048]{2,1,0:T(8,128)(2,1)}, f32[32,2048]{1,0:T(8,12...) custom-call(bf16[4,128,1024]{2,1,0:T(8,128)(2,1)} %bitcast.218, ...), custom_call_target="tpu_custom_call" | custom-call | flops 3221225472 | bytes 23953664 | tf_op jit(solution)/shard_map/pallas_call | solution.py:1330
  646.2 54.8 %shard_map.414 = (bf16[4,4,32,1024]{3,2,1,0:T(8,128)(2,1)}, f32[128,1024]{1,0:T(8,128)}, f32[1,1024]{1,0:T(1,128)}, bf16[4,128,4224]{2,1,0:T(8,128)(2,1)}) custom-call(bf16[4,128,4224]{2,1,0:T(8,128)(2,1)} %get-tuple-element.135.refs_0_.refs_16_, bf16[512,4224]{1,0:T(8,128)(2,1)} %pad_maximum_fusion.1.refs_1_, ...), custom_call_target="tpu_custom_call" | custom-call | flops 6576668672 | bytes 28320256 | tf_op jit(solution)/shard_map/pallas_call | solution.py:1330
  703.0 2.7 convolution_convert_fusion
  705.7 2.8 convolution_bitcast_fusion.2.refs_19_
  710.6 81.3 %shard_map.415 = (bf16[4,4,32,1024]{3,2,1,0:T(8,128)(2,1)}, f32[128,1024]{1,0:T(8,128)}, f32[1,1024]{1,0:T(1,128)}, bf16[4,128,3072]{2,1,0:T(8,128)(2,1)}, f32[512,4224]{1,0:T(8,128)}, /*index=5*/f32[72,128]{1,0:T(8,128)}) custom-call(bf16[4,128,4224]{2,1,0:T(8,128)(2,1)} %get-tuple-element.140.refs_0_.refs_17_, ...), custom_call_target="tpu_custom_call" | custom-call | flops 9932111872 | bytes 42353152 | tf_op jit(solution)/shard_map/pallas_call | solution.py:1330
  791.9 108.6 %shard_map.416 = (f32[1,1024]{1,0:T(1,128)}, bf16[4,32,4096]{2,1,0:T(8,128)(2,1)}, bf16[4,128,3072]{2,1,0:T(8,128)(2,1)}, f32[2048,512]{1,0:T(8,128)}, f32[1024,256]{1,0:T(8,128)}) custom-call(bf16[4,128,3072]{2,1,0:T(8,128)(2,1)} %get-tuple-element.157.refs_0_.refs_10_, bf16[3,512,1024]{2,1,0:T(8,128)(2,1)} %bitcast.223, ...), custom_call_target="tpu_custom_call" | custom-call | flops 6442450944 | bytes 37167616 | tf_op jit(solution)/shard_map/pallas_call | solution.py:1330
  902.5 4.4 convert_add_fusion
  908.1 5.8 add_bitcast_fusion
  915.8 63.2 %shard_map.417 = (f32[1,1024]{1,0:T(1,128)}, bf16[4,32,4096]{2,1,0:T(8,128)(2,1)}, f32[3,512,1024]{2,1,0:T(8,128)}, f32[1024,512]{1,0:T(8,128)}) custom-call(bf16[4,128,3072]{2,1,0:T(8,128)(2,1)} %get-tuple-element.168.refs_0_.refs_11_, bf16[3,512,1024]{2,1,0:T(8,128)(2,1)} %bitcast.224, bf16[3,512,1024]{2,1,0:T(8,128)(2,1)} %collective-permute-done.1.refs_2_.refs_7_, ...), custom_call_target="tpu_custom_call" | custom-call | flops 7516192768 | bytes 33038848 | tf_op jit(solution)/shard_map/pallas_call | solution.py:1330
  983.3 4.0 slice_bitcast_fusion.1
  996.2 11.3 %copy.205 = f32[512,2,2048]{2,1,0:T(2,128)} copy(f32[512,2,2048]{2,0,1:T(8,128)S(1)} %pad_maximum_fusion) | data formatting | bytes 16777216
  1018.7 3.0 collective-permute-done.17
  1021.7 13.9 %collective-permute-done.16 = bf16[1024,128]{1,0:T(8,128)(2,1)S(1)} collective-permute-done((bf16[1024,128]{1,0:T(8,128)(2,1)S(1)}, bf16[1024,128]{1,0:T(8,128)(2,1)S(1)}, u32[]{:S(2)}, u32[]{:S(2)}) %collective-permute-start.16) | collective-permute-done | bytes 262176 | tf_op jit(solution)/shard_map/ppermute | solution.py:314
  1043.4 6.8 copy.237
  (395 shorter events, 127.5 us)
Async XLA Ops:
  7.2 225.8 %all-gather.5.cloned.1.call-start = ((), (), s32[]{:S(2)}) async-start(), calls=%async_computation.4 | async-start | bytes 1179648 | tf_op jit(solution)/shard_map/all_gather | solution.py:1949
  8.7 7.6 collective-permute-start
  9.2 30.0 %collective-permute-start.1 = (bf16[3,512,1024]{2,1,0:T(8,128)(2,1)}, bf16[3,512,1024]{2,1,0:T(8,128)(2,1)}, u32[]{:S(2)}, u32[]{:S(2)}) collective-permute-start(bf16[3,512,1024]{2,1,0:T(8,128)(2,1)} %bitcast.220), channel_id=1, source_target_pairs={{0,4},{4,0},{8,12},{12,8},{16,20},{20,16},{24,28},{28,24},{1,5},{5... | collective-permute-start | bytes 9437192 | tf_op jit(solution)/shard_map/ppermute | solution.py:308
  39.3 92.5 %copy-start.77 = (bf16[256]{0:T(256)(128)(2,1)S(1)}, bf16[256]{0:T(256)(128)(2,1)}, u32[]{:S(2)}) copy-start(bf16[256]{0:T(256)(128)(2,1)} %param.36) | copy-start | bytes 1540
  39.3 92.6 %copy-start.69 = (bf16[256,16]{0,1:T(8,128)(2,1)S(1)}, bf16[256,16]{0,1:T(8,128)(2,1)}, u32[]{:S(2)}) copy-start(bf16[256,16]{0,1:T(8,128)(2,1)} %param.39) | copy-start | bytes 24580
  39.3 94.5 %copy-start.48 = (bf16[1024,256]{1,0:T(8,128)(2,1)S(1)}, bf16[1024,256]{1,0:T(8,128)(2,1)}, u32[]{:S(2)}) copy-start(bf16[1024,256]{1,0:T(8,128)(2,1)} %param.40) | copy-start | bytes 1572868
  39.3 95.4 %copy-start.44 = (bf16[256,2,1024]{2,1,0:T(2,128)(2,1)S(1)}, bf16[256,2,1024]{2,1,0:T(2,128)(2,1)}, u32[]{:S(2)}) copy-start(bf16[256,2,1024]{2,1,0:T(2,128)(2,1)} %param.37) | copy-start | bytes 3145732
  131.7 286.5 %all-gather.9.cloned.1.call-start = ((), (), s32[]{:S(2)}) async-start(), calls=%async_computation.6 | async-start | bytes 1769472 | tf_op jit(solution)/shard_map/all_gather | solution.py:1950
  133.7 290.3 %all-gather.11.cloned.1.call-start = ((), (), s32[]{:S(2)}) async-start(), calls=%async_computation.7 | async-start | bytes 4718592 | tf_op jit(solution)/shard_map/all_gather | solution.py:1957
  134.6 294.1 %all-gather.7.cloned.1.call-start = ((), (), s32[]{:S(2)}) async-start(), calls=%async_computation.5 | async-start | bytes 9437184 | tf_op jit(solution)/shard_map/all_gather | solution.py:1955
  136.8 872.6 %reduce-scatter.5.cloned.1.call-start = ((), (), s32[]{:S(2)}) async-start(), calls=%async_computation.8 | async-start | bytes 1253376 | tf_op jit(solution)/shard_map/reduce_scatter | solution.py:1976
  151.1 81.8 %collective-permute-start.3 = (bf16[512,4224]{1,0:T(8,128)(2,1)}, bf16[512,4224]{1,0:T(8,128)(2,1)}, u32[]{:S(2)}, u32[]{:S(2)}) collective-permute-start(bf16[512,4224]{1,0:T(8,128)(2,1)} %pad_maximum_fusion.1.refs_1_), channel_id=1, source_target_pairs={{0,4},{4,0},{8,12},{12,8},{16,20},{20,16},{24,28},{28,24},{1,5},{5... | collective-permute-start | bytes 12976136 | tf_op jit(solution)/shard_map/ppermute | solution.py:308
  151.1 7.4 collective-permute-start.2
  151.6 191.3 %collective-permute-start.4 = (bf16[2048,512]{1,0:T(8,128)(2,1)}, bf16[2048,512]{1,0:T(8,128)(2,1)}, u32[]{:S(2)}, u32[]{:S(2)}) collective-permute-start(bf16[2048,512]{1,0:T(8,128)(2,1)} %refs_8_.2), channel_id=1, source_target_pairs={{0,4},{4,0},{8,12},{12,8},{16,20},{20,16},{24,28},{28,24},{1,5},{5... | collective-permute-start | bytes 6291464 | tf_op jit(solution)/shard_map/ppermute | solution.py:308
  436.7 7.1 collective-permute-start.7
  438.7 5.5 collective-permute-start.6
  440.7 5.0 collective-permute-start.5
  532.1 16.7 %collective-permute-start.10 = (f32[128,2]{1,0:T(8,128)S(1)}, f32[128,2]{1,0:T(8,128)}, u32[]{:S(2)}, u32[]{:S(2)}) collective-permute-start(f32[128,2]{1,0:T(8,128)S(1)} %get-tuple-element.129), channel_id=1, source_target_pairs={{0,3},{1,2},{2,1},{3,0},{4,7},{5,6},{6,5},{7,4},{8,11},{9,10},{10,... | collective-permute-start | bytes 3080 | tf_op jit(solution)/shard_map/mix_micro1/ppermute | solution.py:314
  535.3 13.5 %collective-permute-start.9 = (f32[128,2]{1,0:T(8,128)S(1)}, f32[128,2]{1,0:T(8,128)}, u32[]{:S(2)}, u32[]{:S(2)}) collective-permute-start(f32[128,2]{1,0:T(8,128)S(1)} %get-tuple-element.129), channel_id=1, source_target_pairs={{0,2},{1,3},{2,0},{3,1},{4,6},{5,7},{6,4},{7,5},{8,10},{9,11},{10,... | collective-permute-start | bytes 3080 | tf_op jit(solution)/shard_map/mix_micro1/ppermute | solution.py:314
  535.3 13.5 %collective-permute-start.8 = (f32[128,2]{1,0:T(8,128)S(1)}, f32[128,2]{1,0:T(8,128)}, u32[]{:S(2)}, u32[]{:S(2)}) collective-permute-start(f32[128,2]{1,0:T(8,128)S(1)} %get-tuple-element.129), channel_id=1, source_target_pairs={{0,1},{1,0},{2,3},{3,2},{4,5},{5,4},{6,7},{7,6},{8,9},{9,8},{10,11... | collective-permute-start | bytes 3080 | tf_op jit(solution)/shard_map/mix_micro1/ppermute | solution.py:314
  642.5 373.1 %reduce-scatter.7.cloned.1.call-start = ((), (), s32[]{:S(2)}) async-start(), calls=%async_computation.9 | async-start | bytes 1179648 | tf_op jit(solution)/shard_map/reduce_scatter | solution.py:1978
  710.6 326.7 %reduce-scatter.11.cloned.1.call-start = ((), (), s32[]{:S(2)}) async-start(), calls=%async_computation.11 | async-start | bytes 4718592 | tf_op jit(solution)/shard_map/reduce_scatter | solution.py:1984
  791.9 110.6 %copy-start.28 = (bf16[128,2048]{1,0:T(8,128)(2,1)S(1)}, bf16[128,2048]{1,0:T(8,128)(2,1)}, u32[]{:S(2)}) copy-start(bf16[128,2048]{1,0:T(8,128)(2,1)} %get-tuple-element.330) | copy-start | bytes 1572868
  791.9 110.6 %copy-start.40 = (bf16[128,1024]{1,0:T(8,128)(2,1)S(1)}, bf16[128,1024]{1,0:T(8,128)(2,1)}, u32[]{:S(2)}) copy-start(bf16[128,1024]{1,0:T(8,128)(2,1)} %get-tuple-element.345) | copy-start | bytes 786436
  907.0 132.7 %reduce-scatter.9.cloned.1.call-start = ((), (), s32[]{:S(2)}) async-start(), calls=%async_computation.10 | async-start | bytes 9437184 | tf_op jit(solution)/shard_map/reduce_scatter | solution.py:1972
  979.7 9.4 collective-permute-start.11
  989.1 20.3 %collective-permute-start.14 = (f32[2,512]{1,0:T(2,128)S(1)}, f32[2,512]{1,0:T(2,128)S(1)}, u32[]{:S(2)}, u32[]{:S(2)}) collective-permute-start(f32[2,512]{1,0:T(2,128)S(1)} %slice_add_fusion), channel_id=1, source_target_pairs={{0,3},{1,2},{2,1},{3,0},{4,7},{5,6},{6,5},{7,4},{8,11},{9,10},{10,... | collective-permute-start | bytes 12296 | tf_op jit(solution)/shard_map/ppermute | solution.py:314
  991.0 18.3 %collective-permute-start.13 = (f32[2,512]{1,0:T(2,128)S(1)}, f32[2,512]{1,0:T(2,128)S(1)}, u32[]{:S(2)}, u32[]{:S(2)}) collective-permute-start(f32[2,512]{1,0:T(2,128)S(1)} %slice_add_fusion), channel_id=1, source_target_pairs={{0,2},{1,3},{2,0},{3,1},{4,6},{5,7},{6,4},{7,5},{8,10},{9,11},{10,... | collective-permute-start | bytes 12296 | tf_op jit(solution)/shard_map/ppermute | solution.py:314
  992.4 16.9 %collective-permute-start.12 = (f32[2,512]{1,0:T(2,128)S(1)}, f32[2,512]{1,0:T(2,128)S(1)}, u32[]{:S(2)}, u32[]{:S(2)}) collective-permute-start(f32[2,512]{1,0:T(2,128)S(1)} %slice_add_fusion), channel_id=1, source_target_pairs={{0,1},{1,0},{2,3},{3,2},{4,5},{5,4},{6,7},{7,6},{8,9},{9,8},{10,11... | collective-permute-start | bytes 12296 | tf_op jit(solution)/shard_map/ppermute | solution.py:314
  1010.5 11.2 %collective-permute-start.17 = (bf16[1024,128]{1,0:T(8,128)(2,1)S(1)}, bf16[1024,128]{1,0:T(8,128)(2,1)S(1)}, u32[]{:S(2)}, u32[]{:S(2)}) collective-permute-start(bf16[1024,128]{1,0:T(8,128)(2,1)S(1)} %pad_maximum_fusion.15), channel_id=1, source_target_pairs={{0,3},{1,2},{2,1},{3,0},{4,7},{5,6},{6,5},{7,4},{8,11},{9,10},{10,... | collective-permute-start | bytes 786440 | tf_op jit(solution)/shard_map/ppermute | solution.py:314
  1012.4 23.2 %collective-permute-start.16 = (bf16[1024,128]{1,0:T(8,128)(2,1)S(1)}, bf16[1024,128]{1,0:T(8,128)(2,1)S(1)}, u32[]{:S(2)}, u32[]{:S(2)}) collective-permute-start(bf16[1024,128]{1,0:T(8,128)(2,1)S(1)} %pad_maximum_fusion.15), channel_id=1, source_target_pairs={{0,2},{1,3},{2,0},{3,1},{4,6},{5,7},{6,4},{7,5},{8,10},{9,11},{10,... | collective-permute-start | bytes 786440 | tf_op jit(solution)/shard_map/ppermute | solution.py:314
  1012.9 22.7 %collective-permute-start.15 = (bf16[1024,128]{1,0:T(8,128)(2,1)S(1)}, bf16[1024,128]{1,0:T(8,128)(2,1)S(1)}, u32[]{:S(2)}, u32[]{:S(2)}) collective-permute-start(bf16[1024,128]{1,0:T(8,128)(2,1)S(1)} %pad_maximum_fusion.15), channel_id=1, source_target_pairs={{0,1},{1,0},{2,3},{3,2},{4,5},{5,4},{6,7},{7,6},{8,9},{9,8},{10,11... | collective-permute-start | bytes 786440 | tf_op jit(solution)/shard_map/ppermute | solution.py:314
  (77 other events, 986.2 us)
Sparse Core Ops, SparseCore 0:
  131.8 24.5 all-gather.4
  158.8 35.6 all-gather.8
  197.0 42.1 all-gather.10
  241.5 85.4 all-gather.6
  642.6 38.4 reduce-scatter.4
  710.7 35.3 reduce-scatter.6
  907.1 52.4 reduce-scatter.10
  963.5 70.8 reduce-scatter.8

commit v5 on v4

--- a/solution.py
+++ b/solution.py
@@ -948,13 +948,13 @@
         first, middle, second = scratch
         wide = self.wide
         d = lax.axis_index("dp")
-        sent = [wire.start(terms.at[z], first.at[i], z_partner(1)) for i, z in enumerate((1, 3))]
-        yield
-        sent[1].wait_recv()
+        sent = [wire.start(terms.at[z], first.at[i], z_partner(1)) for i, z in ((1, 3), (0, 1))]
+        yield
+        sent[0].wait_recv()
         middle[...] = (terms[2].astype(F32) + first[1].astype(F32)).astype(BF16)
         sent.append(wire.start(middle, second, z_partner(2)))
         yield
-        sent[0].wait_recv()
+        sent[1].wait_recv()
         sent[2].wait_recv()
         summed = terms[0].astype(F32) + first[0].astype(F32) + second[...].astype(F32)
         state[...] = summed[:, wide:].astype(BF16)
@@ -1059,9 +1059,9 @@
             copy.wait_recv()
         here = xor(lax.axis_index("dp") // 2, lax.axis_index("tensor"))
         at = [xor(here, z) for z in range(4)]
-        more = [wire.start(came.at[at[z]], first.at[i], z_partner(1)) for i, z in enumerate((1, 3))]
-        yield
-        more[1].wait_recv()
+        more = [wire.start(came.at[at[z]], first.at[i], z_partner(1)) for i, z in ((1, 3), (0, 1))]
+        yield
+        more[0].wait_recv()
 
         def middle(i, carry):
             to = pl.ds(pl.multiple_of(i * tile, tile), tile)
@@ -1072,7 +1072,7 @@
         lax.fori_loop(0, rows // tile, middle, 0)
         more.append(wire.start(swapped.at[0], second, z_partner(2)))
         yield
-        more[0].wait_recv()
+        more[1].wait_recv()
         more[2].wait_recv()
 
         def finish(i, carry):
@@ -1102,13 +1102,13 @@
         terms, base, valid = args
         (gathered,) = outs
         first, middle, second = scratch
-        sent = [wire.start(terms.at[z], first.at[i], z_partner(1)) for i, z in enumerate((1, 3))]
-        yield
-        sent[1].wait_recv()
+        sent = [wire.start(terms.at[z], first.at[i], z_partner(1)) for i, z in ((1, 3), (0, 1))]
+        yield
+        sent[0].wait_recv()
         middle[...] = (terms[2].astype(F32) + first[1].astype(F32)).astype(BF16)
         sent.append(wire.start(middle, second, z_partner(2)))
         yield
-        sent[0].wait_recv()
+        sent[1].wait_recv()
         sent[2].wait_recv()
         summed = terms[0].astype(F32) + first[0].astype(F32) + second[...].astype(F32)
         gathered[lax.axis_index("tensor")] = ((base[...] + summed) * valid[...]).astype(BF16)

time: 1070 us -> 1070 us (level)
  no operation moved by 1% of the time
where the time goes in v5:
time: 1070 us; the launch traced here: 1060 us
  Pallas kernels  823 us (77%)
  local copies, waits for them, and re-layouts  86.1 us (8%)
  matrix products  54.4 us (5%)
  other arithmetic  45.8 us (4%)
  starting transfers between devices  19.3 us (2%)
  waiting for transfers between devices  18.9 us (2%)
  between operations  17.7 us (2%)
    pallas_call x11, Pallas kernels, together(): pl.pallas_call(kernel, out_shape=outs, in_specs=[pl.BlockSpec(memory_spac...  809 us
    dot_general x13, matrix products, dotf(): return jnp.einsum(spec, a, b, preferred_element_type=F32)  34.8 us
    unnamed x179, local copies, waits for them, and re-layouts  34.2 us
  transfers between devices with their start and end apart: 26, of which 5 were waited for; matrix products, arithmetic and copies ran while one was open for 11% of the time, Pallas kernels for 55%

profile of v5, /device:TPU:0, one launch (start us, length us, event | category | flops | bytes accessed | tf_op | source)
XLA Modules:
  0.0 1064.9 jit_solution(17824986927296989675)
XLA Ops:
  16.9 22.3 %shard_map.407 = (bf16[4,128,1024]{2,1,0:T(8,128)(2,1)}, f32[128,1024]{1,0:T(8,128)}, f32[128,1]{1,0:T(8,128)}) custom-call(bf16[128,2048]{1,0:T(8,128)(2,1)} %get-tuple-element.327.refs_0_, bf16[128,2048]{1,0:T(8,128)(2,1)} %get-tuple-element.333.refs_1_, f32[1,1024]{1,0:T(1,128)} %get-tuple-element.370.refs_2_.refs_9_.refs_5_), custom_call_target="tpu_custom_call" | custom-call | bytes 2626048 | tf_op jit(solution)/shard_map/pallas_call | solution.py:1330
  39.3 89.7 %shard_map.408 = (bf16[4,128,1024]{2,1,0:T(8,128)(2,1)}, bf16[128,3072]{1,0:T(8,128)(2,1)}, bf16[4,2,1024,256]{3,2,1,0:T(8,128)(2,1)}, bf16[4,128,1024]{2,1,0:T(...) custom-call(bf16[4,128,1024]{2,1,0:T(8,128)(2,1)} %get-tuple-element.105.refs_0_.refs_8_, ...), custom_call_target="tpu_custom_call" | custom-call | flops 3221225472 | bytes 16716288 | tf_op jit(solution)/shard_map/pallas_call | solution.py:1330
  136.9 9.3 fusion.89
  158.6 74.4 %shard_map.409 = (bf16[4,4,32,1024]{3,2,1,0:T(8,128)(2,1)}, f32[128,1024]{1,0:T(8,128)}, f32[128,1]{1,0:T(8,128)}, bf16[4,128,1024]{2,1,0:T(8,128)(2,1)}, bf16[128,3072]{1,0:T(8,128)(2,1)}) custom-call(bf16[4,128,1024]{2,1,0:T(8,128)(2,1)} %get-tuple-element.106.refs_0_.refs_12_, bf16[1024,512]{1,0:T(8,128)(2,1)} %refs_9_.1, ...), custom_call_target="tpu_custom_call" | custom-call | flops 4294967296 | bytes 14619136 | tf_op jit(solution)/shard_map/pallas_call | solution.py:1330
  233.0 110.0 %shard_map.410 = (bf16[4,128,2048]{2,1,0:T(8,128)(2,1)}, f32[128,4096]{1,0:T(8,128)}, bf16[128,128]{1,0:T(8,128)(2,1)}, bf16[4,4,32,1024]{3,2,1,0:T(8,128)(2,1)}, f32[128,1024]{1,0:T(8,128)}, /*index=5*/f32[128,1]{1,0:T(8,128)}) custom-call(bf16[4,128,1024]{2,1,0:T(8,128)(2,1)} %bitcast.258, bf16[512,4224]{1,0:T(8,128)(2,1)} %pad_maximum_fusion.1.refs_1_, ...), custom_call_target="tpu_custom_call" | custom-call | flops 5502926848 | bytes 20222464 | tf_op jit(solution)/shard_map/pallas_call | solution.py:1330
  343.0 72.0 %shard_map.411 = (bf16[4,128,2048]{2,1,0:T(8,128)(2,1)}, f32[128,4096]{1,0:T(8,128)}, bf16[128,128]{1,0:T(8,128)(2,1)}, bf16[128,1024]{1,0:T(8,128)(2,1)}, bf16[...) custom-call(bf16[4,128,1024]{2,1,0:T(8,128)(2,1)} %bitcast.260, bf16[512,4224]{1,0:T(8,128)(2,1)} %pad_maximum_fusion.1.refs_1_, ...), custom_call_target="tpu_custom_call" | custom-call | flops 6576668672 | bytes 26902528 | tf_op jit(solution)/shard_map/pallas_call | solution.py:1330
  424.1 4.5 broadcast_multiply_fusion.1
  428.7 6.4 convolution_bitcast_fusion.4.gate_ref
  445.9 4.9 mix_micro0.3
  453.7 61.2 %shard_map.412 = (bf16[128,1024]{1,0:T(8,128)(2,1)}, bf16[4,32,2048]{2,1,0:T(8,128)(2,1)}, bf16[32,2048]{1,0:T(8,128)(2,1)}, bf16[4,4,32,1024]{3,2,1,0:T(8,128)(...) custom-call(bf16[4,128,2048]{2,1,0:T(8,128)(2,1)} %get-tuple-element, ...), custom_call_target="tpu_custom_call" | custom-call | flops 3221225472 | bytes 20545536 | tf_op jit(solution)/shard_map/pallas_call | solution.py:1330
  517.8 6.5 convolution_bitcast_fusion.3.gate_ref
  524.9 3.0 multiply_reduce_fusion.3
  529.5 2.7 collective-permute-start.10
  535.2 3.0 convolution_convert_fusion.3
  547.9 5.3 mix_micro1.3
  554.9 4.7 convolution_bitcast_fusion
  565.9 68.0 %shard_map.413 = (bf16[4,128,4224]{2,1,0:T(8,128)(2,1)}, bf16[4,4,32,1024]{3,2,1,0:T(8,128)(2,1)}, bf16[4,32,2048]{2,1,0:T(8,128)(2,1)}, f32[32,2048]{1,0:T(8,12...) custom-call(bf16[4,128,1024]{2,1,0:T(8,128)(2,1)} %bitcast.218, ...), custom_call_target="tpu_custom_call" | custom-call | flops 3221225472 | bytes 23953664 | tf_op jit(solution)/shard_map/pallas_call | solution.py:1330
  644.2 59.8 %shard_map.414 = (bf16[4,4,32,1024]{3,2,1,0:T(8,128)(2,1)}, f32[128,1024]{1,0:T(8,128)}, f32[1,1024]{1,0:T(1,128)}, bf16[4,128,4224]{2,1,0:T(8,128)(2,1)}) custom-call(bf16[4,128,4224]{2,1,0:T(8,128)(2,1)} %get-tuple-element.135.refs_0_.refs_16_, bf16[512,4224]{1,0:T(8,128)(2,1)} %pad_maximum_fusion.1.refs_1_, ...), custom_call_target="tpu_custom_call" | custom-call | flops 6576668672 | bytes 28320256 | tf_op jit(solution)/shard_map/pallas_call | solution.py:1330
  706.0 2.7 convolution_convert_fusion
  708.7 2.8 convolution_bitcast_fusion.2.refs_19_
  713.6 77.5 %shard_map.415 = (bf16[4,4,32,1024]{3,2,1,0:T(8,128)(2,1)}, f32[128,1024]{1,0:T(8,128)}, f32[1,1024]{1,0:T(1,128)}, bf16[4,128,3072]{2,1,0:T(8,128)(2,1)}, f32[512,4224]{1,0:T(8,128)}, /*index=5*/f32[72,128]{1,0:T(8,128)}) custom-call(bf16[4,128,4224]{2,1,0:T(8,128)(2,1)} %get-tuple-element.140.refs_0_.refs_17_, ...), custom_call_target="tpu_custom_call" | custom-call | flops 9932111872 | bytes 42353152 | tf_op jit(solution)/shard_map/pallas_call | solution.py:1330
  791.1 110.7 %shard_map.416 = (f32[1,1024]{1,0:T(1,128)}, bf16[4,32,4096]{2,1,0:T(8,128)(2,1)}, bf16[4,128,3072]{2,1,0:T(8,128)(2,1)}, f32[2048,512]{1,0:T(8,128)}, f32[1024,256]{1,0:T(8,128)}) custom-call(bf16[4,128,3072]{2,1,0:T(8,128)(2,1)} %get-tuple-element.157.refs_0_.refs_10_, bf16[3,512,1024]{2,1,0:T(8,128)(2,1)} %bitcast.223, ...), custom_call_target="tpu_custom_call" | custom-call | flops 6442450944 | bytes 37167616 | tf_op jit(solution)/shard_map/pallas_call | solution.py:1330
  903.8 4.4 convert_add_fusion
  909.4 6.0 add_bitcast_fusion
  917.2 63.8 %shard_map.417 = (f32[1,1024]{1,0:T(1,128)}, bf16[4,32,4096]{2,1,0:T(8,128)(2,1)}, f32[3,512,1024]{2,1,0:T(8,128)}, f32[1024,512]{1,0:T(8,128)}) custom-call(bf16[4,128,3072]{2,1,0:T(8,128)(2,1)} %get-tuple-element.168.refs_0_.refs_11_, bf16[3,512,1024]{2,1,0:T(8,128)(2,1)} %bitcast.224, bf16[3,512,1024]{2,1,0:T(8,128)(2,1)} %collective-permute-done.1.refs_2_.refs_7_, ...), custom_call_target="tpu_custom_call" | custom-call | flops 7516192768 | bytes 33038848 | tf_op jit(solution)/shard_map/pallas_call | solution.py:1330
  985.4 4.0 slice_bitcast_fusion.1
  992.8 2.7 collective-permute-start.12
  998.3 11.3 %copy.205 = f32[512,2,2048]{2,1,0:T(2,128)} copy(f32[512,2,2048]{2,0,1:T(8,128)S(1)} %pad_maximum_fusion) | data formatting | bytes 16777216
  1014.1 3.0 collective-permute-start.15
  1020.8 3.0 collective-permute-done.17
  1023.8 13.2 %collective-permute-done.16 = bf16[1024,128]{1,0:T(8,128)(2,1)S(1)} collective-permute-done((bf16[1024,128]{1,0:T(8,128)(2,1)S(1)}, bf16[1024,128]{1,0:T(8,128)(2,1)S(1)}, u32[]{:S(2)}, u32[]{:S(2)}) %collective-permute-start.16) | collective-permute-done | bytes 262176 | tf_op jit(solution)/shard_map/ppermute | solution.py:314
  1044.9 6.8 copy.237
  (395 shorter events, 127.6 us)
Async XLA Ops:
  7.2 225.8 %all-gather.5.cloned.1.call-start = ((), (), s32[]{:S(2)}) async-start(), calls=%async_computation.4 | async-start | bytes 1179648 | tf_op jit(solution)/shard_map/all_gather | solution.py:1949
  8.7 7.6 collective-permute-start
  9.2 30.0 %collective-permute-start.1 = (bf16[3,512,1024]{2,1,0:T(8,128)(2,1)}, bf16[3,512,1024]{2,1,0:T(8,128)(2,1)}, u32[]{:S(2)}, u32[]{:S(2)}) collective-permute-start(bf16[3,512,1024]{2,1,0:T(8,128)(2,1)} %bitcast.220), channel_id=1, source_target_pairs={{0,4},{4,0},{8,12},{12,8},{16,20},{20,16},{24,28},{28,24},{1,5},{5... | collective-permute-start | bytes 9437192 | tf_op jit(solution)/shard_map/ppermute | solution.py:308
  39.3 92.5 %copy-start.77 = (bf16[256]{0:T(256)(128)(2,1)S(1)}, bf16[256]{0:T(256)(128)(2,1)}, u32[]{:S(2)}) copy-start(bf16[256]{0:T(256)(128)(2,1)} %param.36) | copy-start | bytes 1540
  39.3 92.6 %copy-start.69 = (bf16[256,16]{0,1:T(8,128)(2,1)S(1)}, bf16[256,16]{0,1:T(8,128)(2,1)}, u32[]{:S(2)}) copy-start(bf16[256,16]{0,1:T(8,128)(2,1)} %param.39) | copy-start | bytes 24580
  39.3 94.5 %copy-start.48 = (bf16[1024,256]{1,0:T(8,128)(2,1)S(1)}, bf16[1024,256]{1,0:T(8,128)(2,1)}, u32[]{:S(2)}) copy-start(bf16[1024,256]{1,0:T(8,128)(2,1)} %param.40) | copy-start | bytes 1572868
  39.3 95.4 %copy-start.44 = (bf16[256,2,1024]{2,1,0:T(2,128)(2,1)S(1)}, bf16[256,2,1024]{2,1,0:T(2,128)(2,1)}, u32[]{:S(2)}) copy-start(bf16[256,2,1024]{2,1,0:T(2,128)(2,1)} %param.37) | copy-start | bytes 3145732
  131.7 286.5 %all-gather.9.cloned.1.call-start = ((), (), s32[]{:S(2)}) async-start(), calls=%async_computation.6 | async-start | bytes 1769472 | tf_op jit(solution)/shard_map/all_gather | solution.py:1950
  133.7 290.3 %all-gather.11.cloned.1.call-start = ((), (), s32[]{:S(2)}) async-start(), calls=%async_computation.7 | async-start | bytes 4718592 | tf_op jit(solution)/shard_map/all_gather | solution.py:1957
  134.6 294.1 %all-gather.7.cloned.1.call-start = ((), (), s32[]{:S(2)}) async-start(), calls=%async_computation.5 | async-start | bytes 9437184 | tf_op jit(solution)/shard_map/all_gather | solution.py:1955
  136.8 874.6 %reduce-scatter.5.cloned.1.call-start = ((), (), s32[]{:S(2)}) async-start(), calls=%async_computation.8 | async-start | bytes 1253376 | tf_op jit(solution)/shard_map/reduce_scatter | solution.py:1976
  151.1 81.8 %collective-permute-start.3 = (bf16[512,4224]{1,0:T(8,128)(2,1)}, bf16[512,4224]{1,0:T(8,128)(2,1)}, u32[]{:S(2)}, u32[]{:S(2)}) collective-permute-start(bf16[512,4224]{1,0:T(8,128)(2,1)} %pad_maximum_fusion.1.refs_1_), channel_id=1, source_target_pairs={{0,4},{4,0},{8,12},{12,8},{16,20},{20,16},{24,28},{28,24},{1,5},{5... | collective-permute-start | bytes 12976136 | tf_op jit(solution)/shard_map/ppermute | solution.py:308
  151.1 7.4 collective-permute-start.2
  151.6 191.3 %collective-permute-start.4 = (bf16[2048,512]{1,0:T(8,128)(2,1)}, bf16[2048,512]{1,0:T(8,128)(2,1)}, u32[]{:S(2)}, u32[]{:S(2)}) collective-permute-start(bf16[2048,512]{1,0:T(8,128)(2,1)} %refs_8_.2), channel_id=1, source_target_pairs={{0,4},{4,0},{8,12},{12,8},{16,20},{20,16},{24,28},{28,24},{1,5},{5... | collective-permute-start | bytes 6291464 | tf_op jit(solution)/shard_map/ppermute | solution.py:308
  436.7 7.1 collective-permute-start.7
  438.7 5.5 collective-permute-start.6
  440.7 5.0 collective-permute-start.5
  529.5 16.7 %collective-permute-start.10 = (f32[128,2]{1,0:T(8,128)S(1)}, f32[128,2]{1,0:T(8,128)}, u32[]{:S(2)}, u32[]{:S(2)}) collective-permute-start(f32[128,2]{1,0:T(8,128)S(1)} %get-tuple-element.129), channel_id=1, source_target_pairs={{0,3},{1,2},{2,1},{3,0},{4,7},{5,6},{6,5},{7,4},{8,11},{9,10},{10,... | collective-permute-start | bytes 3080 | tf_op jit(solution)/shard_map/mix_micro1/ppermute | solution.py:314
  532.2 14.0 %collective-permute-start.9 = (f32[128,2]{1,0:T(8,128)S(1)}, f32[128,2]{1,0:T(8,128)}, u32[]{:S(2)}, u32[]{:S(2)}) collective-permute-start(f32[128,2]{1,0:T(8,128)S(1)} %get-tuple-element.129), channel_id=1, source_target_pairs={{0,2},{1,3},{2,0},{3,1},{4,6},{5,7},{6,4},{7,5},{8,10},{9,11},{10,... | collective-permute-start | bytes 3080 | tf_op jit(solution)/shard_map/mix_micro1/ppermute | solution.py:314
  532.6 13.6 %collective-permute-start.8 = (f32[128,2]{1,0:T(8,128)S(1)}, f32[128,2]{1,0:T(8,128)}, u32[]{:S(2)}, u32[]{:S(2)}) collective-permute-start(f32[128,2]{1,0:T(8,128)S(1)} %get-tuple-element.129), channel_id=1, source_target_pairs={{0,1},{1,0},{2,3},{3,2},{4,5},{5,4},{6,7},{7,6},{8,9},{9,8},{10,11... | collective-permute-start | bytes 3080 | tf_op jit(solution)/shard_map/mix_micro1/ppermute | solution.py:314
  640.5 377.1 %reduce-scatter.7.cloned.1.call-start = ((), (), s32[]{:S(2)}) async-start(), calls=%async_computation.9 | async-start | bytes 1179648 | tf_op jit(solution)/shard_map/reduce_scatter | solution.py:1978
  713.6 325.1 %reduce-scatter.11.cloned.1.call-start = ((), (), s32[]{:S(2)}) async-start(), calls=%async_computation.11 | async-start | bytes 4718592 | tf_op jit(solution)/shard_map/reduce_scatter | solution.py:1984
  791.1 112.7 %copy-start.28 = (bf16[128,2048]{1,0:T(8,128)(2,1)S(1)}, bf16[128,2048]{1,0:T(8,128)(2,1)}, u32[]{:S(2)}) copy-start(bf16[128,2048]{1,0:T(8,128)(2,1)} %get-tuple-element.330) | copy-start | bytes 1572868
  791.1 112.7 %copy-start.40 = (bf16[128,1024]{1,0:T(8,128)(2,1)S(1)}, bf16[128,1024]{1,0:T(8,128)(2,1)}, u32[]{:S(2)}) copy-start(bf16[128,1024]{1,0:T(8,128)(2,1)} %get-tuple-element.345) | copy-start | bytes 786436
  908.3 132.9 %reduce-scatter.9.cloned.1.call-start = ((), (), s32[]{:S(2)}) async-start(), calls=%async_computation.10 | async-start | bytes 9437184 | tf_op jit(solution)/shard_map/reduce_scatter | solution.py:1972
  981.7 9.4 collective-permute-start.11
  991.1 20.3 %collective-permute-start.14 = (f32[2,512]{1,0:T(2,128)S(1)}, f32[2,512]{1,0:T(2,128)S(1)}, u32[]{:S(2)}, u32[]{:S(2)}) collective-permute-start(f32[2,512]{1,0:T(2,128)S(1)} %slice_add_fusion), channel_id=1, source_target_pairs={{0,3},{1,2},{2,1},{3,0},{4,7},{5,6},{6,5},{7,4},{8,11},{9,10},{10,... | collective-permute-start | bytes 12296 | tf_op jit(solution)/shard_map/ppermute | solution.py:314
  992.0 19.4 %collective-permute-start.13 = (f32[2,512]{1,0:T(2,128)S(1)}, f32[2,512]{1,0:T(2,128)S(1)}, u32[]{:S(2)}, u32[]{:S(2)}) collective-permute-start(f32[2,512]{1,0:T(2,128)S(1)} %slice_add_fusion), channel_id=1, source_target_pairs={{0,2},{1,3},{2,0},{3,1},{4,6},{5,7},{6,4},{7,5},{8,10},{9,11},{10,... | collective-permute-start | bytes 12296 | tf_op jit(solution)/shard_map/ppermute | solution.py:314
  992.8 18.6 %collective-permute-start.12 = (f32[2,512]{1,0:T(2,128)S(1)}, f32[2,512]{1,0:T(2,128)S(1)}, u32[]{:S(2)}, u32[]{:S(2)}) collective-permute-start(f32[2,512]{1,0:T(2,128)S(1)} %slice_add_fusion), channel_id=1, source_target_pairs={{0,1},{1,0},{2,3},{3,2},{4,5},{5,4},{6,7},{7,6},{8,9},{9,8},{10,11... | collective-permute-start | bytes 12296 | tf_op jit(solution)/shard_map/ppermute | solution.py:314
  1012.6 11.2 %collective-permute-start.17 = (bf16[1024,128]{1,0:T(8,128)(2,1)S(1)}, bf16[1024,128]{1,0:T(8,128)(2,1)S(1)}, u32[]{:S(2)}, u32[]{:S(2)}) collective-permute-start(bf16[1024,128]{1,0:T(8,128)(2,1)S(1)} %pad_maximum_fusion.15), channel_id=1, source_target_pairs={{0,3},{1,2},{2,1},{3,0},{4,7},{5,6},{6,5},{7,4},{8,11},{9,10},{10,... | collective-permute-start | bytes 786440 | tf_op jit(solution)/shard_map/ppermute | solution.py:314
  1013.3 23.7 %collective-permute-start.16 = (bf16[1024,128]{1,0:T(8,128)(2,1)S(1)}, bf16[1024,128]{1,0:T(8,128)(2,1)S(1)}, u32[]{:S(2)}, u32[]{:S(2)}) collective-permute-start(bf16[1024,128]{1,0:T(8,128)(2,1)S(1)} %pad_maximum_fusion.15), channel_id=1, source_target_pairs={{0,2},{1,3},{2,0},{3,1},{4,6},{5,7},{6,4},{7,5},{8,10},{9,11},{10,... | collective-permute-start | bytes 786440 | tf_op jit(solution)/shard_map/ppermute | solution.py:314
  1014.1 22.9 %collective-permute-start.15 = (bf16[1024,128]{1,0:T(8,128)(2,1)S(1)}, bf16[1024,128]{1,0:T(8,128)(2,1)S(1)}, u32[]{:S(2)}, u32[]{:S(2)}) collective-permute-start(bf16[1024,128]{1,0:T(8,128)(2,1)S(1)} %pad_maximum_fusion.15), channel_id=1, source_target_pairs={{0,1},{1,0},{2,3},{3,2},{4,5},{5,4},{6,7},{7,6},{8,9},{9,8},{10,11... | collective-permute-start | bytes 786440 | tf_op jit(solution)/shard_map/ppermute | solution.py:314
  (77 other events, 996.6 us)
Sparse Core Ops, SparseCore 0:
  131.8 24.5 all-gather.4
  158.8 35.6 all-gather.8
  197.0 42.1 all-gather.10
  241.5 85.4 all-gather.6
  640.6 38.0 reduce-scatter.4
  713.7 34.8 reduce-scatter.6
  908.4 51.8 reduce-scatter.10
  964.1 72.1 reduce-scatter.8
